TPU v7x, 256 devices: a whole 4x4x8 slice. The times are simulated.
256 devices in a mesh: leaf: 32 (over x, z_hi, core), seq: 8 (over z_lo, y).
Axes of the slice: x: 4, y: 4, z: 8 (z_hi: 4, z_lo: 2; z = z_hi * 2 + z_lo), core: 2. Of those that a mesh axis runs over, the one named last changes fastest.
Arguments:
- queries: bfloat16 [32, 512, 8192], P('leaf', 'seq'), may hold values from -120 to 120
- leaf_kv: bfloat16 [32, 512, 2048], P('leaf', 'seq'), may hold values from -144 to 144
- cache: bfloat16 [4096, 2048], P(('leaf', 'seq')), may hold values from -144 to 144
- out_weight: bfloat16 [8192, 5120], P(None, 'seq'), may hold values from -0.0625 to 0.0625
- parent: int32 [48], replicated, may hold values from 0 to 15, as said below
- owner: int32 [16], replicated, may hold values from 0 to 31, as said below
- lengths: int32 [16], replicated, may hold values from 32 to 128, as said below
Outputs:
- projected: bfloat16 [32, 512, 5120], P('leaf', None, 'seq')
Inputs may be any that keep to these rules, and one draw needn't show every extreme that they name: Entries 0 to 15 are segments: segment i < 4 has parent i - 1 (segment 0 has 0), the next 4 have parent 4 - 1, the next 8 each a segment of those 4; entries 16 on are the leaves, each with a parent among the last 8 segments. `owner`: distinct slots. `lengths`: some segment has exactly 128.
All inputs are finite; a program needn't handle non-finite values.
Results may differ from a plain program's by a relative error of at most 0.012.
Values may be sent and summed in bfloat16 or wider, within the bound.
No kernel may reach another device: no remote copies, remote signals or barrier semaphores. Data moves between devices by JAX's collectives and lax.ppermute only.
A program may use at most 256 MiB of HBM per device.

v0:
```python
import math

import jax
import jax.numpy as jnp
from jax import lax
from jax.sharding import PartitionSpec as P

KVH = 8
GROUP = 8
HD = 128
CAP = 128
DEPTH = 6


def branch(parent, leaf_index, seg_count):
    segment = parent[seg_count + leaf_index]
    ancestry = [segment]
    for level in range(DEPTH - 1):
        segment = parent[segment]
        ancestry.append(segment)
    return jnp.stack(ancestry)


def update(carry_state, query_rows, key_value, usable):
    running_max, running_sum, weighted = carry_state
    kv_heads = query_rows.shape[1]
    head_size = query_rows.shape[3]
    width = kv_heads * head_size
    keys = key_value[:, :width].reshape(-1, kv_heads, head_size)
    values = key_value[:, width:].reshape(-1, kv_heads, head_size)
    scores = jnp.einsum("thgd,khd->thgk", query_rows, keys, preferred_element_type=jnp.float32)
    scores = scores * (1.0 / math.sqrt(head_size))
    usable_four = usable[:, None, None, :]
    scores = jnp.where(usable_four, scores, -1e30)
    new_max = jnp.maximum(running_max, jnp.max(scores, axis=3))
    factor = jnp.exp(running_max - new_max)
    expon = jnp.where(usable_four, jnp.exp(scores - new_max[:, :, :, None]), 0.0)
    running_sum = running_sum * factor + jnp.sum(expon, axis=3)
    weights = expon.astype(jnp.bfloat16)
    weighted = weighted * factor[:, :, :, None] + jnp.einsum(
        "thgk,khd->thgd", weights, values, preferred_element_type=jnp.float32
    )
    return (new_max, running_sum, weighted)


def per_device(queries, leaf_kv, cache, out_weight, parent, owner, lengths):
    tokens = queries.shape[1]
    leaf_index = lax.axis_index("leaf")
    seq_index = lax.axis_index("seq")
    ancestry = branch(parent, leaf_index, owner.shape[0])
    owner_slots = owner[ancestry]
    limits = lengths[ancestry]
    query_rows = queries[0].reshape(tokens, KVH, GROUP, HD)
    initial = (
        jnp.full((tokens, KVH, GROUP), -1e30, jnp.float32),
        jnp.zeros((tokens, KVH, GROUP), jnp.float32),
        jnp.zeros((tokens, KVH, GROUP, HD), jnp.float32),
    )
    block_rows = lax.all_gather(cache, ("leaf", "seq"), axis=0, tiled=True)
    row_index = jnp.arange(block_rows.shape[0])
    slot_index = row_index // CAP
    offset = row_index % CAP
    matched = slot_index[:, None] == owner_slots[None, :]
    row_limit = jnp.sum(jnp.where(matched, limits[None, :], 0), axis=1)
    usable = offset < row_limit
    carry_state = lax.cond(
        jnp.any(usable),
        lambda inner: update(inner, query_rows, block_rows, usable[None, :]),
        lambda inner: inner,
        initial,
    )
    position = seq_index * tokens + jnp.arange(tokens)
    fold_block_rows = lax.all_gather(leaf_kv[0], "seq", axis=0, tiled=True)
    key_pos = jnp.arange(fold_block_rows.shape[0])
    fold_usable = key_pos[None, :] <= position[:, None]
    carry_state = lax.cond(
        jnp.int32(0) <= position[-1],
        lambda inner: update(inner, query_rows, fold_block_rows, fold_usable),
        lambda inner: inner,
        carry_state,
    )
    running_max, running_sum, weighted = carry_state
    attended = (weighted / running_sum[:, :, :, None]).astype(jnp.bfloat16).reshape(tokens, -1)
    projected = jnp.dot(
        lax.all_gather(attended, "seq", axis=0, tiled=True),
        out_weight,
        preferred_element_type=jnp.float32,
    ).astype(jnp.bfloat16)
    return projected[None]


def solution(mesh):
    in_specs = (
        P("leaf", "seq", None),
        P("leaf", "seq", None),
        P(("leaf", "seq"), None),
        P(None, "seq"),
        P(),
        P(),
        P(),
    )
    out_specs = P("leaf", None, "seq")
    return jax.shard_map(
        per_device, mesh=mesh, in_specs=in_specs, out_specs=out_specs, check_vma=False
    )
```

profile of v0, /device:TPU:1, one launch (start us, length us, event | category | flops | bytes accessed | tf_op | source)
XLA Modules:
  0.0 989.2 jit_solution(10834719726749072252)
XLA Ops:
  6.5 0.0 copy-start
  6.5 0.0 all-gather.5.cloned.1.call-start
  6.5 0.7 all-gather.5.cloned.1.call-update
  7.3 0.0 all-gather.9.cloned.1.call-start
  7.3 0.7 all-gather.9.cloned.1.call-update
  8.0 0.0 all-gather.7.cloned.1.call-start
  8.1 1.2 dynamic_slice.18
  11.2 1.3 dynamic_slice.19
  14.6 1.2 dynamic_slice.20
  17.6 1.2 dynamic_slice.21
  20.5 1.3 dynamic_slice.22
  23.7 1.3 dynamic_slice.23
  24.9 3.8 stack.21
  28.8 0.0 copy-done
  28.8 0.6 gather_fusion
  29.4 1.3 gather_fusion.1
  30.7 1.5 copy.67
  32.2 0.1 select_reduce_fusion
  32.3 0.6 fusion.33
  33.7 0.6 slice.15
  34.9 709.5 %all-gather.5.cloned.1.call-done = bf16[4096,2048]{1,0:T(8,128)(2,1)} async-done(((bf16[16,2048]{1,0:T(8,128)(2,1)}), bf16[4096,2048]{1,0:T(8,128)(2,1)}) %all-gather.5.cloned.1.call-update) | async-done | bytes 16777232 | tf_op jit(solution)/shard_map/all_gather | solution.py:59
  744.3 105.2 %conditional.2 = (f32[64,8,8]{0,2,1:T(8,128)}, f32[64,8,8]{0,2,1:T(8,128)S(1)}, f32[64,8,8,128]{3,0,2,1:T(8,128)}) conditional(s32[]{:T(128)} %convert_element_type.23, () %tuple.20, (pred[4096]{0:T(1024)(128)(4,1)S(1)}, bf16[4096,2048]{1,0:T(8,128)(2,1)}, bf16[64,8,8,128]{3,2,1,0:T(8,128)(2,1)S(1)}) %tuple.50), branch_computations={%region_2.3_spmd, %region_3.6_spmd} | conditional | flops 8808579072 | bytes 288550944 | solution.py:66
  744.3 20.8 %copy.47 = bf16[4096,2048]{0,1:T(8,128)(2,1)} copy(bf16[4096,2048]{1,0:T(8,128)(2,1)} %get-tuple-element.82) | data formatting | bytes 33554432 | tf_op jit(solution)/shard_map
  765.2 9.5 fusion.35
  774.7 23.6 %bitcast_reduce_fusion = (f32[64,8,8]{0,2,1:T(8,128)S(1)}, f32[8,4096,64,8]{1,2,3,0:T(8,128)}) fusion(pred[4096]{0:T(1024)(128)(4,1)S(1)} %get-tuple-element.36, bf16[4096,8,128,1]{0,2,3,1:T(8,128)(2,1)S(1)} %bitcast.82, bf16[64,8,8,128]{3,2,1,0:T(8,128)(2,1)S(1)} %get-tuple-element.83), kind=kOutput, calls=%fused_computation.3 | convolution fusion | flops 4345294848 | bytes 76566528 | tf_op jit(solution)/shard_map/cond/branch_1_fun/thgd,khd->thgk/dot_general | solution.py:31
  798.3 0.6 exponential_multiply_fusion
  798.9 28.0 %bitcast_add_fusion = f32[64,8,8,128]{3,0,2,1:T(8,128)} fusion(bf16[4096,8,128,1]{0,2,3,1:T(8,128)(2,1)} %bitcast.85, f32[8,4096,64,8]{1,2,3,0:T(8,128)} %get-tuple-element.103, f32[64,8,8]{0,2,1:T(8,128)} %get-tuple-element.113, pred[4096]{0:T(1024)(128)(4,1)S(1)} %get-tuple-element.36, f32[64,8,8]{0,2,1:T(8,128)S(1)} %get-tuple-element.94), kind=kOutput, calls=%fused_computation.12 | convolution fusion | flops 4379377664 | bytes 77631488 | tf_op jit(solution)/shard_map/cond/branch_1_fun/thgk,khd->thgd/dot_general | solution.py:40
  826.8 21.9 %fusion.3 = f32[64,8,8]{0,2,1:T(8,128)S(1)} fusion(f32[8,4096,64,8]{1,2,3,0:T(8,128)} %get-tuple-element.103, f32[64,8,8]{0,2,1:T(8,128)} %get-tuple-element.113, pred[4096]{0:T(1024)(128)(4,1)S(1)} %get-tuple-element.36), kind=kLoop, calls=%fused_computation.8 | loop fusion | flops 83881984 | bytes 67145728 | tf_op jit(solution)/shard_map/cond/branch_1_fun/reduce_sum | solution.py:38
  848.8 0.8 fusion.15
  849.6 0.0 all-gather.9.cloned.1.call-done
  849.6 21.6 %conditional.3 = (f32[64,8,8]{0,2,1:T(8,128)S(1)}, f32[64,8,8,128]{3,2,0,1:T(8,128)}) conditional(s32[]{:T(128)} %bitcast.13, (f32[64,8,8]{0,2,1:T(8,128)S(1)}, f32[64,8,8,128]{3,0,2,1:T(8,128)}) %tuple.22, (s32[]{:T(128)}, s32[64,1]{0,1:T(1,128)S(1)}, s32[64,512]{1,0:T(8,128)S(1)}, bf16[512,2048]{1,0:T(8,128)(2,1)}, ...), branch_computations={%region_6.7_spmd, %region_7.10_spmd} | conditional | flops 1093705728 | bytes 41370388 | solution.py:76
  849.8 3.9 copy.50
  853.8 1.7 fusion.36
  855.4 0.1 broadcast_compare_fusion
  855.5 2.0 fusion.16
  857.6 0.8 max.2
  858.3 4.0 fusion.17
  862.4 0.8 multiply_add_fusion
  863.2 0.1 copy.44
  863.3 8.0 bitcast_add_fusion.1
  871.3 0.1 copy.53
  871.4 2.0 divide_convert_fusion
  873.4 0.3 copy.54
  873.6 1.8 copy.85
  875.4 0.0 all-gather.7.cloned.1.call-update
  875.5 94.4 %all-gather.7.cloned.1.call-done = bf16[512,8192]{1,0:T(8,128)(2,1)} async-done(((bf16[64,8192]{1,0:T(8,128)(2,1)}), bf16[512,8192]{1,0:T(8,128)(2,1)}) %all-gather.7.cloned.1.call-update) | async-done | bytes 8388624 | tf_op jit(solution)/shard_map/all_gather | solution.py:85
  969.8 12.8 %fusion.25 = bf16[1,512,640]{2,1,0:T(8,128)(2,1)} fusion(bf16[512,8192]{1,0:T(8,128)(2,1)} %all-gather.7.cloned.1.call-done, bf16[8192,640]{1,0:T(8,128)(2,1)} %param.14), kind=kOutput, calls=%fused_computation.38 | convolution fusion | flops 5369036800 | bytes 19529728 | tf_op jit(solution)/shard_map/dot_general | solution.py:84
  982.7 0.0 copy-done.1
  (8 shorter events, 0.0 us)
Async XLA Ops:
  6.5 22.2 %copy-start = (s32[16]{0:T(128)S(1)}, s32[16]{0:T(128)}, u32[]{:S(2)}) copy-start(s32[16]{0:T(128)} %param.16) | copy-start | bytes 196
  6.5 737.8 %all-gather.5.cloned.1.call-start = ((), (), s32[]{:S(2)}) async-start(), calls=%async_computation | async-start | bytes 16842752 | tf_op jit(solution)/shard_map/all_gather | solution.py:59
  7.3 842.3 %all-gather.9.cloned.1.call-start = ((), (), s32[]{:S(2)}) async-start(), calls=%async_computation.2 | async-start | bytes 2359296 | tf_op jit(solution)/shard_map/all_gather | solution.py:73
  8.0 961.8 %all-gather.7.cloned.1.call-start = ((), (), s32[]{:S(2)}) async-start(), calls=%async_computation.1 | async-start | bytes 9437184 | tf_op jit(solution)/shard_map/all_gather | solution.py:85
  969.8 12.8 %copy-start.1 = (s32[16]{0:T(128)S(1)}, s32[16]{0:T(128)}, u32[]{:S(2)}) copy-start(s32[16]{0:T(128)} %param.16) | copy-start | bytes 196
Sparse Core Ops, SparseCore 0:
  9.2 735.0 all-gather.4
  746.1 38.8 all-gather.8
  875.6 94.2 all-gather.6
where the time goes:
time: 990 us; the launch traced here: 989 us
  waiting for transfers between devices  805 us (81%)
  matrix products  74.3 us (8%)
  local copies, waits for them, and re-layouts  53.7 us (5%)
  other arithmetic  31.8 us (3%)
  between operations  23.8 us (2%)
    all_gather x1, waiting for transfers between devices, per_device(): block_rows = lax.all_gather(cache, ('leaf', 'seq'), axis=0, tiled=True)  709 us
    all_gather x1, waiting for transfers between devices, per_device(): lax.all_gather(attended, 'seq', axis=0, tiled=True)  94.4 us
    dot_general x2, matrix products, update(): jnp.einsum('thgk,khd->thgd', weights, values, preferred_element_type=jnp....  35.9 us
    dot_general x2, matrix products, update(): jnp.einsum('thgd,khd->thgk', query_rows, keys, preferred_element_type=jnp...  25.6 us
    another operation x2, local copies, waits for them, and re-layouts  24.8 us
    reduce_sum x1, other arithmetic, update(): running_sum = running_sum * factor + jnp.sum(expon, axis=3)  21.9 us
  transfers between devices with their start and end apart: 3, of which 2 were waited for; matrix products, arithmetic and copies ran while one was open for 12% of the time, Pallas kernels for 0%

commit v1 on v0

v1 whole, which is shorter than its diff:
```python
import functools
import math

import jax
import jax.numpy as jnp
from jax import lax
from jax.experimental import pallas as pl
from jax.experimental.pallas import tpu as pltpu
from jax.sharding import PartitionSpec as P

KVH = 8
GROUP = 8
HD = 128
CAP = 128
DEPTH = 6
SEGS = 16
TOK = 64
UNITS = 4
QROWS = 4 * TOK
PACK = QROWS + TOK + 16
MASKED = -1e30
VMEM_LIMIT = 50 * 1024 * 1024

Z_SWAP = [(s, (s + 4) % 8) for s in range(8)]
CORE_SWAP = [(l, l ^ 1) for l in range(32)]


def y_shift(k):
    return [(z * 4 + y, z * 4 + (y + k) % 4) for z in range(2) for y in range(4)]


def x_shift(k):
    return [(l, (l + 8 * k) % 32) for l in range(32)]


def z_shift(k):
    return [
        ((x * 4 + z) * 2 + c, (x * 4 + (z + k) % 4) * 2 + c)
        for x in range(4)
        for z in range(4)
        for c in range(2)
    ]


def weight_pairs():
    pairs = []
    for x in range(4):
        for h in range(4):
            for zl in range(2):
                for y in range(4):
                    for c in range(2):
                        h_to = h if c == 0 else (h - 1 + 2 * zl) % 4
                        source = ((x * 4 + h) * 2 + c) * 8 + zl * 4 + y
                        target = ((x * 4 + h_to) * 2 + c) * 8 + (1 - zl) * 4 + y
                        pairs.append((source, target))
    return pairs


def params():
    return pltpu.CompilerParams(vmem_limit_bytes=VMEM_LIMIT)


def whole():
    return pl.BlockSpec(memory_space=pltpu.VMEM)


def anywhere():
    return pl.BlockSpec(memory_space=pl.ANY)


def scalars():
    return pl.BlockSpec(memory_space=pltpu.SMEM)


def chase(parent_ref, leaf):
    segment = parent_ref[SEGS + leaf]
    ancestry = [segment]
    for _ in range(DEPTH - 1):
        segment = parent_ref[segment]
        ancestry.append(segment)
    return ancestry


def pack_body(q_hbm, kv_hbm, cache_hbm, out_ref, q_ref, kv_ref, cache_ref, sem):
    pairs = ((kv_hbm, kv_ref), (cache_hbm, cache_ref), (q_hbm, q_ref))
    copies = [pltpu.make_async_copy(a, b, sem.at[i]) for i, (a, b) in enumerate(pairs)]
    for copy in copies:
        copy.start()
    copies[0].wait()
    copies[1].wait()
    for t in range(KVH):
        for half in range(2):
            lo = half * KVH * HD + t * HD
            cols = slice(half * HD, (half + 1) * HD)
            out_ref[t, QROWS : QROWS + TOK, cols] = kv_ref[:, lo : lo + HD]
            out_ref[t, QROWS + TOK :, cols] = cache_ref[:, lo : lo + HD]
    copies[2].wait()
    for t in range(KVH):
        for j in range(4):
            lo = t * GROUP * HD + j * 256
            out_ref[t, j * TOK : (j + 1) * TOK, :] = q_ref[:, lo : lo + 256]


def pack(queries, leaf_kv, cache):
    arrays = (queries, leaf_kv, cache)
    return pl.pallas_call(
        pack_body,
        out_shape=jax.ShapeDtypeStruct((KVH, PACK, 256), jnp.bfloat16),
        in_specs=[anywhere()] * 3,
        out_specs=whole(),
        scratch_shapes=[pltpu.VMEM(x.shape, x.dtype) for x in arrays] + [pltpu.SemaphoreType.DMA((3,))],
        compiler_params=params(),
        name="pack",
    )(*arrays)


def order_body(ids_ref, in_ref, sent_ref, first_ref, second_ref):
    step = pl.program_id(0)
    for i, out_ref in enumerate((sent_ref, first_ref, second_ref)):

        @pl.when(step // 4 == i)
        def _():
            out_ref[0] = in_ref[0, 0]


def order(ids, weight):
    cols = weight.shape[1]

    def source(i, ids):
        plane = jnp.where(i < 4, 1 - ids[2], ids[2])
        half = jnp.where(i < 8, ids[8], 1 - ids[8])
        return (plane * 4 + ids[4 + lax.rem(i, 4)], half, 0, 0)

    def target(part):
        return lambda i, ids: (jnp.clip(i - 4 * part, 0, 3), 0, 0)

    return pl.pallas_call(
        order_body,
        out_shape=[jax.ShapeDtypeStruct((4, 512, cols), jnp.bfloat16)] * 3,
        grid_spec=pltpu.PrefetchScalarGridSpec(
            num_scalar_prefetch=1,
            grid=(12,),
            in_specs=[pl.BlockSpec((1, 1, 512, cols), source)],
            out_specs=[pl.BlockSpec((1, 512, cols), target(part)) for part in range(3)],
        ),
        compiler_params=params(),
        cost_estimate=pl.CostEstimate(flops=0, bytes_accessed=24 * 512 * cols * 2, transcendentals=0),
        name="order",
    )(ids, weight.reshape(KVH, 2, 512, cols))


def join_body(units, *refs):
    outs = refs[-2:]
    for u in range(units):
        for k in range(4):
            for half in range(2):
                rows = slice(2 * TOK * u, 2 * TOK * (u + 1))
                outs[half][rows, 512 * k : 512 * (k + 1)] = refs[4 * u + k][:, 512 * half : 512 * (half + 1)]


def join(units):
    count = 2 * TOK * len(units)
    return pl.pallas_call(
        functools.partial(join_body, len(units)),
        out_shape=[jax.ShapeDtypeStruct((count, 2048), jnp.bfloat16)] * 2,
        in_specs=[whole()] * (4 * len(units)),
        out_specs=[whole()] * 2,
        compiler_params=params(),
        name="join",
    )(*[part for unit in units for part in unit])


def pick_body(flip, extra, ids_ref, parent_ref, owner_ref, *refs):
    columns = refs[:4]
    out_ref, sem = refs[-2], refs[-1]
    leaf = ids_ref[0]
    core = lax.rem(leaf, 2)
    z_hi = lax.rem(lax.div(leaf, 2), 4)
    x = lax.div(leaf, 8)
    target = leaf + flip * (1 - 2 * core)
    for act in ("start", "wait"):
        for a, segment in enumerate(chase(parent_ref, target)):
            slot = owner_ref[segment]
            here = lax.rem(slot, 2) == core
            near_x = lax.rem(x - lax.div(slot, 8) + 4, 4)
            near_z = lax.rem(z_hi - lax.rem(lax.div(slot, 2), 4) + 4, 4)
            for k in range(4):

                @pl.when(jnp.logical_and(here, near_x == k))
                def _():
                    copy = pltpu.make_async_copy(columns[k].at[near_z], out_ref.at[a], sem.at[a])
                    getattr(copy, act)()

            if extra:

                @pl.when(jnp.logical_not(here))
                def _():
                    copy = pltpu.make_async_copy(refs[4].at[a], out_ref.at[a], sem.at[a])
                    getattr(copy, act)()


def pick(flip, ids, parent, owner, columns, received=None):
    extra = received is not None
    operands = list(columns) + ([received] if extra else [])
    return pl.pallas_call(
        functools.partial(pick_body, flip, extra),
        out_shape=jax.ShapeDtypeStruct((DEPTH, CAP, 256), jnp.bfloat16),
        in_specs=[scalars()] * 3 + [anywhere()] * len(operands),
        out_specs=anywhere(),
        scratch_shapes=[pltpu.SemaphoreType.DMA((DEPTH,))],
        compiler_params=params(),
        name="pick",
    )(ids, parent, owner, *operands)


def attend_body(unit, ids_ref, parent_ref, lengths_ref, mine_ref, cache_ref, out_ref):
    first = 2 * unit
    tokens = 2 * TOK
    scale = math.log2(math.e) / math.sqrt(HD)
    limits = [lengths_ref[segment] for segment in chase(parent_ref, ids_ref[0])]
    lane = lax.broadcasted_iota(jnp.int32, (1, CAP), 1)
    bias = jnp.concatenate([jnp.where(lane < limit, 0.0, MASKED) for limit in limits], axis=1)
    cache_keys = cache_ref[:, :, :HD].reshape(DEPTH * CAP, HD)
    cache_values = cache_ref[:, :, HD:].reshape(DEPTH * CAP, HD)
    leaf_keys = mine_ref[: first + 2, QROWS : QROWS + TOK, :HD].reshape(-1, HD)
    leaf_values = mine_ref[: first + 2, QROWS : QROWS + TOK, HD:].reshape(-1, HD)
    keys = jnp.concatenate([cache_keys, leaf_keys], axis=0)
    values = jnp.concatenate([cache_values, leaf_values], axis=0)
    row = lax.broadcasted_iota(jnp.int32, (tokens, tokens), 0)
    col = lax.broadcasted_iota(jnp.int32, (tokens, tokens), 1)
    causal = jnp.where(col <= row, 0.0, MASKED)
    per = 4
    causal = jnp.concatenate([causal] * per, axis=0)
    for tile in range(GROUP // per):
        rows = []
        for g in range(tile * per, (tile + 1) * per):
            j, half = g // 2, g % 2
            part = mine_ref[first : first + 2, j * TOK : (j + 1) * TOK, half * HD : (half + 1) * HD]
            rows.append(part.reshape(tokens, HD))
        scores = lax.dot_general(
            jnp.concatenate(rows, axis=0), keys, (((1,), (1,)), ((), ())), preferred_element_type=jnp.float32
        )
        seen = DEPTH * CAP
        diagonal = seen + unit * tokens
        parts = [scores[:, :seen] + bias]
        if unit:
            parts.append(scores[:, seen:diagonal])
        parts.append(scores[:, diagonal:] + causal)
        scores = jnp.concatenate(parts, axis=1)
        largest = jnp.max(scores, axis=1, keepdims=True)
        expon = jnp.exp2((scores - largest) * scale)
        total = jnp.sum(expon, axis=1, keepdims=True)
        summed = jnp.dot(expon.astype(jnp.bfloat16), values, preferred_element_type=jnp.float32)
        done = (summed / total).astype(jnp.bfloat16)
        for i in range(per):
            g = tile * per + i
            column = pl.multiple_of(lax.rem(g + GROUP // 2 * ids_ref[8], GROUP) * HD, HD)
            out_ref[:, pl.ds(column, HD)] = done[i * tokens : (i + 1) * tokens]


def attend(unit, ids, parent, lengths, mine, cache_rows):
    keys = DEPTH * CAP + (unit + 1) * 2 * TOK
    count = 2 * TOK * GROUP
    return pl.pallas_call(
        functools.partial(attend_body, unit),
        out_shape=jax.ShapeDtypeStruct((2 * TOK, GROUP * HD), jnp.bfloat16),
        in_specs=[scalars()] * 3 + [whole()] * 2,
        out_specs=whole(),
        compiler_params=params(),
        cost_estimate=pl.CostEstimate(
            flops=count * keys * HD * 4, bytes_accessed=2_000_000, transcendentals=count * keys
        ),
        name=f"attend{unit}",
    )(ids, parent, lengths, mine, cache_rows)


def after(value, *earlier):
    return lax.optimization_barrier((value, earlier))[0]


def project(blocks, matrices):
    total = None
    for rows, matrix in zip(blocks, matrices):
        product = jnp.dot(rows, matrix.reshape(2048, -1), preferred_element_type=jnp.float32)
        total = product if total is None else total + product
    return total


def per_device(queries, leaf_kv, cache, out_weight, parent, owner, lengths):
    leaf = lax.axis_index("leaf")
    seq = lax.axis_index("seq")
    z, y, core = seq // 4, seq % 4, leaf % 2
    ids = jnp.stack([leaf, seq, z, y, y, (y + 3) % 4, (y + 1) % 4, (y + 2) % 4, core]).astype(jnp.int32)

    mine = lax.all_to_all(pack(queries[0], leaf_kv[0], cache), "seq", 0, 0)
    sent, *matrix = order(ids, out_weight)
    slot = after(mine[:, QROWS + TOK :, :].reshape(CAP, 256), sent)
    column = jnp.stack([slot] + [lax.ppermute(slot, "leaf", z_shift(k)) for k in (1, 2, 3)])
    columns = [column] + [lax.ppermute(column, "leaf", x_shift(k)) for k in (1, 2, 3)]
    near = lax.ppermute(after(sent, column), ("leaf", "seq"), weight_pairs())

    given = pick(1, ids, parent, owner, columns)
    received = lax.ppermute(given, "leaf", CORE_SWAP)
    cache_rows = pick(0, ids, parent, owner, columns, received)

    def up(part):
        return lax.ppermute(part, "seq", y_shift(1))

    def down(part):
        return lax.ppermute(part, "seq", y_shift(-1))

    def attention(unit, cache_rows):
        return attend(unit, ids, parent, lengths, mine, cache_rows)

    part0 = attention(0, cache_rows)
    up0, down0 = up(part0), down(part0)
    part1 = attention(1, after(cache_rows, part0))
    up1, down1 = up(part1), down(part1)
    part2 = attention(2, after(cache_rows, part1))
    up2, down2 = up(part2), down(part2)
    far0 = up(after(up0, part2))
    part3 = attention(3, after(cache_rows, part2, up0))
    up3, down3 = up(part3), down(part3)
    far1 = down(after(down1, part3))
    far2 = up(after(up2, part3))
    far3 = down(after(down3, part3))
    far = lax.ppermute(after(near, part3, up1, down1), "leaf", CORE_SWAP)

    low = join([(part0, up0, down0, far0), (part1, up1, down1, far1), (part2, up2, down2, far2)])
    mine_low = project(low, matrix)
    other_low = project(after(low, mine_low), (near, far)).astype(jnp.bfloat16)
    result_low = mine_low + lax.ppermute(other_low, "seq", Z_SWAP).astype(jnp.float32)
    high = join([(after(part3, other_low), up3, down3, far3)])
    other_high = project(high, (near, far)).astype(jnp.bfloat16)
    mine_high = project(after(high, other_high), matrix)
    result_high = mine_high + lax.ppermute(other_high, "seq", Z_SWAP).astype(jnp.float32)
    return jnp.concatenate([result_low, result_high], axis=0).astype(jnp.bfloat16)[None]


def solution(mesh):
    in_specs = (
        P("leaf", "seq", None),
        P("leaf", "seq", None),
        P(("leaf", "seq"), None),
        P(None, "seq"),
        P(),
        P(),
        P(),
    )
    out_specs = P("leaf", None, "seq")
    return jax.shard_map(per_device, mesh=mesh, in_specs=in_specs, out_specs=out_specs, check_vma=False)
```

time: 990 us -> 138 us (0.14)
  waiting for transfers between devices: 805 us -> 50.1 us
  matrix products: 74.3 us -> 10.3 us
  local copies, waits for them, and re-layouts: 53.7 us -> 4.63 us
  starting transfers between devices: 0.08 us -> 42 us
  other arithmetic: 31.8 us -> 1.05 us
  Pallas kernels: 0 us -> 27.7 us
  between operations: 23.8 us -> 0.24 us
    all_gather x3 -> x0, waiting for transfers between devices: 804 us -> none  [the longest x1 709 us: per_device(): block_rows = lax.all_gather(cache, ('leaf', 'seq'), axis=0, tiled=True)]
    dot_general x5 -> x8, matrix products: 74.3 us -> 10.3 us  [project(): jnp.dot(rows, matrix.reshape(2048, -1), preferred_element_type=jnp.float32)]
    ppermute x0 -> x23, waiting for transfers between devices: none -> 43.7 us  [the longest x3 11.2 us: per_device(): lax.ppermute(column, 'leaf', x_shift(k))]
    ppermute x0 -> x23, starting transfers between devices: none -> 35.6 us  [the longest x6 10.4 us: down(): return lax.ppermute(part, 'seq', y_shift(-1))]
    another operation x3 -> x1, local copies, waits for them, and re-layouts: 28.6 us -> 0.08 us  [per_device(): jnp.stack([leaf, seq, z, y, y, (y + 3) % 4, (y + 1) % 4, (y + 2) % 4, core])]
    pallas_call x0 -> x10, Pallas kernels: none -> 27.7 us  [the longest x4 11.3 us: attend(): pl.pallas_call(functools.partial(attend_body, unit), out_shape=jax.ShapeD...]
    reduce_sum x2 -> x0, other arithmetic: 22.1 us -> none  [the longest x1 21.9 us: update(): running_sum = running_sum * factor + jnp.sum(expon, axis=3)]
    slice x3 -> x1, local copies, waits for them, and re-layouts: 11.8 us -> 0.01 us  [per_device(): slot = after(mine[:, QROWS + TOK:, :].reshape(CAP, 256), sent)]
  transfers between devices with their start and end apart: 3 -> 24, of which waited for: 2 -> 14; matrix products, arithmetic and copies ran while one was open for 12% -> 7% of each run, Pallas kernels for 0% -> 19%
where the time goes in v1:
time: 138 us; the launch traced here: 136 us
  waiting for transfers between devices  50.1 us (36%)
  starting transfers between devices  42 us (30%)
  Pallas kernels  27.7 us (20%)
  matrix products  10.3 us (7%)
  local copies, waits for them, and re-layouts  4.63 us (3%)
    pallas_call x4, Pallas kernels, attend(): pl.pallas_call(functools.partial(attend_body, unit), out_shape=jax.ShapeD...  11.3 us
    ppermute x3, waiting for transfers between devices, per_device(): lax.ppermute(column, 'leaf', x_shift(k))  11.2 us
    pallas_call x1, Pallas kernels, order(): pl.pallas_call(order_body, out_shape=[jax.ShapeDtypeStruct((4, 512, cols)...  10.5 us
    ppermute x6, starting transfers between devices, down(): return lax.ppermute(part, 'seq', y_shift(-1))  10.4 us
    dot_general x8, matrix products, project(): jnp.dot(rows, matrix.reshape(2048, -1), preferred_element_type=jnp.float32)  10.3 us
    ppermute x1, waiting for transfers between devices, per_device(): lax.ppermute(other_low, 'seq', Z_SWAP).astype(jnp.float32)  9.62 us
    ppermute x6, waiting for transfers between devices, up(): return lax.ppermute(part, 'seq', y_shift(1))  9.52 us
    ppermute x3, starting transfers between devices, per_device(): lax.ppermute(slot, 'leaf', z_shift(k))  8.37 us
  transfers between devices with their start and end apart: 24, of which 14 were waited for; matrix products, arithmetic and copies ran while one was open for 7% of the time, Pallas kernels for 19%

profile of v1, /device:TPU:1, one launch (start us, length us, event | category | flops | bytes accessed | tf_op | source)
XLA Modules:
  0.0 136.0 jit_solution(2628300458613034150)
XLA Ops:
  0.0 1.2 copy-done
  1.2 0.9 copy-done.1
  2.2 0.8 copy-done.2
  3.0 1.5 %pack.1 = bf16[8,336,256]{2,1,0:T(8,128)(2,1)} custom-call(bf16[64,8192]{1,0:T(8,128)(2,1)S(1)} %bitcast.40, bf16[64,2048]{1,0:T(8,128)(2,1)S(1)} %bitcast.41, bf16[16,2048]{1,0:T(8,128)(2,1)S(1)} %copy-done.2), custom_call_target="tpu_custom_call" | custom-call | tf_op jit(solution)/shard_map/pack/pallas_call | solution.py:106
  4.5 6.4 %all-to-all-start = ((bf16[8,336,256]{2,1,0:T(8,128)(2,1)}), bf16[8,336,256]{2,1,0:T(8,128)(2,1)S(1)}, u32[]{:S(2)}, u32[]{:S(2)}) async-start(bf16[8,336,256]{2,1,0:T(8,128)(2,1)} %pack.1), calls=%async_computation | async-start | bytes 2752512 | tf_op jit(solution)/shard_map/all_to_all | solution.py:295
  11.0 10.5 %order.1 = (bf16[4,512,640]{2,1,0:T(8,128)(2,1)S(1)}, bf16[4,512,640]{2,1,0:T(8,128)(2,1)}, bf16[4,512,640]{2,1,0:T(8,128)(2,1)}) custom-call(s32[9]{0:T(128)S(1)} %stack.51.ids_ref, bf16[8,2,512,640]{3,2,1,0:T(8,128)(2,1)} %bitcast.42), custom_call_target="tpu_custom_call" | custom-call | bytes 15728640 | tf_op jit(solution)/shard_map/order/pallas_call | solution.py:137
  21.5 1.5 %copy-done.6 = bf16[4,512,640]{2,1,0:T(8,128)(2,1)} copy-done((bf16[4,512,640]{2,1,0:T(8,128)(2,1)}, bf16[4,512,640]{2,1,0:T(8,128)(2,1)S(1)}, u32[]{:S(2)}) %copy-start.6) | copy-done | bytes 2621464
  23.0 6.4 %all-to-all-done.mine_ref = bf16[8,336,256]{2,1,0:T(8,128)(2,1)S(1)} async-done(((bf16[8,336,256]{2,1,0:T(8,128)(2,1)}), bf16[8,336,256]{2,1,0:T(8,128)(2,1)S(1)}, u32[]{:S(2)}, u32[]{:S(2)}) %all-to-all-start) | async-done | bytes 1376288 | tf_op jit(solution)/shard_map/all_to_all | solution.py:295
  29.3 5.1 %collective-permute-start.2 = (bf16[128,256]{1,0:T(8,128)(2,1)S(1)}, bf16[128,256]{1,0:T(8,128)(2,1)S(1)}, u32[]{:S(2)}, u32[]{:S(2)}) collective-permute-start(bf16[128,256]{1,0:T(8,128)(2,1)S(1)} %bitcast.51), channel_id=1, source_target_pairs={{0,48},{8,56},{16,0},{24,8},{32,16},{40,24},{48,32},{56,40},{64,11... | collective-permute-start | bytes 196616 | tf_op jit(solution)/shard_map/ppermute | solution.py:298
  34.5 1.2 collective-permute-start.1
  35.6 2.1 %collective-permute-start = (bf16[128,256]{1,0:T(8,128)(2,1)S(1)}, bf16[128,256]{1,0:T(8,128)(2,1)S(1)}, u32[]{:S(2)}, u32[]{:S(2)}) collective-permute-start(bf16[128,256]{1,0:T(8,128)(2,1)S(1)} %bitcast.53), channel_id=1, source_target_pairs={{0,16},{8,24},{16,32},{24,40},{32,48},{40,56},{48,0},{56,8},{64,80... | collective-permute-start | bytes 196616 | tf_op jit(solution)/shard_map/ppermute | solution.py:298
  37.7 3.9 %collective-permute-done.1 = bf16[128,256]{1,0:T(8,128)(2,1)S(1)} collective-permute-done((bf16[128,256]{1,0:T(8,128)(2,1)S(1)}, bf16[128,256]{1,0:T(8,128)(2,1)S(1)}, u32[]{:S(2)}, u32[]{:S(2)}) %collective-permute-start.1) | collective-permute-done | bytes 65568 | tf_op jit(solution)/shard_map/ppermute | solution.py:298
  41.7 5.3 %collective-permute-start.16 = (bf16[4,512,640]{2,1,0:T(8,128)(2,1)}, bf16[4,512,640]{2,1,0:T(8,128)(2,1)S(1)}, u32[]{:S(2)}, u32[]{:S(2)}) collective-permute-start(bf16[4,512,640]{2,1,0:T(8,128)(2,1)} %copy-done.6), channel_id=1, source_target_pairs={{0,4},{8,60},{1,5},{9,61},{2,6},{10,62},{3,7},{11,63},{4,0},{12,24... | collective-permute-start | bytes 7864328 | tf_op jit(solution)/shard_map/ppermute | solution.py:300
  47.0 1.2 collective-permute-start.3
  48.2 2.5 %collective-permute-start.4 = (bf16[4,128,256]{2,1,0:T(8,128)(2,1)S(1)}, bf16[4,128,256]{2,1,0:T(8,128)(2,1)S(1)}, u32[]{:S(2)}, u32[]{:S(2)}) collective-permute-start(bf16[4,128,256]{2,1,0:T(8,128)(2,1)S(1)} %pad_maximum_fusion.1.refs_0_), channel_id=1, source_target_pairs={{0,128},{8,136},{16,144},{24,152},{32,160},{40,168},{48,176},{56,1... | collective-permute-start | bytes 786440 | tf_op jit(solution)/shard_map/ppermute | solution.py:299
  50.7 1.2 collective-permute-start.5
  51.8 4.6 %collective-permute-done.3.refs_1_ = bf16[4,128,256]{2,1,0:T(8,128)(2,1)S(1)} collective-permute-done((bf16[4,128,256]{2,1,0:T(8,128)(2,1)S(1)}, bf16[4,128,256]{2,1,0:T(8,128)(2,1)S(1)}, u32[]{:S(2)}, u32[]{:S(2)}) %collective-permute-start.3) | collective-permute-done | bytes 262176 | tf_op jit(solution)/shard_map/ppermute | solution.py:299
  56.5 6.6 %collective-permute-done.4.refs_2_ = bf16[4,128,256]{2,1,0:T(8,128)(2,1)S(1)} collective-permute-done((bf16[4,128,256]{2,1,0:T(8,128)(2,1)S(1)}, bf16[4,128,256]{2,1,0:T(8,128)(2,1)S(1)}, u32[]{:S(2)}, u32[]{:S(2)}) %collective-permute-start.4) | collective-permute-done | bytes 262176 | tf_op jit(solution)/shard_map/ppermute | solution.py:299
  63.1 1.0 pick.2
  64.9 1.3 collective-permute-done.6.refs_4_
  66.2 1.4 %pick.3.cache_ref = bf16[6,128,256]{2,1,0:T(8,128)(2,1)S(1)} custom-call(s32[9]{0:T(128)S(1)} %stack.51.ids_ref, s32[48]{0:T(128)S(1)} %copy-done.3, s32[16]{0:T(128)S(1)} %copy-done.4, bf16[4,128,256]{2,1,0:T(8,128)(2,1)S(1)} %pad_maximum_fusion.1.refs_0_, bf16[4,128,256]{2,1,0:T(8,128)(2,1)S(1)} %collective-permute-done.3.refs_1_, ...), custom_call_target="tpu_custom_call" | custom-call | tf_op jit(solution)/shard_map/pick/pallas_call | solution.py:205
  67.7 2.5 %attend0.1.refs_0_ = bf16[128,1024]{1,0:T(8,128)(2,1)S(1)} custom-call(s32[9]{0:T(128)S(1)} %stack.51.ids_ref, s32[48]{0:T(128)S(1)} %copy-done.3, s32[16]{0:T(128)S(1)} %copy-done.5, bf16[8,336,256]{2,1,0:T(8,128)(2,1)S(1)} %all-to-all-done.mine_ref, bf16[6,128,256]{2,1,0:T(8,128)(2,1)S(1)} %pick.3.cache_ref), custom_call_target="tpu_custom_call" | custom-call | flops 469762048 | bytes 2000000 | tf_op jit(solution)/shard_map/attend0/pallas_call | solution.py:264
  70.3 2.6 %attend1.1.refs_4_ = bf16[128,1024]{1,0:T(8,128)(2,1)S(1)} custom-call(s32[9]{0:T(128)S(1)} %stack.51.ids_ref, s32[48]{0:T(128)S(1)} %copy-done.3, s32[16]{0:T(128)S(1)} %copy-done.5, bf16[8,336,256]{2,1,0:T(8,128)(2,1)S(1)} %all-to-all-done.mine_ref, bf16[6,128,256]{2,1,0:T(8,128)(2,1)S(1)} %pick.3.cache_ref), custom_call_target="tpu_custom_call" | custom-call | flops 536870912 | bytes 2000000 | tf_op jit(solution)/shard_map/attend1/pallas_call | solution.py:264
  73.0 2.9 %collective-permute-start.11 = (bf16[128,1024]{1,0:T(8,128)(2,1)S(1)}, bf16[128,1024]{1,0:T(8,128)(2,1)S(1)}, u32[]{:S(2)}, u32[]{:S(2)}) collective-permute-start(bf16[128,1024]{1,0:T(8,128)(2,1)S(1)} %attend1.1.refs_4_), channel_id=1, source_target_pairs={{0,3},{1,0},{2,1},{3,2},{4,7},{5,4},{6,5},{7,6},{8,11},{9,8},{10,9... | collective-permute-start | bytes 786440 | tf_op jit(solution)/shard_map/ppermute | solution.py:310
  75.9 3.0 %attend2.1.refs_8_ = bf16[128,1024]{1,0:T(8,128)(2,1)S(1)} custom-call(s32[9]{0:T(128)S(1)} %stack.51.ids_ref, s32[48]{0:T(128)S(1)} %copy-done.3, s32[16]{0:T(128)S(1)} %copy-done.5, bf16[8,336,256]{2,1,0:T(8,128)(2,1)S(1)} %all-to-all-done.mine_ref, bf16[6,128,256]{2,1,0:T(8,128)(2,1)S(1)} %pick.3.cache_ref), custom_call_target="tpu_custom_call" | custom-call | flops 603979776 | bytes 2000000 | tf_op jit(solution)/shard_map/attend2/pallas_call | solution.py:264
  79.0 3.1 %attend3.1.refs_0_ = bf16[128,1024]{1,0:T(8,128)(2,1)S(1)} custom-call(s32[9]{0:T(128)S(1)} %stack.51.ids_ref, s32[48]{0:T(128)S(1)} %copy-done.3, s32[16]{0:T(128)S(1)} %copy-done.5, bf16[8,336,256]{2,1,0:T(8,128)(2,1)S(1)} %all-to-all-done.mine_ref, bf16[6,128,256]{2,1,0:T(8,128)(2,1)S(1)} %pick.3.cache_ref), custom_call_target="tpu_custom_call" | custom-call | flops 671088640 | bytes 2000000 | tf_op jit(solution)/shard_map/attend3/pallas_call | solution.py:264
  82.1 2.5 %collective-permute-done.10.refs_5_ = bf16[128,1024]{1,0:T(8,128)(2,1)S(1)} collective-permute-done((bf16[128,1024]{1,0:T(8,128)(2,1)S(1)}, bf16[128,1024]{1,0:T(8,128)(2,1)S(1)}, u32[]{:S(2)}, u32[]{:S(2)}) %collective-permute-start.10) | collective-permute-done | bytes 262176 | tf_op jit(solution)/shard_map/ppermute | solution.py:307
  84.6 1.2 collective-permute-start.17
  85.8 2.7 %collective-permute-start.8 = (bf16[128,1024]{1,0:T(8,128)(2,1)S(1)}, bf16[128,1024]{1,0:T(8,128)(2,1)S(1)}, u32[]{:S(2)}, u32[]{:S(2)}) collective-permute-start(bf16[128,1024]{1,0:T(8,128)(2,1)S(1)} %attend0.1.refs_0_), channel_id=1, source_target_pairs={{0,3},{1,0},{2,1},{3,2},{4,7},{5,4},{6,5},{7,6},{8,11},{9,8},{10,9... | collective-permute-start | bytes 786440 | tf_op jit(solution)/shard_map/ppermute | solution.py:310
  88.5 1.4 %collective-permute-start.9 = (bf16[128,1024]{1,0:T(8,128)(2,1)S(1)}, bf16[128,1024]{1,0:T(8,128)(2,1)S(1)}, u32[]{:S(2)}, u32[]{:S(2)}) collective-permute-start(bf16[128,1024]{1,0:T(8,128)(2,1)S(1)} %collective-permute-done.7.refs_1_), channel_id=1, source_target_pairs={{0,1},{1,2},{2,3},{3,0},{4,5},{5,6},{6,7},{7,4},{8,9},{9,10},{10,1... | collective-permute-start | bytes 786440 | tf_op jit(solution)/shard_map/ppermute | solution.py:307
  90.0 4.9 %collective-permute-done.13.refs_9_ = bf16[128,1024]{1,0:T(8,128)(2,1)S(1)} collective-permute-done((bf16[128,1024]{1,0:T(8,128)(2,1)S(1)}, bf16[128,1024]{1,0:T(8,128)(2,1)S(1)}, u32[]{:S(2)}, u32[]{:S(2)}) %collective-permute-start.13) | collective-permute-done | bytes 262176 | tf_op jit(solution)/shard_map/ppermute | solution.py:307
  94.9 1.5 %collective-permute-start.15 = (bf16[128,1024]{1,0:T(8,128)(2,1)S(1)}, bf16[128,1024]{1,0:T(8,128)(2,1)S(1)}, u32[]{:S(2)}, u32[]{:S(2)}) collective-permute-start(bf16[128,1024]{1,0:T(8,128)(2,1)S(1)} %collective-permute-done.13.refs_9_), channel_id=1, source_target_pairs={{0,1},{1,2},{2,3},{3,0},{4,5},{5,6},{6,7},{7,4},{8,9},{9,10},{10,1... | collective-permute-start | bytes 786440 | tf_op jit(solution)/shard_map/ppermute | solution.py:307
  96.4 3.1 %collective-permute-done.14.refs_10_ = bf16[128,1024]{1,0:T(8,128)(2,1)S(1)} collective-permute-done((bf16[128,1024]{1,0:T(8,128)(2,1)S(1)}, bf16[128,1024]{1,0:T(8,128)(2,1)S(1)}, u32[]{:S(2)}, u32[]{:S(2)}) %collective-permute-start.14) | collective-permute-done | bytes 262176 | tf_op jit(solution)/shard_map/ppermute | solution.py:310
  99.5 1.0 collective-permute-done.9.refs_3_
  100.5 2.4 %collective-permute-start.20 = (bf16[128,1024]{1,0:T(8,128)(2,1)S(1)}, bf16[128,1024]{1,0:T(8,128)(2,1)S(1)}, u32[]{:S(2)}, u32[]{:S(2)}) collective-permute-start(bf16[128,1024]{1,0:T(8,128)(2,1)S(1)} %attend3.1.refs_0_), channel_id=1, source_target_pairs={{0,3},{1,0},{2,1},{3,2},{4,7},{5,4},{6,5},{7,6},{8,11},{9,8},{10,9... | collective-permute-start | bytes 786440 | tf_op jit(solution)/shard_map/ppermute | solution.py:310
  102.9 2.2 %collective-permute-done.12.refs_7_ = bf16[128,1024]{1,0:T(8,128)(2,1)S(1)} collective-permute-done((bf16[128,1024]{1,0:T(8,128)(2,1)S(1)}, bf16[128,1024]{1,0:T(8,128)(2,1)S(1)}, u32[]{:S(2)}, u32[]{:S(2)}) %collective-permute-start.12) | collective-permute-done | bytes 262176 | tf_op jit(solution)/shard_map/ppermute | solution.py:310
  105.1 1.1 collective-permute-done.15.refs_11_
  106.1 1.9 %join.2 = (bf16[384,2048]{1,0:T(8,128)(2,1)}, bf16[384,2048]{1,0:T(8,128)(2,1)}) custom-call(bf16[128,1024]{1,0:T(8,128)(2,1)S(1)} %attend0.1.refs_0_, bf16[128,1024]{1,0:T(8,128)(2,1)S(1)} %collective-permute-done.7.refs_1_, bf16[128,1024]{1,0:T(8,128)(2,1)S(1)} %collective-permute-done.8.refs_2_, bf16[128,1024]{1,0:T(8,128)(2,1)S(1)} %collective-permute-done.9.refs_3_, ...), custom_call_target="tpu_custom_call" | custom-call | tf_op jit(solution)/shard_map/join/pallas_call | solution.py:163
  108.1 3.7 %fusion.4 = f32[384,640]{1,0:T(8,128)S(1)} fusion(bf16[384,2048]{1,0:T(8,128)(2,1)} %get-tuple-element.41, bf16[2048,640]{1,0:T(8,128)(2,1)} %bitcast.49), kind=kOutput, calls=%fused_computation.12 | convolution fusion | flops 1006632960 | bytes 5177344 | tf_op jit(solution)/shard_map/dot_general | solution.py:284
  111.8 1.4 %convolution_add_fusion.1 = f32[384,640]{1,0:T(8,128)S(1)} fusion(f32[384,640]{1,0:T(8,128)S(1)} %fusion.4, bf16[384,2048]{1,0:T(8,128)(2,1)S(1)} %copy-done.9, bf16[2048,640]{1,0:T(8,128)(2,1)S(1)} %bitcast.45), kind=kOutput, calls=%fused_computation.1 | convolution fusion | flops 1006878720 | bytes 6160384 | tf_op jit(solution)/shard_map/dot_general | solution.py:284
  113.3 2.4 %collective-permute-start.21 = (bf16[128,1024]{1,0:T(8,128)(2,1)S(1)}, bf16[128,1024]{1,0:T(8,128)(2,1)S(1)}, u32[]{:S(2)}, u32[]{:S(2)}) collective-permute-start(bf16[128,1024]{1,0:T(8,128)(2,1)S(1)} %collective-permute-done.20.refs_2_), channel_id=1, source_target_pairs={{0,3},{1,0},{2,1},{3,2},{4,7},{5,4},{6,5},{7,6},{8,11},{9,8},{10,9... | collective-permute-start | bytes 786440 | tf_op jit(solution)/shard_map/ppermute | solution.py:310
  115.7 1.4 %fusion.5 = f32[384,640]{1,0:T(8,128)S(1)} fusion(bf16[384,2048]{1,0:T(8,128)(2,1)S(1)} %copy-done.10, bf16[2048,640]{1,0:T(8,128)(2,1)S(1)} %bitcast.47), kind=kOutput, calls=%fused_computation.13 | convolution fusion | flops 1006632960 | bytes 5177344 | tf_op jit(solution)/shard_map/dot_general | solution.py:284
  117.1 1.4 %fusion = bf16[384,640]{1,0:T(8,128)(2,1)S(1)} fusion(f32[384,640]{1,0:T(8,128)S(1)} %fusion.5, bf16[384,2048]{1,0:T(8,128)(2,1)S(1)} %copy-done.9, bf16[2048,640]{1,0:T(8,128)(2,1)S(1)} %bitcast.43), kind=kOutput, calls=%fused_computation.2 | convolution fusion | flops 1007124480 | bytes 5668864 | tf_op jit(solution)/shard_map/dot_general | solution.py:284
  118.6 1.3 collective-permute-done.21.refs_3_
  121.2 1.5 %collective-permute-start.18 = (bf16[384,640]{1,0:T(8,128)(2,1)S(1)}, bf16[384,640]{1,0:T(8,128)(2,1)S(1)}, u32[]{:S(2)}, u32[]{:S(2)}) collective-permute-start(bf16[384,640]{1,0:T(8,128)(2,1)S(1)} %fusion), channel_id=1, source_target_pairs={{0,4},{1,5},{2,6},{3,7},{4,0},{5,1},{6,2},{7,3},{8,12},{9,13},{10,... | collective-permute-start | bytes 1474568 | tf_op jit(solution)/shard_map/ppermute | solution.py:332
  123.8 1.5 %collective-permute-done.22 = bf16[128,640]{1,0:T(8,128)(2,1)S(1)} collective-permute-done((bf16[128,640]{1,0:T(8,128)(2,1)S(1)}, bf16[128,640]{1,0:T(8,128)(2,1)S(1)}, u32[]{:S(2)}, u32[]{:S(2)}) %collective-permute-start.22) | collective-permute-done | bytes 163872 | tf_op jit(solution)/shard_map/ppermute | solution.py:336
  125.4 9.6 %collective-permute-done.18 = bf16[384,640]{1,0:T(8,128)(2,1)S(1)} collective-permute-done((bf16[384,640]{1,0:T(8,128)(2,1)S(1)}, bf16[384,640]{1,0:T(8,128)(2,1)S(1)}, u32[]{:S(2)}, u32[]{:S(2)}) %collective-permute-start.18) | collective-permute-done | bytes 491552 | tf_op jit(solution)/shard_map/ppermute | solution.py:332
  135.1 0.9 pad_maximum_fusion
  (46 shorter events, 3.9 us)
Async XLA Ops:
  0.0 1.2 copy-start
  1.2 0.9 copy-start.1
  2.2 0.8 copy-start.2
  4.5 24.8 %all-to-all-start = ((bf16[8,336,256]{2,1,0:T(8,128)(2,1)}), bf16[8,336,256]{2,1,0:T(8,128)(2,1)S(1)}, u32[]{:S(2)}, u32[]{:S(2)}) async-start(bf16[8,336,256]{2,1,0:T(8,128)(2,1)} %pack.1), calls=%async_computation | async-start | bytes 2752512 | tf_op jit(solution)/shard_map/all_to_all | solution.py:295
  11.0 52.1 %copy-start.3 = (s32[48]{0:T(128)S(1)}, s32[48]{0:T(128)}, u32[]{:S(2)}) copy-start(s32[48]{0:T(128)} %parent_ref.11) | copy-start | bytes 580
  11.0 52.1 %copy-start.4 = (s32[16]{0:T(128)S(1)}, s32[16]{0:T(128)}, u32[]{:S(2)}) copy-start(s32[16]{0:T(128)} %owner_ref.3) | copy-start | bytes 196
  21.5 1.5 %copy-start.6 = (bf16[4,512,640]{2,1,0:T(8,128)(2,1)}, bf16[4,512,640]{2,1,0:T(8,128)(2,1)S(1)}, u32[]{:S(2)}) copy-start(bf16[4,512,640]{2,1,0:T(8,128)(2,1)S(1)} %get-tuple-element.40) | copy-start | bytes 7864324
  23.0 44.7 %copy-start.5 = (s32[16]{0:T(128)S(1)}, s32[16]{0:T(128)}, u32[]{:S(2)}) copy-start(s32[16]{0:T(128)} %lengths_ref.7) | copy-start | bytes 196
  29.3 8.4 %collective-permute-start.2 = (bf16[128,256]{1,0:T(8,128)(2,1)S(1)}, bf16[128,256]{1,0:T(8,128)(2,1)S(1)}, u32[]{:S(2)}, u32[]{:S(2)}) collective-permute-start(bf16[128,256]{1,0:T(8,128)(2,1)S(1)} %bitcast.51), channel_id=1, source_target_pairs={{0,48},{8,56},{16,0},{24,8},{32,16},{40,24},{48,32},{56,40},{64,11... | collective-permute-start | bytes 196616 | tf_op jit(solution)/shard_map/ppermute | solution.py:298
  34.5 7.2 %collective-permute-start.1 = (bf16[128,256]{1,0:T(8,128)(2,1)S(1)}, bf16[128,256]{1,0:T(8,128)(2,1)S(1)}, u32[]{:S(2)}, u32[]{:S(2)}) collective-permute-start(bf16[128,256]{1,0:T(8,128)(2,1)S(1)} %bitcast.52), channel_id=1, source_target_pairs={{0,32},{8,40},{16,48},{24,56},{32,0},{40,8},{48,16},{56,24},{64,96... | collective-permute-start | bytes 196616 | tf_op jit(solution)/shard_map/ppermute | solution.py:298
  35.6 6.0 %collective-permute-start = (bf16[128,256]{1,0:T(8,128)(2,1)S(1)}, bf16[128,256]{1,0:T(8,128)(2,1)S(1)}, u32[]{:S(2)}, u32[]{:S(2)}) collective-permute-start(bf16[128,256]{1,0:T(8,128)(2,1)S(1)} %bitcast.53), channel_id=1, source_target_pairs={{0,16},{8,24},{16,32},{24,40},{32,48},{40,56},{48,0},{56,8},{64,80... | collective-permute-start | bytes 196616 | tf_op jit(solution)/shard_map/ppermute | solution.py:298
  41.7 42.9 %collective-permute-start.16 = (bf16[4,512,640]{2,1,0:T(8,128)(2,1)}, bf16[4,512,640]{2,1,0:T(8,128)(2,1)S(1)}, u32[]{:S(2)}, u32[]{:S(2)}) collective-permute-start(bf16[4,512,640]{2,1,0:T(8,128)(2,1)} %copy-done.6), channel_id=1, source_target_pairs={{0,4},{8,60},{1,5},{9,61},{2,6},{10,62},{3,7},{11,63},{4,0},{12,24... | collective-permute-start | bytes 7864328 | tf_op jit(solution)/shard_map/ppermute | solution.py:300
  47.0 9.4 %collective-permute-start.3 = (bf16[4,128,256]{2,1,0:T(8,128)(2,1)S(1)}, bf16[4,128,256]{2,1,0:T(8,128)(2,1)S(1)}, u32[]{:S(2)}, u32[]{:S(2)}) collective-permute-start(bf16[4,128,256]{2,1,0:T(8,128)(2,1)S(1)} %pad_maximum_fusion.1.refs_0_), channel_id=1, source_target_pairs={{0,64},{8,72},{16,80},{24,88},{32,96},{40,104},{48,112},{56,120},{... | collective-permute-start | bytes 786440 | tf_op jit(solution)/shard_map/ppermute | solution.py:299
  48.2 14.8 %collective-permute-start.4 = (bf16[4,128,256]{2,1,0:T(8,128)(2,1)S(1)}, bf16[4,128,256]{2,1,0:T(8,128)(2,1)S(1)}, u32[]{:S(2)}, u32[]{:S(2)}) collective-permute-start(bf16[4,128,256]{2,1,0:T(8,128)(2,1)S(1)} %pad_maximum_fusion.1.refs_0_), channel_id=1, source_target_pairs={{0,128},{8,136},{16,144},{24,152},{32,160},{40,168},{48,176},{56,1... | collective-permute-start | bytes 786440 | tf_op jit(solution)/shard_map/ppermute | solution.py:299
  50.7 12.4 %collective-permute-start.5 = (bf16[4,128,256]{2,1,0:T(8,128)(2,1)S(1)}, bf16[4,128,256]{2,1,0:T(8,128)(2,1)S(1)}, u32[]{:S(2)}, u32[]{:S(2)}) collective-permute-start(bf16[4,128,256]{2,1,0:T(8,128)(2,1)S(1)} %pad_maximum_fusion.1.refs_0_), channel_id=1, source_target_pairs={{0,192},{8,200},{16,208},{24,216},{32,224},{40,232},{48,240},{56,2... | collective-permute-start | bytes 786440 | tf_op jit(solution)/shard_map/ppermute | solution.py:299
  64.1 2.2 %collective-permute-start.6 = (bf16[6,128,256]{2,1,0:T(8,128)(2,1)S(1)}, bf16[6,128,256]{2,1,0:T(8,128)(2,1)S(1)}, u32[]{:S(2)}, u32[]{:S(2)}) collective-permute-start(bf16[6,128,256]{2,1,0:T(8,128)(2,1)S(1)} %pick.2), channel_id=1, source_target_pairs={{0,8},{8,0},{16,24},{24,16},{32,40},{40,32},{48,56},{56,48},{64,72... | collective-permute-start | bytes 1179656 | tf_op jit(solution)/shard_map/ppermute | solution.py:303
  70.2 8.8 %collective-permute-start.7 = (bf16[128,1024]{1,0:T(8,128)(2,1)S(1)}, bf16[128,1024]{1,0:T(8,128)(2,1)S(1)}, u32[]{:S(2)}, u32[]{:S(2)}) collective-permute-start(bf16[128,1024]{1,0:T(8,128)(2,1)S(1)} %attend0.1.refs_0_), channel_id=1, source_target_pairs={{0,1},{1,2},{2,3},{3,0},{4,5},{5,6},{6,7},{7,4},{8,9},{9,10},{10,1... | collective-permute-start | bytes 786440 | tf_op jit(solution)/shard_map/ppermute | solution.py:307
  72.9 11.7 %collective-permute-start.10 = (bf16[128,1024]{1,0:T(8,128)(2,1)S(1)}, bf16[128,1024]{1,0:T(8,128)(2,1)S(1)}, u32[]{:S(2)}, u32[]{:S(2)}) collective-permute-start(bf16[128,1024]{1,0:T(8,128)(2,1)S(1)} %attend1.1.refs_4_), channel_id=1, source_target_pairs={{0,1},{1,2},{2,3},{3,0},{4,5},{5,6},{6,7},{7,4},{8,9},{9,10},{10,1... | collective-permute-start | bytes 786440 | tf_op jit(solution)/shard_map/ppermute | solution.py:307
  73.0 11.6 %collective-permute-start.11 = (bf16[128,1024]{1,0:T(8,128)(2,1)S(1)}, bf16[128,1024]{1,0:T(8,128)(2,1)S(1)}, u32[]{:S(2)}, u32[]{:S(2)}) collective-permute-start(bf16[128,1024]{1,0:T(8,128)(2,1)S(1)} %attend1.1.refs_4_), channel_id=1, source_target_pairs={{0,3},{1,0},{2,1},{3,2},{4,7},{5,4},{6,5},{7,6},{8,11},{9,8},{10,9... | collective-permute-start | bytes 786440 | tf_op jit(solution)/shard_map/ppermute | solution.py:310
  84.6 31.1 %collective-permute-start.17 = (bf16[4,512,640]{2,1,0:T(8,128)(2,1)S(1)}, bf16[4,512,640]{2,1,0:T(8,128)(2,1)S(1)}, u32[]{:S(2)}, u32[]{:S(2)}) collective-permute-start(bf16[4,512,640]{2,1,0:T(8,128)(2,1)S(1)} %collective-permute-done.16), channel_id=1, source_target_pairs={{0,8},{8,0},{16,24},{24,16},{32,40},{40,32},{48,56},{56,48},{64,72... | collective-permute-start | bytes 7864328 | tf_op jit(solution)/shard_map/ppermute | solution.py:327
  85.8 9.1 %collective-permute-start.13 = (bf16[128,1024]{1,0:T(8,128)(2,1)S(1)}, bf16[128,1024]{1,0:T(8,128)(2,1)S(1)}, u32[]{:S(2)}, u32[]{:S(2)}) collective-permute-start(bf16[128,1024]{1,0:T(8,128)(2,1)S(1)} %attend2.1.refs_8_), channel_id=1, source_target_pairs={{0,1},{1,2},{2,3},{3,0},{4,5},{5,6},{6,7},{7,4},{8,9},{9,10},{10,1... | collective-permute-start | bytes 786440 | tf_op jit(solution)/shard_map/ppermute | solution.py:307
  85.8 9.1 %collective-permute-start.8 = (bf16[128,1024]{1,0:T(8,128)(2,1)S(1)}, bf16[128,1024]{1,0:T(8,128)(2,1)S(1)}, u32[]{:S(2)}, u32[]{:S(2)}) collective-permute-start(bf16[128,1024]{1,0:T(8,128)(2,1)S(1)} %attend0.1.refs_0_), channel_id=1, source_target_pairs={{0,3},{1,0},{2,1},{3,2},{4,7},{5,4},{6,5},{7,6},{8,11},{9,8},{10,9... | collective-permute-start | bytes 786440 | tf_op jit(solution)/shard_map/ppermute | solution.py:310
  88.5 11.0 %collective-permute-start.14 = (bf16[128,1024]{1,0:T(8,128)(2,1)S(1)}, bf16[128,1024]{1,0:T(8,128)(2,1)S(1)}, u32[]{:S(2)}, u32[]{:S(2)}) collective-permute-start(bf16[128,1024]{1,0:T(8,128)(2,1)S(1)} %attend2.1.refs_8_), channel_id=1, source_target_pairs={{0,3},{1,0},{2,1},{3,2},{4,7},{5,4},{6,5},{7,6},{8,11},{9,8},{10,9... | collective-permute-start | bytes 786440 | tf_op jit(solution)/shard_map/ppermute | solution.py:310
  88.5 12.0 %collective-permute-start.9 = (bf16[128,1024]{1,0:T(8,128)(2,1)S(1)}, bf16[128,1024]{1,0:T(8,128)(2,1)S(1)}, u32[]{:S(2)}, u32[]{:S(2)}) collective-permute-start(bf16[128,1024]{1,0:T(8,128)(2,1)S(1)} %collective-permute-done.7.refs_1_), channel_id=1, source_target_pairs={{0,1},{1,2},{2,3},{3,0},{4,5},{5,6},{6,7},{7,4},{8,9},{9,10},{10,1... | collective-permute-start | bytes 786440 | tf_op jit(solution)/shard_map/ppermute | solution.py:307
  94.9 10.2 %collective-permute-start.12 = (bf16[128,1024]{1,0:T(8,128)(2,1)S(1)}, bf16[128,1024]{1,0:T(8,128)(2,1)S(1)}, u32[]{:S(2)}, u32[]{:S(2)}) collective-permute-start(bf16[128,1024]{1,0:T(8,128)(2,1)S(1)} %collective-permute-done.11.refs_6_), channel_id=1, source_target_pairs={{0,3},{1,0},{2,1},{3,2},{4,7},{5,4},{6,5},{7,6},{8,11},{9,8},{10,9... | collective-permute-start | bytes 786440 | tf_op jit(solution)/shard_map/ppermute | solution.py:310
  94.9 11.2 %collective-permute-start.15 = (bf16[128,1024]{1,0:T(8,128)(2,1)S(1)}, bf16[128,1024]{1,0:T(8,128)(2,1)S(1)}, u32[]{:S(2)}, u32[]{:S(2)}) collective-permute-start(bf16[128,1024]{1,0:T(8,128)(2,1)S(1)} %collective-permute-done.13.refs_9_), channel_id=1, source_target_pairs={{0,1},{1,2},{2,3},{3,0},{4,5},{5,6},{6,7},{7,4},{8,9},{9,10},{10,1... | collective-permute-start | bytes 786440 | tf_op jit(solution)/shard_map/ppermute | solution.py:307
  99.5 19.1 %collective-permute-start.19 = (bf16[128,1024]{1,0:T(8,128)(2,1)S(1)}, bf16[128,1024]{1,0:T(8,128)(2,1)S(1)}, u32[]{:S(2)}, u32[]{:S(2)}) collective-permute-start(bf16[128,1024]{1,0:T(8,128)(2,1)S(1)} %attend3.1.refs_0_), channel_id=1, source_target_pairs={{0,1},{1,2},{2,3},{3,0},{4,5},{5,6},{6,7},{7,4},{8,9},{9,10},{10,1... | collective-permute-start | bytes 786440 | tf_op jit(solution)/shard_map/ppermute | solution.py:307
  100.5 12.8 %collective-permute-start.20 = (bf16[128,1024]{1,0:T(8,128)(2,1)S(1)}, bf16[128,1024]{1,0:T(8,128)(2,1)S(1)}, u32[]{:S(2)}, u32[]{:S(2)}) collective-permute-start(bf16[128,1024]{1,0:T(8,128)(2,1)S(1)} %attend3.1.refs_0_), channel_id=1, source_target_pairs={{0,3},{1,0},{2,1},{3,2},{4,7},{5,4},{6,5},{7,6},{8,11},{9,8},{10,9... | collective-permute-start | bytes 786440 | tf_op jit(solution)/shard_map/ppermute | solution.py:310
  108.1 3.7 %copy-start.7 = (bf16[4,512,640]{2,1,0:T(8,128)(2,1)S(1)}, bf16[4,512,640]{2,1,0:T(8,128)(2,1)}, u32[]{:S(2)}) copy-start(bf16[4,512,640]{2,1,0:T(8,128)(2,1)} %get-tuple-element.36) | copy-start | bytes 7864324
  108.1 3.8 %copy-start.9 = (bf16[384,2048]{1,0:T(8,128)(2,1)S(1)}, bf16[384,2048]{1,0:T(8,128)(2,1)}, u32[]{:S(2)}) copy-start(bf16[384,2048]{1,0:T(8,128)(2,1)} %get-tuple-element.39) | copy-start | bytes 4718596
  111.8 3.9 %copy-start.10 = (bf16[384,2048]{1,0:T(8,128)(2,1)S(1)}, bf16[384,2048]{1,0:T(8,128)(2,1)}, u32[]{:S(2)}) copy-start(bf16[384,2048]{1,0:T(8,128)(2,1)} %get-tuple-element.41) | copy-start | bytes 4718596
  113.3 6.6 %collective-permute-start.21 = (bf16[128,1024]{1,0:T(8,128)(2,1)S(1)}, bf16[128,1024]{1,0:T(8,128)(2,1)S(1)}, u32[]{:S(2)}, u32[]{:S(2)}) collective-permute-start(bf16[128,1024]{1,0:T(8,128)(2,1)S(1)} %collective-permute-done.20.refs_2_), channel_id=1, source_target_pairs={{0,3},{1,0},{2,1},{3,2},{4,7},{5,4},{6,5},{7,6},{8,11},{9,8},{10,9... | collective-permute-start | bytes 786440 | tf_op jit(solution)/shard_map/ppermute | solution.py:310
  121.1 2.2 %copy-start.8 = (bf16[4,512,640]{2,1,0:T(8,128)(2,1)S(1)}, bf16[4,512,640]{2,1,0:T(8,128)(2,1)}, u32[]{:S(2)}) copy-start(bf16[4,512,640]{2,1,0:T(8,128)(2,1)} %get-tuple-element.38) | copy-start | bytes 7864324
  121.1 4.3 %collective-permute-start.22 = (bf16[128,640]{1,0:T(8,128)(2,1)S(1)}, bf16[128,640]{1,0:T(8,128)(2,1)S(1)}, u32[]{:S(2)}, u32[]{:S(2)}) collective-permute-start(bf16[128,640]{1,0:T(8,128)(2,1)S(1)} %fusion.1), channel_id=1, source_target_pairs={{0,4},{1,5},{2,6},{3,7},{4,0},{5,1},{6,2},{7,3},{8,12},{9,13},{10,... | collective-permute-start | bytes 491528 | tf_op jit(solution)/shard_map/ppermute | solution.py:336
  121.2 13.8 %collective-permute-start.18 = (bf16[384,640]{1,0:T(8,128)(2,1)S(1)}, bf16[384,640]{1,0:T(8,128)(2,1)S(1)}, u32[]{:S(2)}, u32[]{:S(2)}) collective-permute-start(bf16[384,640]{1,0:T(8,128)(2,1)S(1)} %fusion), channel_id=1, source_target_pairs={{0,4},{1,5},{2,6},{3,7},{4,0},{5,1},{6,2},{7,3},{8,12},{9,13},{10,... | collective-permute-start | bytes 1474568 | tf_op jit(solution)/shard_map/ppermute | solution.py:332

commit v2 on v1

v2 whole, which is shorter than its diff:
```python
import functools
import math

import jax
import jax.numpy as jnp
from jax import lax
from jax.experimental import pallas as pl
from jax.experimental.pallas import tpu as pltpu
from jax.sharding import PartitionSpec as P

KVH = 8
GROUP = 8
HD = 128
CAP = 128
DEPTH = 6
SEGS = 16
TOK = 64
UNITS = 4
QROWS = 4 * TOK
MASKED = -1e30
VMEM_LIMIT = 48 * 1024 * 1024

Z_SWAP = [(s, (s + 4) % 8) for s in range(8)]
CORE_SWAP = [(l, l ^ 1) for l in range(32)]


def y_shift(k):
    return [(z * 4 + y, z * 4 + (y + k) % 4) for z in range(2) for y in range(4)]


def x_shift(k):
    return [(l, (l + 8 * k) % 32) for l in range(32)]


def z_shift(k):
    return [
        ((x * 4 + z) * 2 + c, (x * 4 + (z + k) % 4) * 2 + c)
        for x in range(4)
        for z in range(4)
        for c in range(2)
    ]


def weight_pairs(cores):
    pairs = []
    for x in range(4):
        for h in range(4):
            for zl in range(2):
                for y in range(4):
                    for c in range(2):
                        h_to = h if c in cores else (h - 1 + 2 * zl) % 4
                        source = ((x * 4 + h) * 2 + c) * 8 + zl * 4 + y
                        target = ((x * 4 + h_to) * 2 + c) * 8 + (1 - zl) * 4 + y
                        pairs.append((source, target))
    return pairs


SMALL = pl.CostEstimate(flops=1, bytes_accessed=1, transcendentals=0)


def params():
    return pltpu.CompilerParams(vmem_limit_bytes=VMEM_LIMIT)


def whole():
    return pl.BlockSpec(memory_space=pltpu.VMEM)


def anywhere():
    return pl.BlockSpec(memory_space=pl.ANY)


def scalars():
    return pl.BlockSpec(memory_space=pltpu.SMEM)


def chase(parent_ref, leaf):
    segment = parent_ref[SEGS + leaf]
    ancestry = [segment]
    for _ in range(DEPTH - 1):
        segment = parent_ref[segment]
        ancestry.append(segment)
    return ancestry


def pack_rows_body(kv_hbm, cache_hbm, *refs):
    received, (out_ref, kv_ref, cache_ref, sem) = refs[:3], refs[3:]
    copies = [
        pltpu.make_async_copy(kv_hbm.at[0], kv_ref, sem.at[0]),
        pltpu.make_async_copy(cache_hbm, cache_ref, sem.at[1]),
    ]
    for copy in copies:
        copy.start()
    for copy in copies:
        copy.wait()
    for t in range(KVH):
        for half in range(2):
            lo = half * KVH * HD + t * HD
            cols = slice(half * HD, (half + 1) * HD)
            out_ref[t, :TOK, cols] = kv_ref[:, lo : lo + HD]
            for k, slot_ref in enumerate((cache_ref, *received)):
                out_ref[t, TOK + 16 * k : TOK + 16 * (k + 1), cols] = slot_ref[:, lo : lo + HD]


def pack_rows(leaf_kv, cache, received):
    return pl.pallas_call(
        pack_rows_body,
        out_shape=jax.ShapeDtypeStruct((KVH, 2 * TOK, 256), jnp.bfloat16),
        in_specs=[pl.BlockSpec(memory_space=pltpu.HBM)] * 2 + [whole()] * 3,
        out_specs=whole(),
        scratch_shapes=[
            pltpu.VMEM(leaf_kv.shape[1:], jnp.bfloat16),
            pltpu.VMEM(cache.shape, jnp.bfloat16),
            pltpu.SemaphoreType.DMA((2,)),
        ],
        compiler_params=params(),
        cost_estimate=SMALL,
        name="pack_rows",
    )(leaf_kv, cache, *received)


def pack_queries_body(ids_ref, parent_ref, lengths_ref, q_ref, out_ref, bias_ref):
    for t in range(KVH):
        for j in range(4):
            lo = t * GROUP * HD + j * 256
            out_ref[t, j * TOK : (j + 1) * TOK, :] = q_ref[:, lo : lo + 256]
    lane = lax.broadcasted_iota(jnp.int32, (1, CAP), 1)
    for a, segment in enumerate(chase(parent_ref, ids_ref[0])):
        bias_ref[:, a * CAP : (a + 1) * CAP] = jnp.where(lane < lengths_ref[segment], 0.0, MASKED)


def pack_queries(ids, parent, lengths, queries):
    return pl.pallas_call(
        pack_queries_body,
        out_shape=[
            jax.ShapeDtypeStruct((KVH, QROWS, 256), jnp.bfloat16),
            jax.ShapeDtypeStruct((1, DEPTH * CAP), jnp.float32),
        ],
        in_specs=[scalars()] * 3 + [whole()],
        out_specs=[whole()] * 2,
        compiler_params=params(),
        cost_estimate=SMALL,
        name="pack_queries",
    )(ids, parent, lengths, queries)


def order_body(count, ids_ref, in_ref, *out_refs):
    step = pl.program_id(0)
    for i, out_ref in enumerate(out_refs):

        @pl.when(step // 4 == i)
        def _():
            out_ref[0] = in_ref[0, 0]


def order(ids, weight, here, places):
    cols = weight.shape[1]
    count = len(places)
    first, step = places[0], 1

    def source(i, ids):
        plane = ids[2] if here else 1 - ids[2]
        place = first + step * (i // 4)
        quarter = place + ids[8] * (1 - 2 * lax.rem(place, 2))
        return (plane * 4 + ids[4 + lax.rem(i, 4)], quarter, 0, 0)

    def target(part):
        return lambda i, ids: (jnp.clip(i - 4 * part, 0, 3), 0, 0)

    return pl.pallas_call(
        functools.partial(order_body, count),
        out_shape=[jax.ShapeDtypeStruct((4, 256, cols), jnp.bfloat16)] * count,
        grid_spec=pltpu.PrefetchScalarGridSpec(
            num_scalar_prefetch=1,
            grid=(4 * count,),
            in_specs=[pl.BlockSpec((1, 1, 256, cols), source)],
            out_specs=[pl.BlockSpec((1, 256, cols), target(part)) for part in range(count)],
        ),
        compiler_params=params(),
        cost_estimate=SMALL,
        name="order",
    )(ids, weight.reshape(KVH, 4, 256, cols))


def join_body(ids_ref, own_ref, up_ref, down_ref, low_ref, high_ref, *outs):
    tokens = 2 * TOK
    for place in range(4):
        quarter = place + ids_ref[8] * (1 - 2 * (place % 2))
        cols = pl.ds(pl.multiple_of(quarter * 256, 256), 256)
        for k, part_ref in enumerate((own_ref, up_ref, down_ref)):
            outs[place][:, 256 * k : 256 * (k + 1)] = part_ref[:, cols]
        outs[place][:tokens, 768:] = low_ref[:, cols]
        outs[place][tokens:, 768:] = high_ref[:, cols]


def join(ids, *parts):
    return pl.pallas_call(
        join_body,
        out_shape=[jax.ShapeDtypeStruct((4 * TOK, 1024), jnp.bfloat16)] * 4,
        in_specs=[scalars()] + [whole()] * 5,
        out_specs=[whole()] * 4,
        compiler_params=params(),
        cost_estimate=SMALL,
        name="join",
    )(ids, *parts)


def pick_body(ids_ref, parent_ref, owner_ref, *refs):
    columns, outs, sem = refs[:4], refs[4:6], refs[6]
    leaf = ids_ref[0]
    core = lax.rem(leaf, 2)
    x = lax.div(leaf, 8)
    for act in ("start", "wait"):
        for i, target in enumerate((leaf + 1 - 2 * core, leaf)):
            for a, segment in enumerate(chase(parent_ref, target)):
                slot = owner_ref[segment]
                here = lax.rem(slot, 2) == core
                near_x = lax.rem(x - lax.div(slot, 8) + 4, 4)
                near_z = lax.rem(lax.rem(lax.div(leaf, 2), 4) - lax.rem(lax.div(slot, 2), 4) + 4, 4)
                rows = pl.ds(pl.multiple_of(near_z * 16, 16), 16)
                for k in range(4):

                    @pl.when(jnp.logical_and(here, near_x == k))
                    def _():
                        copy = pltpu.make_async_copy(columns[k].at[:, rows], outs[i].at[a], sem.at[i, a])
                        getattr(copy, act)()


def pick(ids, parent, owner, columns):
    return pl.pallas_call(
        pick_body,
        out_shape=[jax.ShapeDtypeStruct((DEPTH, KVH, 16, 256), jnp.bfloat16)] * 2,
        in_specs=[scalars()] * 3 + [anywhere()] * 4,
        out_specs=[anywhere()] * 2,
        scratch_shapes=[pltpu.SemaphoreType.DMA((2, DEPTH))],
        compiler_params=params(),
        cost_estimate=SMALL,
        name="pick",
    )(ids, parent, owner, *columns)


def merge_body(ids_ref, parent_ref, owner_ref, own_ref, received_ref, out_ref, sem):
    core = lax.rem(ids_ref[0], 2)
    for act in ("start", "wait"):
        for a, segment in enumerate(chase(parent_ref, ids_ref[0])):
            here = lax.rem(owner_ref[segment], 2) == core

            @pl.when(here)
            def _():
                getattr(pltpu.make_async_copy(own_ref.at[a], out_ref.at[a], sem.at[a]), act)()

            @pl.when(jnp.logical_not(here))
            def _():
                getattr(pltpu.make_async_copy(received_ref.at[a], out_ref.at[a], sem.at[a]), act)()


def merge(ids, parent, owner, own, received):
    return pl.pallas_call(
        merge_body,
        out_shape=jax.ShapeDtypeStruct((DEPTH, KVH, 16, 256), jnp.bfloat16),
        in_specs=[scalars()] * 3 + [anywhere()] * 2,
        out_specs=anywhere(),
        scratch_shapes=[pltpu.SemaphoreType.DMA((DEPTH,))],
        compiler_params=params(),
        cost_estimate=SMALL,
        name="merge",
    )(ids, parent, owner, own, received)


def attend_body(chunk, bias_ref, mine_ref, rows_ref, cache_ref, out_ref):
    for i in range(2):
        attend_unit(2 * chunk + i, 2 * TOK * i, bias_ref, mine_ref, rows_ref, cache_ref, out_ref)


def attend_unit(unit, top, bias_ref, mine_ref, rows_ref, cache_ref, out_ref):
    first = 2 * unit
    tokens = 2 * TOK
    scale = math.log2(math.e) / math.sqrt(HD)
    bias = bias_ref[...]
    cache_keys = cache_ref[:, :, :, :HD].reshape(DEPTH * CAP, HD)
    cache_values = cache_ref[:, :, :, HD:].reshape(DEPTH * CAP, HD)
    leaf_keys = rows_ref[: first + 2, :TOK, :HD].reshape(-1, HD)
    leaf_values = rows_ref[: first + 2, :TOK, HD:].reshape(-1, HD)
    keys = jnp.concatenate([cache_keys, leaf_keys], axis=0)
    values = jnp.concatenate([cache_values, leaf_values], axis=0)
    row = lax.broadcasted_iota(jnp.int32, (tokens, tokens), 0)
    col = lax.broadcasted_iota(jnp.int32, (tokens, tokens), 1)
    causal = jnp.where(col <= row, 0.0, MASKED)
    per = 4
    causal = jnp.concatenate([causal] * per, axis=0)
    for tile in range(GROUP // per):
        rows = []
        for g in range(tile * per, (tile + 1) * per):
            j, half = g // 2, g % 2
            part = mine_ref[first : first + 2, j * TOK : (j + 1) * TOK, half * HD : (half + 1) * HD]
            rows.append(part.reshape(tokens, HD))
        scores = lax.dot_general(
            jnp.concatenate(rows, axis=0), keys, (((1,), (1,)), ((), ())), preferred_element_type=jnp.float32
        )
        seen = DEPTH * CAP
        diagonal = seen + unit * tokens
        parts = [scores[:, :seen] + bias]
        if unit:
            parts.append(scores[:, seen:diagonal])
        parts.append(scores[:, diagonal:] + causal)
        scores = jnp.concatenate(parts, axis=1)
        largest = jnp.max(scores, axis=1, keepdims=True)
        expon = jnp.exp2((scores - largest) * scale)
        total = jnp.sum(expon, axis=1, keepdims=True)
        summed = jnp.dot(expon.astype(jnp.bfloat16), values, preferred_element_type=jnp.float32)
        done = (summed / total).astype(jnp.bfloat16)
        for i in range(per):
            g = tile * per + i
            out_ref[top : top + tokens, g * HD : (g + 1) * HD] = done[i * tokens : (i + 1) * tokens]


def attend(chunk, bias, mine, rows, cache_rows):
    return pl.pallas_call(
        functools.partial(attend_body, chunk),
        out_shape=jax.ShapeDtypeStruct((4 * TOK, GROUP * HD), jnp.bfloat16),
        in_specs=[whole()] * 4,
        out_specs=whole(),
        compiler_params=params(),
        cost_estimate=pl.CostEstimate(flops=1_500_000_000, bytes_accessed=1, transcendentals=2_500_000),
        name=f"attend{chunk}",
    )(bias, mine, rows, cache_rows)


def after(value, *earlier):
    return lax.optimization_barrier((value, earlier))[0]


def project(blocks, matrices):
    total = None
    for rows, matrix in zip(blocks, matrices):
        product = jnp.dot(rows, matrix.reshape(rows.shape[1], -1), preferred_element_type=jnp.float32)
        total = product if total is None else total + product
    return total


def per_device(queries, leaf_kv, cache, out_weight, parent, owner, lengths):
    leaf = lax.axis_index("leaf")
    seq = lax.axis_index("seq")
    z, y, core = seq // 4, seq % 4, leaf % 2
    ids = jnp.stack([leaf, seq, z, y, y, (y + 3) % 4, (y + 1) % 4, (y + 2) % 4, core]).astype(jnp.int32)

    slots = [lax.ppermute(cache, "leaf", z_shift(k)) for k in (1, 2, 3)]
    (sent0,) = order(after(ids, slots[0]), out_weight, False, (0,))
    rows = lax.all_to_all(pack_rows(leaf_kv, cache, after(slots, sent0)), "seq", 0, 0)
    (sent2,) = order(after(ids, slots), out_weight, False, (2,))
    packed, bias = pack_queries(after(ids, sent2), parent, lengths, queries[0])
    column = after(rows[:, TOK:, :], packed)
    columns = [column] + [lax.ppermute(column, "leaf", x_shift(k)) for k in (1, 2, 3)]
    mine = lax.all_to_all(after(packed, rows), "seq", 0, 0)
    matrix = order(after(ids, column), out_weight, True, (0, 1, 2, 3))

    given, own = pick(after(ids, matrix), parent, owner, columns)
    received = lax.ppermute(given, "leaf", CORE_SWAP)
    cache_rows = merge(ids, parent, owner, own, received)
    near0 = lax.ppermute(after(sent0, given), ("leaf", "seq"), weight_pairs((0,)))
    near2 = lax.ppermute(after(sent2, given), ("leaf", "seq"), weight_pairs((0,)))

    def up(part):
        return lax.ppermute(part, "seq", y_shift(1))

    def down(part):
        return lax.ppermute(part, "seq", y_shift(-1))

    half = 2 * TOK
    low = attend(0, bias, mine, rows, cache_rows)
    low_up, low_down = up(low), down(low)
    high = attend(1, bias, mine, rows, after(cache_rows, low))
    high_up, high_down = up(high), down(high)
    low_far = up(after(low_up, high)[:half]), down(after(low_down, high)[half:])
    near1 = lax.ppermute(after(near0, low_up, low_down, high), "leaf", CORE_SWAP)
    near3 = lax.ppermute(after(near2, low_far, high_up, high_down), "leaf", CORE_SWAP)
    near = (near0, near1, near2, near3)
    high_far = up(after(high_up, low_far)[:half]), down(after(high_down, low_far)[half:])

    rows_low = join(ids, low, low_up, low_down, *low_far)
    other_low = project(rows_low, near).astype(jnp.bfloat16)
    mine_low = project(after(rows_low, other_low), matrix)
    other_low = lax.ppermute(other_low, "seq", Z_SWAP)
    result_low = mine_low + other_low.astype(jnp.float32)
    rows_high = join(after(ids, mine_low), high, high_up, high_down, *high_far)
    other_high = project(rows_high, near).astype(jnp.bfloat16)
    mine_high = project(after(rows_high, other_high, other_low), matrix)
    result_high = mine_high + lax.ppermute(other_high, "seq", Z_SWAP).astype(jnp.float32)
    return jnp.concatenate([result_low, result_high], axis=0).astype(jnp.bfloat16)[None]


def solution(mesh):
    in_specs = (
        P("leaf", "seq", None),
        P("leaf", "seq", None),
        P(("leaf", "seq"), None),
        P(None, "seq"),
        P(),
        P(),
        P(),
    )
    out_specs = P("leaf", None, "seq")
    return jax.shard_map(per_device, mesh=mesh, in_specs=in_specs, out_specs=out_specs, check_vma=False)
```

time: 138 us -> 128 us (0.928); the launches traced: 136 us -> 128 us
  waiting for transfers between devices: 50.1 us -> 33 us
  Pallas kernels: 27.7 us -> 34.6 us
  matrix products: 10.3 us -> 14.8 us
  local copies, waits for them, and re-layouts: 4.63 us -> 3.06 us
    ppermute x6 -> x8, waiting for transfers between devices: 13.6 us -> 3.68 us  [the longest x1 2.37 us: per_device(): lax.ppermute(after(sent2, given), ('leaf', 'seq'), weight_pairs((0,)))]
    ppermute x3, waiting for transfers between devices: 11.2 us -> 2.95 us  [per_device(): lax.ppermute(column, 'leaf', x_shift(k))]
    pallas_call x10 -> x11, Pallas kernels: 27.7 us -> 34.6 us  [the longest x3 17.2 us: order(): pl.pallas_call(functools.partial(order_body, count), out_shape=[jax.Shape...]
    ppermute x6 -> x4, starting transfers between devices: 10.4 us -> 5.56 us  [down(): return lax.ppermute(part, 'seq', y_shift(-1))]
    dot_general x8 -> x16, matrix products: 10.3 us -> 14.8 us  [project(): jnp.dot(rows, matrix.reshape(rows.shape[1], -1), preferred_element_type=j...]
    all_to_all x1 -> x2, waiting for transfers between devices: 6.37 us -> 2.18 us  [the longest x1 2.17 us: per_device(): lax.all_to_all(pack_rows(leaf_kv, cache, after(slots, sent0)), 'seq', 0, 0)]
    ppermute x1, waiting for transfers between devices: 1.51 us -> 5.38 us  [per_device(): lax.ppermute(other_high, 'seq', Z_SWAP).astype(jnp.float32)]
    all_to_all x1 -> x2, starting transfers between devices: 6.39 us -> 9.37 us  [the longest x1 5.16 us: per_device(): mine = lax.all_to_all(after(packed, rows), 'seq', 0, 0)]
  transfers between devices with their start and end apart: 24 -> 23, of which waited for: 14 -> 12; matrix products, arithmetic and copies ran while one was open for 7% -> 11% of each run, Pallas kernels for 19% -> 26%
where the time goes in v2:
time: 128 us
  starting transfers between devices  40.8 us (32%)
  Pallas kernels  34.6 us (27%)
  waiting for transfers between devices  33 us (26%)
  matrix products  14.8 us (12%)
  local copies, waits for them, and re-layouts  3.06 us (2%)
    pallas_call x3, Pallas kernels, order(): pl.pallas_call(functools.partial(order_body, count), out_shape=[jax.Shape...  17.2 us
    dot_general x16, matrix products, project(): jnp.dot(rows, matrix.reshape(rows.shape[1], -1), preferred_element_type=j...  14.8 us
    ppermute x3, starting transfers between devices, per_device(): slots = [lax.ppermute(cache, 'leaf', z_shift(k)) for k in (1, 2, 3)]  11.3 us
    pallas_call x2, Pallas kernels, attend(): pl.pallas_call(functools.partial(attend_body, chunk), out_shape=jax.Shape...  10.6 us
    ppermute x4, waiting for transfers between devices, up(): return lax.ppermute(part, 'seq', y_shift(1))  9.28 us
    ppermute x4, waiting for transfers between devices, down(): return lax.ppermute(part, 'seq', y_shift(-1))  7.77 us
    ppermute x4, starting transfers between devices, down(): return lax.ppermute(part, 'seq', y_shift(-1))  5.56 us
    ppermute x1, waiting for transfers between devices, per_device(): lax.ppermute(other_high, 'seq', Z_SWAP).astype(jnp.float32)  5.38 us
  transfers between devices with their start and end apart: 23, of which 12 were waited for; matrix products, arithmetic and copies ran while one was open for 11% of the time, Pallas kernels for 26%

profile of v2, /device:TPU:1, one launch (start us, length us, event | category | flops | bytes accessed | tf_op | source)
XLA Modules:
  0.0 127.6 jit_solution(5838273858868324290)
XLA Ops:
  0.0 3.8 %collective-permute-start = (bf16[16,2048]{1,0:T(8,128)(2,1)}, bf16[16,2048]{1,0:T(8,128)(2,1)S(1)}, u32[]{:S(2)}, u32[]{:S(2)}) collective-permute-start(bf16[16,2048]{1,0:T(8,128)(2,1)} %cache_hbm.1), channel_id=1, source_target_pairs={{0,16},{8,24},{16,32},{24,40},{32,48},{40,56},{48,0},{56,8},{64,80... | collective-permute-start | bytes 196616 | tf_op jit(solution)/shard_map/ppermute | solution.py:347
  3.8 5.1 %collective-permute-start.1 = (bf16[16,2048]{1,0:T(8,128)(2,1)}, bf16[16,2048]{1,0:T(8,128)(2,1)S(1)}, u32[]{:S(2)}, u32[]{:S(2)}) collective-permute-start(bf16[16,2048]{1,0:T(8,128)(2,1)} %cache_hbm.1), channel_id=1, source_target_pairs={{0,32},{8,40},{16,48},{24,56},{32,0},{40,8},{48,16},{56,24},{64,96... | collective-permute-start | bytes 196616 | tf_op jit(solution)/shard_map/ppermute | solution.py:347
  8.9 2.4 %collective-permute-start.2 = (bf16[16,2048]{1,0:T(8,128)(2,1)}, bf16[16,2048]{1,0:T(8,128)(2,1)S(1)}, u32[]{:S(2)}, u32[]{:S(2)}) collective-permute-start(bf16[16,2048]{1,0:T(8,128)(2,1)} %cache_hbm.1), channel_id=1, source_target_pairs={{0,48},{8,56},{16,0},{24,8},{32,16},{40,24},{48,32},{56,40},{64,11... | collective-permute-start | bytes 196616 | tf_op jit(solution)/shard_map/ppermute | solution.py:347
  11.4 4.1 %order.4 = bf16[4,256,640]{2,1,0:T(8,128)(2,1)} custom-call(s32[9]{0:T(128)S(1)} %stack.36.ids_ref, bf16[8,4,256,640]{3,2,1,0:T(8,128)(2,1)} %bitcast.63), custom_call_target="tpu_custom_call" | custom-call | flops 1 | bytes 1 | tf_op jit(solution)/shard_map/order/pallas_call | solution.py:170
  15.5 1.3 %collective-permute-done.2.refs_2_ = bf16[16,2048]{1,0:T(8,128)(2,1)S(1)} collective-permute-done((bf16[16,2048]{1,0:T(8,128)(2,1)}, bf16[16,2048]{1,0:T(8,128)(2,1)S(1)}, u32[]{:S(2)}, u32[]{:S(2)}) %collective-permute-start.2) | collective-permute-done | bytes 65568 | tf_op jit(solution)/shard_map/ppermute | solution.py:347
  16.8 1.0 pack_rows.1
  17.8 4.2 %all-to-all-start = ((bf16[8,128,256]{2,1,0:T(8,128)(2,1)}), bf16[8,128,256]{2,1,0:T(8,128)(2,1)S(1)}, u32[]{:S(2)}, u32[]{:S(2)}) async-start(bf16[8,128,256]{2,1,0:T(8,128)(2,1)} %pack_rows.1), calls=%async_computation | async-start | bytes 1048576 | tf_op jit(solution)/shard_map/all_to_all | solution.py:349
  22.0 4.0 %order.3 = bf16[4,256,640]{2,1,0:T(8,128)(2,1)} custom-call(s32[9]{0:T(128)S(1)} %stack.36.ids_ref, bf16[8,4,256,640]{3,2,1,0:T(8,128)(2,1)} %bitcast.64), custom_call_target="tpu_custom_call" | custom-call | flops 1 | bytes 1 | tf_op jit(solution)/shard_map/order/pallas_call | solution.py:170
  26.1 1.6 %pack_queries.1 = (bf16[8,256,256]{2,1,0:T(8,128)(2,1)}, f32[1,768]{1,0:T(1,128)S(1)}) custom-call(s32[9]{0:T(128)S(1)} %stack.36.ids_ref, s32[48]{0:T(128)S(1)} %copy-done.7, s32[16]{0:T(128)S(1)} %copy-done.9, bf16[64,8192]{1,0:T(8,128)(2,1)S(1)} %bitcast.62), custom_call_target="tpu_custom_call" | custom-call | flops 1 | bytes 1 | tf_op jit(solution)/shard_map/pack_queries/pallas_call | solution.py:133
  27.7 2.2 %all-to-all-done.rows_ref = bf16[8,128,256]{2,1,0:T(8,128)(2,1)S(1)} async-done(((bf16[8,128,256]{2,1,0:T(8,128)(2,1)}), bf16[8,128,256]{2,1,0:T(8,128)(2,1)S(1)}, u32[]{:S(2)}, u32[]{:S(2)}) %all-to-all-start) | async-done | bytes 524320 | tf_op jit(solution)/shard_map/all_to_all | solution.py:349
  29.9 5.2 %all-to-all-start.1 = ((bf16[8,256,256]{2,1,0:T(8,128)(2,1)}), bf16[8,256,256]{2,1,0:T(8,128)(2,1)}, u32[]{:S(2)}, u32[]{:S(2)}) async-start(bf16[8,256,256]{2,1,0:T(8,128)(2,1)} %get-tuple-element.57), calls=%async_computation.1 | async-start | bytes 2097152 | tf_op jit(solution)/shard_map/all_to_all | solution.py:354
  35.1 2.6 %collective-permute-start.5 = (bf16[8,64,256]{2,1,0:T(8,128)(2,1)S(1)}, bf16[8,64,256]{2,1,0:T(8,128)(2,1)S(1)}, u32[]{:S(2)}, u32[]{:S(2)}) collective-permute-start(bf16[8,64,256]{2,1,0:T(8,128)(2,1)S(1)} %slice.20.refs_0_), channel_id=1, source_target_pairs={{0,192},{8,200},{16,208},{24,216},{32,224},{40,232},{48,240},{56,2... | collective-permute-start | bytes 786440 | tf_op jit(solution)/shard_map/ppermute | solution.py:353
  38.1 0.6 collective-permute-start.3
  38.7 9.1 %order.5 = (bf16[4,256,640]{2,1,0:T(8,128)(2,1)S(1)}, bf16[4,256,640]{2,1,0:T(8,128)(2,1)S(1)}, bf16[4,256,640]{2,1,0:T(8,128)(2,1)S(1)}, bf16[4,256,640]{2,1,0:T(8,128)(2,1)S(1)}) custom-call(s32[9]{0:T(128)S(1)} %stack.36.ids_ref, bf16[8,4,256,640]{3,2,1,0:T(8,128)(2,1)} %bitcast.65), custom_call_target="tpu_custom_call" | custom-call | flops 1 | bytes 1 | tf_op jit(solution)/shard_map/order/pallas_call | solution.py:170
  47.9 1.0 copy-done
  48.9 1.1 copy-done.2
  50.0 2.9 %collective-permute-done.3.refs_1_ = bf16[8,64,256]{2,1,0:T(8,128)(2,1)S(1)} collective-permute-done((bf16[8,64,256]{2,1,0:T(8,128)(2,1)S(1)}, bf16[8,64,256]{2,1,0:T(8,128)(2,1)S(1)}, u32[]{:S(2)}, u32[]{:S(2)}) %collective-permute-start.3) | collective-permute-done | bytes 262176 | tf_op jit(solution)/shard_map/ppermute | solution.py:353
  53.0 1.3 %pick.1 = (bf16[6,8,16,256]{3,2,1,0:T(8,128)(2,1)S(1)}, bf16[6,8,16,256]{3,2,1,0:T(8,128)(2,1)S(1)}) custom-call(s32[9]{0:T(128)S(1)} %stack.36.ids_ref, s32[48]{0:T(128)S(1)} %copy-done.7, s32[16]{0:T(128)S(1)} %copy-done.8, bf16[8,64,256]{2,1,0:T(8,128)(2,1)S(1)} %slice.20.refs_0_, bf16[8,64,256]{2,1,0:T(8,128)(2,1)S(1)} %collective-permute-done.3.refs_1_, ...), custom_call_target="tpu_custom_call" | custom-call | flops 1 | bytes 1 | tf_op jit(solution)/shard_map/pick/pallas_call | solution.py:230
  54.3 3.3 %collective-permute-start.11 = (bf16[4,256,640]{2,1,0:T(8,128)(2,1)}, bf16[4,256,640]{2,1,0:T(8,128)(2,1)}, u32[]{:S(2)}, u32[]{:S(2)}) collective-permute-start(bf16[4,256,640]{2,1,0:T(8,128)(2,1)} %order.4), channel_id=1, source_target_pairs={{0,4},{8,60},{1,5},{9,61},{2,6},{10,62},{3,7},{11,63},{4,0},{12,24... | collective-permute-start | bytes 3932168 | tf_op jit(solution)/shard_map/ppermute | solution.py:360
  57.7 1.7 %collective-permute-done.6.received_ref = bf16[6,8,16,256]{3,2,1,0:T(8,128)(2,1)S(1)} collective-permute-done((bf16[6,8,16,256]{3,2,1,0:T(8,128)(2,1)S(1)}, bf16[6,8,16,256]{3,2,1,0:T(8,128)(2,1)S(1)}, u32[]{:S(2)}, u32[]{:S(2)}) %collective-permute-start.6) | collective-permute-done | bytes 393248 | tf_op jit(solution)/shard_map/ppermute | solution.py:358
  59.4 1.3 merge.1.cache_ref
  60.7 4.9 %attend0.1.own_ref = bf16[256,1024]{1,0:T(8,128)(2,1)S(1)} custom-call(f32[1,768]{1,0:T(1,128)S(1)} %get-tuple-element.51.bias_ref, bf16[8,256,256]{2,1,0:T(8,128)(2,1)} %all-to-all-done.1.mine_ref, bf16[8,128,256]{2,1,0:T(8,128)(2,1)S(1)} %all-to-all-done.rows_ref, bf16[6,8,16,256]{3,2,1,0:T(8,128)(2,1)S(1)} %merge.1.cache_ref), custom_call_target="tpu_custom_call" | custom-call | flops 1500000000 | bytes 1 | tf_op jit(solution)/shard_map/attend0/pallas_call | solution.py:318
  65.6 2.6 %collective-permute-start.8 = (bf16[256,1024]{1,0:T(8,128)(2,1)S(1)}, bf16[256,1024]{1,0:T(8,128)(2,1)S(1)}, u32[]{:S(2)}, u32[]{:S(2)}) collective-permute-start(bf16[256,1024]{1,0:T(8,128)(2,1)S(1)} %attend0.1.own_ref), channel_id=1, source_target_pairs={{0,3},{1,0},{2,1},{3,2},{4,7},{5,4},{6,5},{7,6},{8,11},{9,8},{10,9... | collective-permute-start | bytes 1572872 | tf_op jit(solution)/shard_map/ppermute | solution.py:367
  68.2 5.7 %attend1.1.own_ref = bf16[256,1024]{1,0:T(8,128)(2,1)S(1)} custom-call(f32[1,768]{1,0:T(1,128)S(1)} %get-tuple-element.51.bias_ref, bf16[8,256,256]{2,1,0:T(8,128)(2,1)} %all-to-all-done.1.mine_ref, bf16[8,128,256]{2,1,0:T(8,128)(2,1)S(1)} %all-to-all-done.rows_ref, bf16[6,8,16,256]{3,2,1,0:T(8,128)(2,1)S(1)} %merge.1.cache_ref), custom_call_target="tpu_custom_call" | custom-call | flops 1500000000 | bytes 1 | tf_op jit(solution)/shard_map/attend1/pallas_call | solution.py:318
  73.9 2.8 %collective-permute-start.15 = (bf16[256,1024]{1,0:T(8,128)(2,1)S(1)}, bf16[256,1024]{1,0:T(8,128)(2,1)S(1)}, u32[]{:S(2)}, u32[]{:S(2)}) collective-permute-start(bf16[256,1024]{1,0:T(8,128)(2,1)S(1)} %attend1.1.own_ref), channel_id=1, source_target_pairs={{0,3},{1,0},{2,1},{3,2},{4,7},{5,4},{6,5},{7,6},{8,11},{9,8},{10,9... | collective-permute-start | bytes 1572872 | tf_op jit(solution)/shard_map/ppermute | solution.py:367
  76.7 2.7 %collective-permute-done.8.down_ref = bf16[256,1024]{1,0:T(8,128)(2,1)S(1)} collective-permute-done((bf16[256,1024]{1,0:T(8,128)(2,1)S(1)}, bf16[256,1024]{1,0:T(8,128)(2,1)S(1)}, u32[]{:S(2)}, u32[]{:S(2)}) %collective-permute-start.8) | collective-permute-done | bytes 524320 | tf_op jit(solution)/shard_map/ppermute | solution.py:367
  79.4 3.1 %collective-permute-done.7.up_ref = bf16[256,1024]{1,0:T(8,128)(2,1)S(1)} collective-permute-done((bf16[256,1024]{1,0:T(8,128)(2,1)S(1)}, bf16[256,1024]{1,0:T(8,128)(2,1)S(1)}, u32[]{:S(2)}, u32[]{:S(2)}) %collective-permute-start.7) | collective-permute-done | bytes 524320 | tf_op jit(solution)/shard_map/ppermute | solution.py:364
  82.5 2.1 %collective-permute-start.12 = (bf16[4,256,640]{2,1,0:T(8,128)(2,1)}, bf16[4,256,640]{2,1,0:T(8,128)(2,1)S(1)}, u32[]{:S(2)}, u32[]{:S(2)}) collective-permute-start(bf16[4,256,640]{2,1,0:T(8,128)(2,1)} %collective-permute-done.11), channel_id=1, source_target_pairs={{0,8},{8,0},{16,24},{24,16},{32,40},{40,32},{48,56},{56,48},{64,72... | collective-permute-start | bytes 3932168 | tf_op jit(solution)/shard_map/ppermute | solution.py:375
  84.8 2.4 %collective-permute-done.13 = bf16[4,256,640]{2,1,0:T(8,128)(2,1)} collective-permute-done((bf16[4,256,640]{2,1,0:T(8,128)(2,1)}, bf16[4,256,640]{2,1,0:T(8,128)(2,1)}, u32[]{:S(2)}, u32[]{:S(2)}) %collective-permute-start.13) | collective-permute-done | bytes 1310752 | tf_op jit(solution)/shard_map/ppermute | solution.py:361
  87.2 1.0 collective-permute-start.9
  88.1 2.5 %collective-permute-done.15.down_ref = bf16[256,1024]{1,0:T(8,128)(2,1)S(1)} collective-permute-done((bf16[256,1024]{1,0:T(8,128)(2,1)S(1)}, bf16[256,1024]{1,0:T(8,128)(2,1)S(1)}, u32[]{:S(2)}, u32[]{:S(2)}) %collective-permute-start.15) | collective-permute-done | bytes 524320 | tf_op jit(solution)/shard_map/ppermute | solution.py:367
  90.7 3.1 %collective-permute-done.14.up_ref = bf16[256,1024]{1,0:T(8,128)(2,1)S(1)} collective-permute-done((bf16[256,1024]{1,0:T(8,128)(2,1)S(1)}, bf16[256,1024]{1,0:T(8,128)(2,1)S(1)}, u32[]{:S(2)}, u32[]{:S(2)}) %collective-permute-start.14) | collective-permute-done | bytes 524320 | tf_op jit(solution)/shard_map/ppermute | solution.py:364
  93.7 2.5 %collective-permute-done.10.high_ref = bf16[128,1024]{1,0:T(8,128)(2,1)S(1)} collective-permute-done((bf16[128,1024]{1,0:T(8,128)(2,1)S(1)}, bf16[128,1024]{1,0:T(8,128)(2,1)S(1)}, u32[]{:S(2)}, u32[]{:S(2)}) %collective-permute-start.10) | collective-permute-done | bytes 262176 | tf_op jit(solution)/shard_map/ppermute | solution.py:367
  96.3 3.1 %collective-permute-done.9.low_ref = bf16[128,1024]{1,0:T(8,128)(2,1)S(1)} collective-permute-done((bf16[128,1024]{1,0:T(8,128)(2,1)S(1)}, bf16[128,1024]{1,0:T(8,128)(2,1)S(1)}, u32[]{:S(2)}, u32[]{:S(2)}) %collective-permute-start.9) | collective-permute-done | bytes 262176 | tf_op jit(solution)/shard_map/ppermute | solution.py:364
  99.4 1.3 collective-permute-start.16
  100.8 1.5 %collective-permute-start.18 = (bf16[128,1024]{1,0:T(8,128)(2,1)S(1)}, bf16[128,1024]{1,0:T(8,128)(2,1)S(1)}, u32[]{:S(2)}, u32[]{:S(2)}) collective-permute-start(bf16[128,1024]{1,0:T(8,128)(2,1)S(1)} %slice.18), channel_id=1, source_target_pairs={{0,1},{1,2},{2,3},{3,0},{4,5},{5,6},{6,7},{7,4},{8,9},{9,10},{10,1... | collective-permute-start | bytes 786440 | tf_op jit(solution)/shard_map/ppermute | solution.py:364
  102.2 0.8 join.2
  103.0 1.9 %fusion.13 = f32[256,640]{1,0:T(8,128)S(1)} fusion(bf16[256,1024]{1,0:T(8,128)(2,1)S(1)} %get-tuple-element.80, bf16[1024,640]{1,0:T(8,128)(2,1)} %bitcast.12), kind=kOutput, calls=%fused_computation.21 | convolution fusion | flops 335544320 | bytes 2490368 | tf_op jit(solution)/shard_map/dot_general | solution.py:336
  106.1 2.1 %fusion.9 = bf16[256,640]{1,0:T(8,128)(2,1)S(1)} fusion(f32[256,640]{1,0:T(8,128)S(1)} %fusion.14, f32[256,640]{1,0:T(8,128)S(1)} %fusion.13, f32[256,640]{1,0:T(8,128)S(1)} %fusion.12, bf16[256,1024]{1,0:T(8,128)(2,1)S(1)} %get-tuple-element.78, bf16[1024,640]{1,0:T(8,128)(2,1)} %bitcast.10), kind=kOutput, calls=%fused_computation.15 | convolution fusion | flops 336199680 | bytes 4128768 | tf_op jit(solution)/shard_map/dot_general | solution.py:336
  109.2 0.6 convolution_add_fusion.4
  110.4 0.7 copy-done.1
  111.7 0.8 join.3
  113.1 1.9 %fusion.17 = f32[256,640]{1,0:T(8,128)S(1)} fusion(bf16[256,1024]{1,0:T(8,128)(2,1)S(1)} %get-tuple-element.91, bf16[1024,640]{1,0:T(8,128)(2,1)} %bitcast.12), kind=kOutput, calls=%fused_computation.25 | convolution fusion | flops 335544320 | bytes 2490368 | tf_op jit(solution)/shard_map/dot_general | solution.py:336
  115.6 1.9 %fusion.8 = bf16[256,640]{1,0:T(8,128)(2,1)S(1)} fusion(f32[256,640]{1,0:T(8,128)S(1)} %fusion.18, f32[256,640]{1,0:T(8,128)S(1)} %fusion.17, f32[256,640]{1,0:T(8,128)S(1)} %fusion.16, bf16[256,1024]{1,0:T(8,128)(2,1)S(1)} %get-tuple-element.89, bf16[1024,640]{1,0:T(8,128)(2,1)} %bitcast.10), kind=kOutput, calls=%fused_computation.14 | convolution fusion | flops 336199680 | bytes 4128768 | tf_op jit(solution)/shard_map/dot_general | solution.py:336
  117.6 1.2 collective-permute-start.20
  120.7 5.4 %collective-permute-done.20 = bf16[256,640]{1,0:T(8,128)(2,1)S(1)} collective-permute-done((bf16[256,640]{1,0:T(8,128)(2,1)S(1)}, bf16[256,640]{1,0:T(8,128)(2,1)S(1)}, u32[]{:S(2)}, u32[]{:S(2)}) %collective-permute-start.20) | collective-permute-done | bytes 327712 | tf_op jit(solution)/shard_map/ppermute | solution.py:388
  126.0 0.6 fusion.10
  126.7 0.9 pad_maximum_fusion
  (53 shorter events, 7.3 us)
Async XLA Ops:
  0.0 11.4 %collective-permute-start = (bf16[16,2048]{1,0:T(8,128)(2,1)}, bf16[16,2048]{1,0:T(8,128)(2,1)S(1)}, u32[]{:S(2)}, u32[]{:S(2)}) collective-permute-start(bf16[16,2048]{1,0:T(8,128)(2,1)} %cache_hbm.1), channel_id=1, source_target_pairs={{0,16},{8,24},{16,32},{24,40},{32,48},{40,56},{48,0},{56,8},{64,80... | collective-permute-start | bytes 196616 | tf_op jit(solution)/shard_map/ppermute | solution.py:347
  3.8 11.7 %collective-permute-start.1 = (bf16[16,2048]{1,0:T(8,128)(2,1)}, bf16[16,2048]{1,0:T(8,128)(2,1)S(1)}, u32[]{:S(2)}, u32[]{:S(2)}) collective-permute-start(bf16[16,2048]{1,0:T(8,128)(2,1)} %cache_hbm.1), channel_id=1, source_target_pairs={{0,32},{8,40},{16,48},{24,56},{32,0},{40,8},{48,16},{56,24},{64,96... | collective-permute-start | bytes 196616 | tf_op jit(solution)/shard_map/ppermute | solution.py:347
  8.9 7.9 %collective-permute-start.2 = (bf16[16,2048]{1,0:T(8,128)(2,1)}, bf16[16,2048]{1,0:T(8,128)(2,1)S(1)}, u32[]{:S(2)}, u32[]{:S(2)}) collective-permute-start(bf16[16,2048]{1,0:T(8,128)(2,1)} %cache_hbm.1), channel_id=1, source_target_pairs={{0,48},{8,56},{16,0},{24,8},{32,16},{40,24},{48,32},{56,40},{64,11... | collective-permute-start | bytes 196616 | tf_op jit(solution)/shard_map/ppermute | solution.py:347
  11.4 5.4 %copy-start.5 = (bf16[1,64,2048]{2,1,0:T(8,128)(2,1)S(1)}, bf16[1,64,2048]{2,1,0:T(8,128)(2,1)}, u32[]{:S(2)}) copy-start(bf16[1,64,2048]{2,1,0:T(8,128)(2,1)} %kv_hbm.1) | copy-start | bytes 786436
  11.4 5.4 %copy-start.6 = (bf16[16,2048]{1,0:T(8,128)(2,1)S(1)}, bf16[16,2048]{1,0:T(8,128)(2,1)}, u32[]{:S(2)}) copy-start(bf16[16,2048]{1,0:T(8,128)(2,1)} %cache_hbm.1) | copy-start | bytes 196612
  17.8 12.0 %all-to-all-start = ((bf16[8,128,256]{2,1,0:T(8,128)(2,1)}), bf16[8,128,256]{2,1,0:T(8,128)(2,1)S(1)}, u32[]{:S(2)}, u32[]{:S(2)}) async-start(bf16[8,128,256]{2,1,0:T(8,128)(2,1)} %pack_rows.1), calls=%async_computation | async-start | bytes 1048576 | tf_op jit(solution)/shard_map/all_to_all | solution.py:349
  22.0 4.1 %copy-start.4 = (bf16[1,64,8192]{2,1,0:T(8,128)(2,1)S(1)}, bf16[1,64,8192]{2,1,0:T(8,128)(2,1)}, u32[]{:S(2)}) copy-start(bf16[1,64,8192]{2,1,0:T(8,128)(2,1)} %param.7) | copy-start | bytes 3145732
  22.0 4.1 %copy-start.7 = (s32[48]{0:T(128)S(1)}, s32[48]{0:T(128)}, u32[]{:S(2)}) copy-start(s32[48]{0:T(128)} %parent_ref.5) | copy-start | bytes 580
  22.0 4.1 %copy-start.9 = (s32[16]{0:T(128)S(1)}, s32[16]{0:T(128)}, u32[]{:S(2)}) copy-start(s32[16]{0:T(128)} %lengths_ref.1) | copy-start | bytes 196
  29.9 30.9 %all-to-all-start.1 = ((bf16[8,256,256]{2,1,0:T(8,128)(2,1)}), bf16[8,256,256]{2,1,0:T(8,128)(2,1)}, u32[]{:S(2)}, u32[]{:S(2)}) async-start(bf16[8,256,256]{2,1,0:T(8,128)(2,1)} %get-tuple-element.57), calls=%async_computation.1 | async-start | bytes 2097152 | tf_op jit(solution)/shard_map/all_to_all | solution.py:354
  35.0 17.9 %copy-start.8 = (s32[16]{0:T(128)S(1)}, s32[16]{0:T(128)}, u32[]{:S(2)}) copy-start(s32[16]{0:T(128)} %owner_ref.3) | copy-start | bytes 196
  35.1 15.0 %collective-permute-start.5 = (bf16[8,64,256]{2,1,0:T(8,128)(2,1)S(1)}, bf16[8,64,256]{2,1,0:T(8,128)(2,1)S(1)}, u32[]{:S(2)}, u32[]{:S(2)}) collective-permute-start(bf16[8,64,256]{2,1,0:T(8,128)(2,1)S(1)} %slice.20.refs_0_), channel_id=1, source_target_pairs={{0,192},{8,200},{16,208},{24,216},{32,224},{40,232},{48,240},{56,2... | collective-permute-start | bytes 786440 | tf_op jit(solution)/shard_map/ppermute | solution.py:353
  37.6 12.4 %collective-permute-start.4 = (bf16[8,64,256]{2,1,0:T(8,128)(2,1)S(1)}, bf16[8,64,256]{2,1,0:T(8,128)(2,1)S(1)}, u32[]{:S(2)}, u32[]{:S(2)}) collective-permute-start(bf16[8,64,256]{2,1,0:T(8,128)(2,1)S(1)} %slice.20.refs_0_), channel_id=1, source_target_pairs={{0,128},{8,136},{16,144},{24,152},{32,160},{40,168},{48,176},{56,1... | collective-permute-start | bytes 786440 | tf_op jit(solution)/shard_map/ppermute | solution.py:353
  38.1 14.8 %collective-permute-start.3 = (bf16[8,64,256]{2,1,0:T(8,128)(2,1)S(1)}, bf16[8,64,256]{2,1,0:T(8,128)(2,1)S(1)}, u32[]{:S(2)}, u32[]{:S(2)}) collective-permute-start(bf16[8,64,256]{2,1,0:T(8,128)(2,1)S(1)} %slice.20.refs_0_), channel_id=1, source_target_pairs={{0,64},{8,72},{16,80},{24,88},{32,96},{40,104},{48,112},{56,120},{... | collective-permute-start | bytes 786440 | tf_op jit(solution)/shard_map/ppermute | solution.py:353
  47.9 1.1 copy-start
  48.9 1.1 copy-start.2
  54.3 22.4 %collective-permute-start.11 = (bf16[4,256,640]{2,1,0:T(8,128)(2,1)}, bf16[4,256,640]{2,1,0:T(8,128)(2,1)}, u32[]{:S(2)}, u32[]{:S(2)}) collective-permute-start(bf16[4,256,640]{2,1,0:T(8,128)(2,1)} %order.4), channel_id=1, source_target_pairs={{0,4},{8,60},{1,5},{9,61},{2,6},{10,62},{3,7},{11,63},{4,0},{12,24... | collective-permute-start | bytes 3932168 | tf_op jit(solution)/shard_map/ppermute | solution.py:360
  57.6 29.5 %collective-permute-start.13 = (bf16[4,256,640]{2,1,0:T(8,128)(2,1)}, bf16[4,256,640]{2,1,0:T(8,128)(2,1)}, u32[]{:S(2)}, u32[]{:S(2)}) collective-permute-start(bf16[4,256,640]{2,1,0:T(8,128)(2,1)} %order.3), channel_id=1, source_target_pairs={{0,4},{8,60},{1,5},{9,61},{2,6},{10,62},{3,7},{11,63},{4,0},{12,24... | collective-permute-start | bytes 3932168 | tf_op jit(solution)/shard_map/ppermute | solution.py:361
  57.7 1.7 %collective-permute-start.6 = (bf16[6,8,16,256]{3,2,1,0:T(8,128)(2,1)S(1)}, bf16[6,8,16,256]{3,2,1,0:T(8,128)(2,1)S(1)}, u32[]{:S(2)}, u32[]{:S(2)}) collective-permute-start(bf16[6,8,16,256]{3,2,1,0:T(8,128)(2,1)S(1)} %get-tuple-element.66), channel_id=1, source_target_pairs={{0,8},{8,0},{16,24},{24,16},{32,40},{40,32},{48,56},{56,48},{64,72... | collective-permute-start | bytes 1179656 | tf_op jit(solution)/shard_map/ppermute | solution.py:358
  65.6 13.8 %collective-permute-start.8 = (bf16[256,1024]{1,0:T(8,128)(2,1)S(1)}, bf16[256,1024]{1,0:T(8,128)(2,1)S(1)}, u32[]{:S(2)}, u32[]{:S(2)}) collective-permute-start(bf16[256,1024]{1,0:T(8,128)(2,1)S(1)} %attend0.1.own_ref), channel_id=1, source_target_pairs={{0,3},{1,0},{2,1},{3,2},{4,7},{5,4},{6,5},{7,6},{8,11},{9,8},{10,9... | collective-permute-start | bytes 1572872 | tf_op jit(solution)/shard_map/ppermute | solution.py:367
  68.2 14.3 %collective-permute-start.7 = (bf16[256,1024]{1,0:T(8,128)(2,1)S(1)}, bf16[256,1024]{1,0:T(8,128)(2,1)S(1)}, u32[]{:S(2)}, u32[]{:S(2)}) collective-permute-start(bf16[256,1024]{1,0:T(8,128)(2,1)S(1)} %attend0.1.own_ref), channel_id=1, source_target_pairs={{0,1},{1,2},{2,3},{3,0},{4,5},{5,6},{6,7},{7,4},{8,9},{9,10},{10,1... | collective-permute-start | bytes 1572872 | tf_op jit(solution)/shard_map/ppermute | solution.py:364
  73.9 16.7 %collective-permute-start.15 = (bf16[256,1024]{1,0:T(8,128)(2,1)S(1)}, bf16[256,1024]{1,0:T(8,128)(2,1)S(1)}, u32[]{:S(2)}, u32[]{:S(2)}) collective-permute-start(bf16[256,1024]{1,0:T(8,128)(2,1)S(1)} %attend1.1.own_ref), channel_id=1, source_target_pairs={{0,3},{1,0},{2,1},{3,2},{4,7},{5,4},{6,5},{7,6},{8,11},{9,8},{10,9... | collective-permute-start | bytes 1572872 | tf_op jit(solution)/shard_map/ppermute | solution.py:367
  76.7 17.1 %collective-permute-start.14 = (bf16[256,1024]{1,0:T(8,128)(2,1)S(1)}, bf16[256,1024]{1,0:T(8,128)(2,1)S(1)}, u32[]{:S(2)}, u32[]{:S(2)}) collective-permute-start(bf16[256,1024]{1,0:T(8,128)(2,1)S(1)} %attend1.1.own_ref), channel_id=1, source_target_pairs={{0,1},{1,2},{2,3},{3,0},{4,5},{5,6},{6,7},{7,4},{8,9},{9,10},{10,1... | collective-permute-start | bytes 1572872 | tf_op jit(solution)/shard_map/ppermute | solution.py:364
  82.5 22.4 %collective-permute-start.12 = (bf16[4,256,640]{2,1,0:T(8,128)(2,1)}, bf16[4,256,640]{2,1,0:T(8,128)(2,1)S(1)}, u32[]{:S(2)}, u32[]{:S(2)}) collective-permute-start(bf16[4,256,640]{2,1,0:T(8,128)(2,1)} %collective-permute-done.11), channel_id=1, source_target_pairs={{0,8},{8,0},{16,24},{24,16},{32,40},{40,32},{48,56},{56,48},{64,72... | collective-permute-start | bytes 3932168 | tf_op jit(solution)/shard_map/ppermute | solution.py:375
  84.7 11.6 %collective-permute-start.10 = (bf16[128,1024]{1,0:T(8,128)(2,1)S(1)}, bf16[128,1024]{1,0:T(8,128)(2,1)S(1)}, u32[]{:S(2)}, u32[]{:S(2)}) collective-permute-start(bf16[128,1024]{1,0:T(8,128)(2,1)S(1)} %slice.17), channel_id=1, source_target_pairs={{0,3},{1,0},{2,1},{3,2},{4,7},{5,4},{6,5},{7,6},{8,11},{9,8},{10,9... | collective-permute-start | bytes 786440 | tf_op jit(solution)/shard_map/ppermute | solution.py:367
  87.2 12.2 %collective-permute-start.9 = (bf16[128,1024]{1,0:T(8,128)(2,1)S(1)}, bf16[128,1024]{1,0:T(8,128)(2,1)S(1)}, u32[]{:S(2)}, u32[]{:S(2)}) collective-permute-start(bf16[128,1024]{1,0:T(8,128)(2,1)S(1)} %slice.16), channel_id=1, source_target_pairs={{0,1},{1,2},{2,3},{3,0},{4,5},{5,6},{6,7},{7,4},{8,9},{9,10},{10,1... | collective-permute-start | bytes 786440 | tf_op jit(solution)/shard_map/ppermute | solution.py:364
  99.4 6.2 %collective-permute-start.16 = (bf16[4,256,640]{2,1,0:T(8,128)(2,1)}, bf16[4,256,640]{2,1,0:T(8,128)(2,1)S(1)}, u32[]{:S(2)}, u32[]{:S(2)}) collective-permute-start(bf16[4,256,640]{2,1,0:T(8,128)(2,1)} %collective-permute-done.13), channel_id=1, source_target_pairs={{0,8},{8,0},{16,24},{24,16},{32,40},{40,32},{48,56},{56,48},{64,72... | collective-permute-start | bytes 3932168 | tf_op jit(solution)/shard_map/ppermute | solution.py:376
  100.7 11.0 %collective-permute-start.19 = (bf16[128,1024]{1,0:T(8,128)(2,1)S(1)}, bf16[128,1024]{1,0:T(8,128)(2,1)S(1)}, u32[]{:S(2)}, u32[]{:S(2)}) collective-permute-start(bf16[128,1024]{1,0:T(8,128)(2,1)S(1)} %slice.19), channel_id=1, source_target_pairs={{0,3},{1,0},{2,1},{3,2},{4,7},{5,4},{6,5},{7,6},{8,11},{9,8},{10,9... | collective-permute-start | bytes 786440 | tf_op jit(solution)/shard_map/ppermute | solution.py:367
  100.8 11.0 %collective-permute-start.18 = (bf16[128,1024]{1,0:T(8,128)(2,1)S(1)}, bf16[128,1024]{1,0:T(8,128)(2,1)S(1)}, u32[]{:S(2)}, u32[]{:S(2)}) collective-permute-start(bf16[128,1024]{1,0:T(8,128)(2,1)S(1)} %slice.18), channel_id=1, source_target_pairs={{0,1},{1,2},{2,3},{3,0},{4,5},{5,6},{6,7},{7,4},{8,9},{9,10},{10,1... | collective-permute-start | bytes 786440 | tf_op jit(solution)/shard_map/ppermute | solution.py:364
  106.1 2.5 %copy-start.3 = (bf16[4,256,640]{2,1,0:T(8,128)(2,1)S(1)}, bf16[4,256,640]{2,1,0:T(8,128)(2,1)}, u32[]{:S(2)}) copy-start(bf16[4,256,640]{2,1,0:T(8,128)(2,1)} %copy-done.2) | copy-start | bytes 3932164
  108.2 10.6 %collective-permute-start.17 = (bf16[256,640]{1,0:T(8,128)(2,1)S(1)}, bf16[256,640]{1,0:T(8,128)(2,1)S(1)}, u32[]{:S(2)}, u32[]{:S(2)}) collective-permute-start(bf16[256,640]{1,0:T(8,128)(2,1)S(1)} %fusion.9), channel_id=1, source_target_pairs={{0,4},{1,5},{2,6},{3,7},{4,0},{5,1},{6,2},{7,3},{8,12},{9,13},{10,... | collective-permute-start | bytes 983048 | tf_op jit(solution)/shard_map/ppermute | solution.py:383
  109.8 1.3 %copy-start.1 = (bf16[4,256,640]{2,1,0:T(8,128)(2,1)S(1)}, bf16[4,256,640]{2,1,0:T(8,128)(2,1)}, u32[]{:S(2)}) copy-start(bf16[4,256,640]{2,1,0:T(8,128)(2,1)} %copy-done) | copy-start | bytes 3932164
  117.6 8.5 %collective-permute-start.20 = (bf16[256,640]{1,0:T(8,128)(2,1)S(1)}, bf16[256,640]{1,0:T(8,128)(2,1)S(1)}, u32[]{:S(2)}, u32[]{:S(2)}) collective-permute-start(bf16[256,640]{1,0:T(8,128)(2,1)S(1)} %fusion.8), channel_id=1, source_target_pairs={{0,4},{1,5},{2,6},{3,7},{4,0},{5,1},{6,2},{7,3},{8,12},{9,13},{10,... | collective-permute-start | bytes 983048 | tf_op jit(solution)/shard_map/ppermute | solution.py:388

commit v3 on v2

--- a/solution.py
+++ b/solution.py
@@ -58,8 +58,8 @@
 SMALL = pl.CostEstimate(flops=1, bytes_accessed=1, transcendentals=0)
 
 
-def params():
-    return pltpu.CompilerParams(vmem_limit_bytes=VMEM_LIMIT)
+def params(limit=VMEM_LIMIT):
+    return pltpu.CompilerParams(vmem_limit_bytes=limit)
 
 
 def whole():
@@ -199,7 +199,7 @@
         out_shape=[jax.ShapeDtypeStruct((4 * TOK, 1024), jnp.bfloat16)] * 4,
         in_specs=[scalars()] + [whole()] * 5,
         out_specs=[whole()] * 4,
-        compiler_params=params(),
+        compiler_params=params(VMEM_LIMIT // 3),
         cost_estimate=SMALL,
         name="join",
     )(ids, *parts)
@@ -320,7 +320,7 @@
         out_shape=jax.ShapeDtypeStruct((4 * TOK, GROUP * HD), jnp.bfloat16),
         in_specs=[whole()] * 4,
         out_specs=whole(),
-        compiler_params=params(),
+        compiler_params=params(VMEM_LIMIT * 2 // 3),
         cost_estimate=pl.CostEstimate(flops=1_500_000_000, bytes_accessed=1, transcendentals=2_500_000),
         name=f"attend{chunk}",
     )(bias, mine, rows, cache_rows)
@@ -379,12 +379,12 @@
 
     rows_low = join(ids, low, low_up, low_down, *low_far)
     other_low = project(rows_low, near).astype(jnp.bfloat16)
-    mine_low = project(after(rows_low, other_low), matrix)
+    rows_high = join(after(ids, other_low), high, high_up, high_down, *high_far)
+    other_high = project(rows_high, near).astype(jnp.bfloat16)
     other_low = lax.ppermute(other_low, "seq", Z_SWAP)
+    mine_low = project(after(rows_low, other_high, other_low), matrix)
     result_low = mine_low + other_low.astype(jnp.float32)
-    rows_high = join(after(ids, mine_low), high, high_up, high_down, *high_far)
-    other_high = project(rows_high, near).astype(jnp.bfloat16)
-    mine_high = project(after(rows_high, other_high, other_low), matrix)
+    mine_high = project(after(rows_high, mine_low), matrix)
     result_high = mine_high + lax.ppermute(other_high, "seq", Z_SWAP).astype(jnp.float32)
     return jnp.concatenate([result_low, result_high], axis=0).astype(jnp.bfloat16)[None]
 

time: 128 us -> 126 us (0.984)
  waiting for transfers between devices: 33 us -> 31.7 us
    ppermute x1, waiting for transfers between devices: 5.38 us -> 2.22 us  [per_device(): lax.ppermute(other_high, 'seq', Z_SWAP).astype(jnp.float32)]
    ppermute x4, waiting for transfers between devices: 9.28 us -> 10.8 us  [up(): return lax.ppermute(part, 'seq', y_shift(1))]
  transfers between devices with their start and end apart: 23 -> 23, of which waited for: 12 -> 15; matrix products, arithmetic and copies ran while one was open for 11% -> 12% of each run, Pallas kernels for 26% -> 27%
where the time goes in v3:
time: 126 us
  starting transfers between devices  40 us (32%)
  Pallas kernels  34.6 us (27%)
  waiting for transfers between devices  31.7 us (25%)
  matrix products  14.9 us (12%)
  local copies, waits for them, and re-layouts  3.08 us (2%)
    pallas_call x3, Pallas kernels, order(): pl.pallas_call(functools.partial(order_body, count), out_shape=[jax.Shape...  17.2 us
    dot_general x16, matrix products, project(): jnp.dot(rows, matrix.reshape(rows.shape[1], -1), preferred_element_type=j...  14.9 us
    ppermute x3, starting transfers between devices, per_device(): slots = [lax.ppermute(cache, 'leaf', z_shift(k)) for k in (1, 2, 3)]  11.3 us
    ppermute x4, waiting for transfers between devices, up(): return lax.ppermute(part, 'seq', y_shift(1))  10.8 us
    pallas_call x2, Pallas kernels, attend(): pl.pallas_call(functools.partial(attend_body, chunk), out_shape=jax.Shape...  10.6 us
    ppermute x4, waiting for transfers between devices, down(): return lax.ppermute(part, 'seq', y_shift(-1))  7.94 us
    ppermute x4, starting transfers between devices, down(): return lax.ppermute(part, 'seq', y_shift(-1))  5.56 us
    all_to_all x1, starting transfers between devices, per_device(): mine = lax.all_to_all(after(packed, rows), 'seq', 0, 0)  5.19 us
  transfers between devices with their start and end apart: 23, of which 15 were waited for; matrix products, arithmetic and copies ran while one was open for 12% of the time, Pallas kernels for 27%

profile of v3, /device:TPU:1, one launch (start us, length us, event | category | flops | bytes accessed | tf_op | source)
XLA Modules:
  0.0 125.7 jit_solution(17637305559578250063)
XLA Ops:
  0.0 3.8 %collective-permute-start = (bf16[16,2048]{1,0:T(8,128)(2,1)}, bf16[16,2048]{1,0:T(8,128)(2,1)S(1)}, u32[]{:S(2)}, u32[]{:S(2)}) collective-permute-start(bf16[16,2048]{1,0:T(8,128)(2,1)} %cache_hbm.1), channel_id=1, source_target_pairs={{0,16},{8,24},{16,32},{24,40},{32,48},{40,56},{48,0},{56,8},{64,80... | collective-permute-start | bytes 196616 | tf_op jit(solution)/shard_map/ppermute | solution.py:347
  3.8 5.1 %collective-permute-start.1 = (bf16[16,2048]{1,0:T(8,128)(2,1)}, bf16[16,2048]{1,0:T(8,128)(2,1)S(1)}, u32[]{:S(2)}, u32[]{:S(2)}) collective-permute-start(bf16[16,2048]{1,0:T(8,128)(2,1)} %cache_hbm.1), channel_id=1, source_target_pairs={{0,32},{8,40},{16,48},{24,56},{32,0},{40,8},{48,16},{56,24},{64,96... | collective-permute-start | bytes 196616 | tf_op jit(solution)/shard_map/ppermute | solution.py:347
  8.9 2.4 %collective-permute-start.2 = (bf16[16,2048]{1,0:T(8,128)(2,1)}, bf16[16,2048]{1,0:T(8,128)(2,1)S(1)}, u32[]{:S(2)}, u32[]{:S(2)}) collective-permute-start(bf16[16,2048]{1,0:T(8,128)(2,1)} %cache_hbm.1), channel_id=1, source_target_pairs={{0,48},{8,56},{16,0},{24,8},{32,16},{40,24},{48,32},{56,40},{64,11... | collective-permute-start | bytes 196616 | tf_op jit(solution)/shard_map/ppermute | solution.py:347
  11.4 4.1 %order.4 = bf16[4,256,640]{2,1,0:T(8,128)(2,1)} custom-call(s32[9]{0:T(128)S(1)} %stack.36.ids_ref, bf16[8,4,256,640]{3,2,1,0:T(8,128)(2,1)} %bitcast.63), custom_call_target="tpu_custom_call" | custom-call | flops 1 | bytes 1 | tf_op jit(solution)/shard_map/order/pallas_call | solution.py:170
  15.5 1.3 %collective-permute-done.2.refs_2_ = bf16[16,2048]{1,0:T(8,128)(2,1)S(1)} collective-permute-done((bf16[16,2048]{1,0:T(8,128)(2,1)}, bf16[16,2048]{1,0:T(8,128)(2,1)S(1)}, u32[]{:S(2)}, u32[]{:S(2)}) %collective-permute-start.2) | collective-permute-done | bytes 65568 | tf_op jit(solution)/shard_map/ppermute | solution.py:347
  16.8 1.0 pack_rows.1
  17.8 4.2 %all-to-all-start = ((bf16[8,128,256]{2,1,0:T(8,128)(2,1)}), bf16[8,128,256]{2,1,0:T(8,128)(2,1)S(1)}, u32[]{:S(2)}, u32[]{:S(2)}) async-start(bf16[8,128,256]{2,1,0:T(8,128)(2,1)} %pack_rows.1), calls=%async_computation | async-start | bytes 1048576 | tf_op jit(solution)/shard_map/all_to_all | solution.py:349
  22.0 4.1 %order.3 = bf16[4,256,640]{2,1,0:T(8,128)(2,1)} custom-call(s32[9]{0:T(128)S(1)} %stack.36.ids_ref, bf16[8,4,256,640]{3,2,1,0:T(8,128)(2,1)} %bitcast.64), custom_call_target="tpu_custom_call" | custom-call | flops 1 | bytes 1 | tf_op jit(solution)/shard_map/order/pallas_call | solution.py:170
  26.1 1.6 %pack_queries.1 = (bf16[8,256,256]{2,1,0:T(8,128)(2,1)}, f32[1,768]{1,0:T(1,128)S(1)}) custom-call(s32[9]{0:T(128)S(1)} %stack.36.ids_ref, s32[48]{0:T(128)S(1)} %copy-done.7, s32[16]{0:T(128)S(1)} %copy-done.9, bf16[64,8192]{1,0:T(8,128)(2,1)S(1)} %bitcast.62), custom_call_target="tpu_custom_call" | custom-call | flops 1 | bytes 1 | tf_op jit(solution)/shard_map/pack_queries/pallas_call | solution.py:133
  27.7 2.1 %all-to-all-done.rows_ref = bf16[8,128,256]{2,1,0:T(8,128)(2,1)S(1)} async-done(((bf16[8,128,256]{2,1,0:T(8,128)(2,1)}), bf16[8,128,256]{2,1,0:T(8,128)(2,1)S(1)}, u32[]{:S(2)}, u32[]{:S(2)}) %all-to-all-start) | async-done | bytes 524320 | tf_op jit(solution)/shard_map/all_to_all | solution.py:349
  29.8 5.2 %all-to-all-start.1 = ((bf16[8,256,256]{2,1,0:T(8,128)(2,1)}), bf16[8,256,256]{2,1,0:T(8,128)(2,1)}, u32[]{:S(2)}, u32[]{:S(2)}) async-start(bf16[8,256,256]{2,1,0:T(8,128)(2,1)} %get-tuple-element.57), calls=%async_computation.1 | async-start | bytes 2097152 | tf_op jit(solution)/shard_map/all_to_all | solution.py:354
  35.1 2.6 %collective-permute-start.5 = (bf16[8,64,256]{2,1,0:T(8,128)(2,1)S(1)}, bf16[8,64,256]{2,1,0:T(8,128)(2,1)S(1)}, u32[]{:S(2)}, u32[]{:S(2)}) collective-permute-start(bf16[8,64,256]{2,1,0:T(8,128)(2,1)S(1)} %slice.20.refs_0_), channel_id=1, source_target_pairs={{0,192},{8,200},{16,208},{24,216},{32,224},{40,232},{48,240},{56,2... | collective-permute-start | bytes 786440 | tf_op jit(solution)/shard_map/ppermute | solution.py:353
  38.1 0.6 collective-permute-start.3
  38.7 9.1 %order.5 = (bf16[4,256,640]{2,1,0:T(8,128)(2,1)S(1)}, bf16[4,256,640]{2,1,0:T(8,128)(2,1)S(1)}, bf16[4,256,640]{2,1,0:T(8,128)(2,1)S(1)}, bf16[4,256,640]{2,1,0:T(8,128)(2,1)S(1)}) custom-call(s32[9]{0:T(128)S(1)} %stack.36.ids_ref, bf16[8,4,256,640]{3,2,1,0:T(8,128)(2,1)} %bitcast.65), custom_call_target="tpu_custom_call" | custom-call | flops 1 | bytes 1 | tf_op jit(solution)/shard_map/order/pallas_call | solution.py:170
  47.9 1.1 copy-done
  48.9 1.1 copy-done.2
  50.0 2.9 %collective-permute-done.3.refs_1_ = bf16[8,64,256]{2,1,0:T(8,128)(2,1)S(1)} collective-permute-done((bf16[8,64,256]{2,1,0:T(8,128)(2,1)S(1)}, bf16[8,64,256]{2,1,0:T(8,128)(2,1)S(1)}, u32[]{:S(2)}, u32[]{:S(2)}) %collective-permute-start.3) | collective-permute-done | bytes 262176 | tf_op jit(solution)/shard_map/ppermute | solution.py:353
  53.0 1.4 %pick.1 = (bf16[6,8,16,256]{3,2,1,0:T(8,128)(2,1)S(1)}, bf16[6,8,16,256]{3,2,1,0:T(8,128)(2,1)S(1)}) custom-call(s32[9]{0:T(128)S(1)} %stack.36.ids_ref, s32[48]{0:T(128)S(1)} %copy-done.7, s32[16]{0:T(128)S(1)} %copy-done.8, bf16[8,64,256]{2,1,0:T(8,128)(2,1)S(1)} %slice.20.refs_0_, bf16[8,64,256]{2,1,0:T(8,128)(2,1)S(1)} %collective-permute-done.3.refs_1_, ...), custom_call_target="tpu_custom_call" | custom-call | flops 1 | bytes 1 | tf_op jit(solution)/shard_map/pick/pallas_call | solution.py:230
  54.3 3.3 %collective-permute-start.11 = (bf16[4,256,640]{2,1,0:T(8,128)(2,1)}, bf16[4,256,640]{2,1,0:T(8,128)(2,1)}, u32[]{:S(2)}, u32[]{:S(2)}) collective-permute-start(bf16[4,256,640]{2,1,0:T(8,128)(2,1)} %order.4), channel_id=1, source_target_pairs={{0,4},{8,60},{1,5},{9,61},{2,6},{10,62},{3,7},{11,63},{4,0},{12,24... | collective-permute-start | bytes 3932168 | tf_op jit(solution)/shard_map/ppermute | solution.py:360
  57.7 1.7 %collective-permute-done.6.received_ref = bf16[6,8,16,256]{3,2,1,0:T(8,128)(2,1)S(1)} collective-permute-done((bf16[6,8,16,256]{3,2,1,0:T(8,128)(2,1)S(1)}, bf16[6,8,16,256]{3,2,1,0:T(8,128)(2,1)S(1)}, u32[]{:S(2)}, u32[]{:S(2)}) %collective-permute-start.6) | collective-permute-done | bytes 393248 | tf_op jit(solution)/shard_map/ppermute | solution.py:358
  59.4 1.3 %merge.1.cache_ref = bf16[6,8,16,256]{3,2,1,0:T(8,128)(2,1)S(1)} custom-call(s32[9]{0:T(128)S(1)} %stack.36.ids_ref, s32[48]{0:T(128)S(1)} %copy-done.7, s32[16]{0:T(128)S(1)} %copy-done.8, bf16[6,8,16,256]{3,2,1,0:T(8,128)(2,1)S(1)} %get-tuple-element.65.own_ref, bf16[6,8,16,256]{3,2,1,0:T(8,128)(2,1)S(1)} %collective-permute-done.6.received_ref), custom_call_target="tpu_custom_call" | custom-call | flops 1 | bytes 1 | tf_op jit(solution)/shard_map/merge/pallas_call | solution.py:258
  60.7 4.9 %attend0.1.own_ref = bf16[256,1024]{1,0:T(8,128)(2,1)S(1)} custom-call(f32[1,768]{1,0:T(1,128)S(1)} %get-tuple-element.51.bias_ref, bf16[8,256,256]{2,1,0:T(8,128)(2,1)} %all-to-all-done.1.mine_ref, bf16[8,128,256]{2,1,0:T(8,128)(2,1)S(1)} %all-to-all-done.rows_ref, bf16[6,8,16,256]{3,2,1,0:T(8,128)(2,1)S(1)} %merge.1.cache_ref), custom_call_target="tpu_custom_call" | custom-call | flops 1500000000 | bytes 1 | tf_op jit(solution)/shard_map/attend0/pallas_call | solution.py:318
  65.6 2.6 %collective-permute-start.8 = (bf16[256,1024]{1,0:T(8,128)(2,1)S(1)}, bf16[256,1024]{1,0:T(8,128)(2,1)S(1)}, u32[]{:S(2)}, u32[]{:S(2)}) collective-permute-start(bf16[256,1024]{1,0:T(8,128)(2,1)S(1)} %attend0.1.own_ref), channel_id=1, source_target_pairs={{0,3},{1,0},{2,1},{3,2},{4,7},{5,4},{6,5},{7,6},{8,11},{9,8},{10,9... | collective-permute-start | bytes 1572872 | tf_op jit(solution)/shard_map/ppermute | solution.py:367
  68.2 5.7 %attend1.1.own_ref = bf16[256,1024]{1,0:T(8,128)(2,1)S(1)} custom-call(f32[1,768]{1,0:T(1,128)S(1)} %get-tuple-element.51.bias_ref, bf16[8,256,256]{2,1,0:T(8,128)(2,1)} %all-to-all-done.1.mine_ref, bf16[8,128,256]{2,1,0:T(8,128)(2,1)S(1)} %all-to-all-done.rows_ref, bf16[6,8,16,256]{3,2,1,0:T(8,128)(2,1)S(1)} %merge.1.cache_ref), custom_call_target="tpu_custom_call" | custom-call | flops 1500000000 | bytes 1 | tf_op jit(solution)/shard_map/attend1/pallas_call | solution.py:318
  73.9 2.8 %collective-permute-start.15 = (bf16[256,1024]{1,0:T(8,128)(2,1)S(1)}, bf16[256,1024]{1,0:T(8,128)(2,1)S(1)}, u32[]{:S(2)}, u32[]{:S(2)}) collective-permute-start(bf16[256,1024]{1,0:T(8,128)(2,1)S(1)} %attend1.1.own_ref), channel_id=1, source_target_pairs={{0,3},{1,0},{2,1},{3,2},{4,7},{5,4},{6,5},{7,6},{8,11},{9,8},{10,9... | collective-permute-start | bytes 1572872 | tf_op jit(solution)/shard_map/ppermute | solution.py:367
  76.7 2.7 %collective-permute-done.8.down_ref = bf16[256,1024]{1,0:T(8,128)(2,1)S(1)} collective-permute-done((bf16[256,1024]{1,0:T(8,128)(2,1)S(1)}, bf16[256,1024]{1,0:T(8,128)(2,1)S(1)}, u32[]{:S(2)}, u32[]{:S(2)}) %collective-permute-start.8) | collective-permute-done | bytes 524320 | tf_op jit(solution)/shard_map/ppermute | solution.py:367
  79.4 3.1 %collective-permute-done.7.up_ref = bf16[256,1024]{1,0:T(8,128)(2,1)S(1)} collective-permute-done((bf16[256,1024]{1,0:T(8,128)(2,1)S(1)}, bf16[256,1024]{1,0:T(8,128)(2,1)S(1)}, u32[]{:S(2)}, u32[]{:S(2)}) %collective-permute-start.7) | collective-permute-done | bytes 524320 | tf_op jit(solution)/shard_map/ppermute | solution.py:364
  82.5 2.2 %collective-permute-start.12 = (bf16[4,256,640]{2,1,0:T(8,128)(2,1)}, bf16[4,256,640]{2,1,0:T(8,128)(2,1)S(1)}, u32[]{:S(2)}, u32[]{:S(2)}) collective-permute-start(bf16[4,256,640]{2,1,0:T(8,128)(2,1)} %collective-permute-done.11), channel_id=1, source_target_pairs={{0,8},{8,0},{16,24},{24,16},{32,40},{40,32},{48,56},{56,48},{64,72... | collective-permute-start | bytes 3932168 | tf_op jit(solution)/shard_map/ppermute | solution.py:375
  84.8 2.4 %collective-permute-done.13 = bf16[4,256,640]{2,1,0:T(8,128)(2,1)} collective-permute-done((bf16[4,256,640]{2,1,0:T(8,128)(2,1)}, bf16[4,256,640]{2,1,0:T(8,128)(2,1)}, u32[]{:S(2)}, u32[]{:S(2)}) %collective-permute-start.13) | collective-permute-done | bytes 1310752 | tf_op jit(solution)/shard_map/ppermute | solution.py:361
  87.1 1.0 collective-permute-start.9
  88.1 2.5 %collective-permute-done.15.down_ref = bf16[256,1024]{1,0:T(8,128)(2,1)S(1)} collective-permute-done((bf16[256,1024]{1,0:T(8,128)(2,1)S(1)}, bf16[256,1024]{1,0:T(8,128)(2,1)S(1)}, u32[]{:S(2)}, u32[]{:S(2)}) %collective-permute-start.15) | collective-permute-done | bytes 524320 | tf_op jit(solution)/shard_map/ppermute | solution.py:367
  90.6 3.1 %collective-permute-done.14.up_ref = bf16[256,1024]{1,0:T(8,128)(2,1)S(1)} collective-permute-done((bf16[256,1024]{1,0:T(8,128)(2,1)S(1)}, bf16[256,1024]{1,0:T(8,128)(2,1)S(1)}, u32[]{:S(2)}, u32[]{:S(2)}) %collective-permute-start.14) | collective-permute-done | bytes 524320 | tf_op jit(solution)/shard_map/ppermute | solution.py:364
  93.7 2.5 %collective-permute-done.10.high_ref = bf16[128,1024]{1,0:T(8,128)(2,1)S(1)} collective-permute-done((bf16[128,1024]{1,0:T(8,128)(2,1)S(1)}, bf16[128,1024]{1,0:T(8,128)(2,1)S(1)}, u32[]{:S(2)}, u32[]{:S(2)}) %collective-permute-start.10) | collective-permute-done | bytes 262176 | tf_op jit(solution)/shard_map/ppermute | solution.py:367
  96.2 3.1 %collective-permute-done.9.low_ref = bf16[128,1024]{1,0:T(8,128)(2,1)S(1)} collective-permute-done((bf16[128,1024]{1,0:T(8,128)(2,1)S(1)}, bf16[128,1024]{1,0:T(8,128)(2,1)S(1)}, u32[]{:S(2)}, u32[]{:S(2)}) %collective-permute-start.9) | collective-permute-done | bytes 262176 | tf_op jit(solution)/shard_map/ppermute | solution.py:364
  99.3 1.3 %collective-permute-start.16 = (bf16[4,256,640]{2,1,0:T(8,128)(2,1)}, bf16[4,256,640]{2,1,0:T(8,128)(2,1)S(1)}, u32[]{:S(2)}, u32[]{:S(2)}) collective-permute-start(bf16[4,256,640]{2,1,0:T(8,128)(2,1)} %collective-permute-done.13), channel_id=1, source_target_pairs={{0,8},{8,0},{16,24},{24,16},{32,40},{40,32},{48,56},{56,48},{64,72... | collective-permute-start | bytes 3932168 | tf_op jit(solution)/shard_map/ppermute | solution.py:376
  100.8 1.5 %collective-permute-start.17 = (bf16[128,1024]{1,0:T(8,128)(2,1)S(1)}, bf16[128,1024]{1,0:T(8,128)(2,1)S(1)}, u32[]{:S(2)}, u32[]{:S(2)}) collective-permute-start(bf16[128,1024]{1,0:T(8,128)(2,1)S(1)} %slice.18), channel_id=1, source_target_pairs={{0,1},{1,2},{2,3},{3,0},{4,5},{5,6},{6,7},{7,4},{8,9},{9,10},{10,1... | collective-permute-start | bytes 786440 | tf_op jit(solution)/shard_map/ppermute | solution.py:364
  102.2 0.8 join.2
  103.0 1.9 %fusion.11 = f32[256,640]{1,0:T(8,128)S(1)} fusion(bf16[256,1024]{1,0:T(8,128)(2,1)S(1)} %get-tuple-element.87, bf16[1024,640]{1,0:T(8,128)(2,1)} %bitcast.12), kind=kOutput, calls=%fused_computation.20 | convolution fusion | flops 335544320 | bytes 2490368 | tf_op jit(solution)/shard_map/dot_general | solution.py:336
  106.1 2.0 %fusion.7 = bf16[256,640]{1,0:T(8,128)(2,1)S(1)} fusion(f32[256,640]{1,0:T(8,128)S(1)} %fusion.12, f32[256,640]{1,0:T(8,128)S(1)} %fusion.11, f32[256,640]{1,0:T(8,128)S(1)} %fusion.10, bf16[256,1024]{1,0:T(8,128)(2,1)S(1)} %get-tuple-element.85, bf16[1024,640]{1,0:T(8,128)(2,1)} %bitcast.10), kind=kOutput, calls=%fused_computation.13 | convolution fusion | flops 336199680 | bytes 4128768 | tf_op jit(solution)/shard_map/dot_general | solution.py:336
  108.7 1.5 %collective-permute-done.17.low_ref = bf16[128,1024]{1,0:T(8,128)(2,1)S(1)} collective-permute-done((bf16[128,1024]{1,0:T(8,128)(2,1)S(1)}, bf16[128,1024]{1,0:T(8,128)(2,1)S(1)}, u32[]{:S(2)}, u32[]{:S(2)}) %collective-permute-start.17) | collective-permute-done | bytes 262176 | tf_op jit(solution)/shard_map/ppermute | solution.py:364
  110.2 0.8 join.3
  111.6 1.9 %fusion.14 = f32[256,640]{1,0:T(8,128)S(1)} fusion(bf16[256,1024]{1,0:T(8,128)(2,1)S(1)} %get-tuple-element.91, bf16[1024,640]{1,0:T(8,128)(2,1)} %bitcast.12), kind=kOutput, calls=%fused_computation.23 | convolution fusion | flops 335544320 | bytes 2490368 | tf_op jit(solution)/shard_map/dot_general | solution.py:336
  114.1 2.1 %fusion.6 = bf16[256,640]{1,0:T(8,128)(2,1)S(1)} fusion(f32[256,640]{1,0:T(8,128)S(1)} %fusion.15, f32[256,640]{1,0:T(8,128)S(1)} %fusion.14, f32[256,640]{1,0:T(8,128)S(1)} %fusion.13, bf16[256,1024]{1,0:T(8,128)(2,1)S(1)} %get-tuple-element.89, bf16[1024,640]{1,0:T(8,128)(2,1)} %bitcast.10), kind=kOutput, calls=%fused_computation.12 | convolution fusion | flops 336199680 | bytes 4128768 | tf_op jit(solution)/shard_map/dot_general | solution.py:336
  118.7 0.7 copy-done.3
  119.4 0.6 fusion.5
  121.9 0.6 convolution_add_fusion
  122.5 2.2 %collective-permute-done.20 = bf16[256,640]{1,0:T(8,128)(2,1)S(1)} collective-permute-done((bf16[256,640]{1,0:T(8,128)(2,1)S(1)}, bf16[256,640]{1,0:T(8,128)(2,1)S(1)}, u32[]{:S(2)}, u32[]{:S(2)}) %collective-permute-start.20) | collective-permute-done | bytes 327712 | tf_op jit(solution)/shard_map/ppermute | solution.py:388
  124.8 0.9 pad_maximum_fusion
  (54 shorter events, 8.3 us)
Async XLA Ops:
  0.0 11.4 %collective-permute-start = (bf16[16,2048]{1,0:T(8,128)(2,1)}, bf16[16,2048]{1,0:T(8,128)(2,1)S(1)}, u32[]{:S(2)}, u32[]{:S(2)}) collective-permute-start(bf16[16,2048]{1,0:T(8,128)(2,1)} %cache_hbm.1), channel_id=1, source_target_pairs={{0,16},{8,24},{16,32},{24,40},{32,48},{40,56},{48,0},{56,8},{64,80... | collective-permute-start | bytes 196616 | tf_op jit(solution)/shard_map/ppermute | solution.py:347
  3.8 11.7 %collective-permute-start.1 = (bf16[16,2048]{1,0:T(8,128)(2,1)}, bf16[16,2048]{1,0:T(8,128)(2,1)S(1)}, u32[]{:S(2)}, u32[]{:S(2)}) collective-permute-start(bf16[16,2048]{1,0:T(8,128)(2,1)} %cache_hbm.1), channel_id=1, source_target_pairs={{0,32},{8,40},{16,48},{24,56},{32,0},{40,8},{48,16},{56,24},{64,96... | collective-permute-start | bytes 196616 | tf_op jit(solution)/shard_map/ppermute | solution.py:347
  8.9 7.9 %collective-permute-start.2 = (bf16[16,2048]{1,0:T(8,128)(2,1)}, bf16[16,2048]{1,0:T(8,128)(2,1)S(1)}, u32[]{:S(2)}, u32[]{:S(2)}) collective-permute-start(bf16[16,2048]{1,0:T(8,128)(2,1)} %cache_hbm.1), channel_id=1, source_target_pairs={{0,48},{8,56},{16,0},{24,8},{32,16},{40,24},{48,32},{56,40},{64,11... | collective-permute-start | bytes 196616 | tf_op jit(solution)/shard_map/ppermute | solution.py:347
  11.4 5.4 %copy-start.5 = (bf16[1,64,2048]{2,1,0:T(8,128)(2,1)S(1)}, bf16[1,64,2048]{2,1,0:T(8,128)(2,1)}, u32[]{:S(2)}) copy-start(bf16[1,64,2048]{2,1,0:T(8,128)(2,1)} %kv_hbm.1) | copy-start | bytes 786436
  11.4 5.4 %copy-start.6 = (bf16[16,2048]{1,0:T(8,128)(2,1)S(1)}, bf16[16,2048]{1,0:T(8,128)(2,1)}, u32[]{:S(2)}) copy-start(bf16[16,2048]{1,0:T(8,128)(2,1)} %cache_hbm.1) | copy-start | bytes 196612
  17.8 12.0 %all-to-all-start = ((bf16[8,128,256]{2,1,0:T(8,128)(2,1)}), bf16[8,128,256]{2,1,0:T(8,128)(2,1)S(1)}, u32[]{:S(2)}, u32[]{:S(2)}) async-start(bf16[8,128,256]{2,1,0:T(8,128)(2,1)} %pack_rows.1), calls=%async_computation | async-start | bytes 1048576 | tf_op jit(solution)/shard_map/all_to_all | solution.py:349
  22.0 4.1 %copy-start.4 = (bf16[1,64,8192]{2,1,0:T(8,128)(2,1)S(1)}, bf16[1,64,8192]{2,1,0:T(8,128)(2,1)}, u32[]{:S(2)}) copy-start(bf16[1,64,8192]{2,1,0:T(8,128)(2,1)} %param.7) | copy-start | bytes 3145732
  22.0 4.1 %copy-start.7 = (s32[48]{0:T(128)S(1)}, s32[48]{0:T(128)}, u32[]{:S(2)}) copy-start(s32[48]{0:T(128)} %parent_ref.5) | copy-start | bytes 580
  22.0 4.1 %copy-start.9 = (s32[16]{0:T(128)S(1)}, s32[16]{0:T(128)}, u32[]{:S(2)}) copy-start(s32[16]{0:T(128)} %lengths_ref.1) | copy-start | bytes 196
  29.8 30.9 %all-to-all-start.1 = ((bf16[8,256,256]{2,1,0:T(8,128)(2,1)}), bf16[8,256,256]{2,1,0:T(8,128)(2,1)}, u32[]{:S(2)}, u32[]{:S(2)}) async-start(bf16[8,256,256]{2,1,0:T(8,128)(2,1)} %get-tuple-element.57), calls=%async_computation.1 | async-start | bytes 2097152 | tf_op jit(solution)/shard_map/all_to_all | solution.py:354
  35.0 17.9 %copy-start.8 = (s32[16]{0:T(128)S(1)}, s32[16]{0:T(128)}, u32[]{:S(2)}) copy-start(s32[16]{0:T(128)} %owner_ref.3) | copy-start | bytes 196
  35.1 15.0 %collective-permute-start.5 = (bf16[8,64,256]{2,1,0:T(8,128)(2,1)S(1)}, bf16[8,64,256]{2,1,0:T(8,128)(2,1)S(1)}, u32[]{:S(2)}, u32[]{:S(2)}) collective-permute-start(bf16[8,64,256]{2,1,0:T(8,128)(2,1)S(1)} %slice.20.refs_0_), channel_id=1, source_target_pairs={{0,192},{8,200},{16,208},{24,216},{32,224},{40,232},{48,240},{56,2... | collective-permute-start | bytes 786440 | tf_op jit(solution)/shard_map/ppermute | solution.py:353
  37.6 12.4 %collective-permute-start.4 = (bf16[8,64,256]{2,1,0:T(8,128)(2,1)S(1)}, bf16[8,64,256]{2,1,0:T(8,128)(2,1)S(1)}, u32[]{:S(2)}, u32[]{:S(2)}) collective-permute-start(bf16[8,64,256]{2,1,0:T(8,128)(2,1)S(1)} %slice.20.refs_0_), channel_id=1, source_target_pairs={{0,128},{8,136},{16,144},{24,152},{32,160},{40,168},{48,176},{56,1... | collective-permute-start | bytes 786440 | tf_op jit(solution)/shard_map/ppermute | solution.py:353
  38.1 14.8 %collective-permute-start.3 = (bf16[8,64,256]{2,1,0:T(8,128)(2,1)S(1)}, bf16[8,64,256]{2,1,0:T(8,128)(2,1)S(1)}, u32[]{:S(2)}, u32[]{:S(2)}) collective-permute-start(bf16[8,64,256]{2,1,0:T(8,128)(2,1)S(1)} %slice.20.refs_0_), channel_id=1, source_target_pairs={{0,64},{8,72},{16,80},{24,88},{32,96},{40,104},{48,112},{56,120},{... | collective-permute-start | bytes 786440 | tf_op jit(solution)/shard_map/ppermute | solution.py:353
  47.9 1.1 copy-start
  48.9 1.1 copy-start.2
  54.3 22.3 %collective-permute-start.11 = (bf16[4,256,640]{2,1,0:T(8,128)(2,1)}, bf16[4,256,640]{2,1,0:T(8,128)(2,1)}, u32[]{:S(2)}, u32[]{:S(2)}) collective-permute-start(bf16[4,256,640]{2,1,0:T(8,128)(2,1)} %order.4), channel_id=1, source_target_pairs={{0,4},{8,60},{1,5},{9,61},{2,6},{10,62},{3,7},{11,63},{4,0},{12,24... | collective-permute-start | bytes 3932168 | tf_op jit(solution)/shard_map/ppermute | solution.py:360
  57.6 29.5 %collective-permute-start.13 = (bf16[4,256,640]{2,1,0:T(8,128)(2,1)}, bf16[4,256,640]{2,1,0:T(8,128)(2,1)}, u32[]{:S(2)}, u32[]{:S(2)}) collective-permute-start(bf16[4,256,640]{2,1,0:T(8,128)(2,1)} %order.3), channel_id=1, source_target_pairs={{0,4},{8,60},{1,5},{9,61},{2,6},{10,62},{3,7},{11,63},{4,0},{12,24... | collective-permute-start | bytes 3932168 | tf_op jit(solution)/shard_map/ppermute | solution.py:361
  57.7 1.7 %collective-permute-start.6 = (bf16[6,8,16,256]{3,2,1,0:T(8,128)(2,1)S(1)}, bf16[6,8,16,256]{3,2,1,0:T(8,128)(2,1)S(1)}, u32[]{:S(2)}, u32[]{:S(2)}) collective-permute-start(bf16[6,8,16,256]{3,2,1,0:T(8,128)(2,1)S(1)} %get-tuple-element.66), channel_id=1, source_target_pairs={{0,8},{8,0},{16,24},{24,16},{32,40},{40,32},{48,56},{56,48},{64,72... | collective-permute-start | bytes 1179656 | tf_op jit(solution)/shard_map/ppermute | solution.py:358
  65.6 13.8 %collective-permute-start.8 = (bf16[256,1024]{1,0:T(8,128)(2,1)S(1)}, bf16[256,1024]{1,0:T(8,128)(2,1)S(1)}, u32[]{:S(2)}, u32[]{:S(2)}) collective-permute-start(bf16[256,1024]{1,0:T(8,128)(2,1)S(1)} %attend0.1.own_ref), channel_id=1, source_target_pairs={{0,3},{1,0},{2,1},{3,2},{4,7},{5,4},{6,5},{7,6},{8,11},{9,8},{10,9... | collective-permute-start | bytes 1572872 | tf_op jit(solution)/shard_map/ppermute | solution.py:367
  68.2 14.3 %collective-permute-start.7 = (bf16[256,1024]{1,0:T(8,128)(2,1)S(1)}, bf16[256,1024]{1,0:T(8,128)(2,1)S(1)}, u32[]{:S(2)}, u32[]{:S(2)}) collective-permute-start(bf16[256,1024]{1,0:T(8,128)(2,1)S(1)} %attend0.1.own_ref), channel_id=1, source_target_pairs={{0,1},{1,2},{2,3},{3,0},{4,5},{5,6},{6,7},{7,4},{8,9},{9,10},{10,1... | collective-permute-start | bytes 1572872 | tf_op jit(solution)/shard_map/ppermute | solution.py:364
  73.9 16.7 %collective-permute-start.15 = (bf16[256,1024]{1,0:T(8,128)(2,1)S(1)}, bf16[256,1024]{1,0:T(8,128)(2,1)S(1)}, u32[]{:S(2)}, u32[]{:S(2)}) collective-permute-start(bf16[256,1024]{1,0:T(8,128)(2,1)S(1)} %attend1.1.own_ref), channel_id=1, source_target_pairs={{0,3},{1,0},{2,1},{3,2},{4,7},{5,4},{6,5},{7,6},{8,11},{9,8},{10,9... | collective-permute-start | bytes 1572872 | tf_op jit(solution)/shard_map/ppermute | solution.py:367
  76.7 17.1 %collective-permute-start.14 = (bf16[256,1024]{1,0:T(8,128)(2,1)S(1)}, bf16[256,1024]{1,0:T(8,128)(2,1)S(1)}, u32[]{:S(2)}, u32[]{:S(2)}) collective-permute-start(bf16[256,1024]{1,0:T(8,128)(2,1)S(1)} %attend1.1.own_ref), channel_id=1, source_target_pairs={{0,1},{1,2},{2,3},{3,0},{4,5},{5,6},{6,7},{7,4},{8,9},{9,10},{10,1... | collective-permute-start | bytes 1572872 | tf_op jit(solution)/shard_map/ppermute | solution.py:364
  82.5 22.5 %collective-permute-start.12 = (bf16[4,256,640]{2,1,0:T(8,128)(2,1)}, bf16[4,256,640]{2,1,0:T(8,128)(2,1)S(1)}, u32[]{:S(2)}, u32[]{:S(2)}) collective-permute-start(bf16[4,256,640]{2,1,0:T(8,128)(2,1)} %collective-permute-done.11), channel_id=1, source_target_pairs={{0,8},{8,0},{16,24},{24,16},{32,40},{40,32},{48,56},{56,48},{64,72... | collective-permute-start | bytes 3932168 | tf_op jit(solution)/shard_map/ppermute | solution.py:375
  84.7 11.6 %collective-permute-start.10 = (bf16[128,1024]{1,0:T(8,128)(2,1)S(1)}, bf16[128,1024]{1,0:T(8,128)(2,1)S(1)}, u32[]{:S(2)}, u32[]{:S(2)}) collective-permute-start(bf16[128,1024]{1,0:T(8,128)(2,1)S(1)} %slice.17), channel_id=1, source_target_pairs={{0,3},{1,0},{2,1},{3,2},{4,7},{5,4},{6,5},{7,6},{8,11},{9,8},{10,9... | collective-permute-start | bytes 786440 | tf_op jit(solution)/shard_map/ppermute | solution.py:367
  87.1 12.2 %collective-permute-start.9 = (bf16[128,1024]{1,0:T(8,128)(2,1)S(1)}, bf16[128,1024]{1,0:T(8,128)(2,1)S(1)}, u32[]{:S(2)}, u32[]{:S(2)}) collective-permute-start(bf16[128,1024]{1,0:T(8,128)(2,1)S(1)} %slice.16), channel_id=1, source_target_pairs={{0,1},{1,2},{2,3},{3,0},{4,5},{5,6},{6,7},{7,4},{8,9},{9,10},{10,1... | collective-permute-start | bytes 786440 | tf_op jit(solution)/shard_map/ppermute | solution.py:364
  99.3 6.2 %collective-permute-start.16 = (bf16[4,256,640]{2,1,0:T(8,128)(2,1)}, bf16[4,256,640]{2,1,0:T(8,128)(2,1)S(1)}, u32[]{:S(2)}, u32[]{:S(2)}) collective-permute-start(bf16[4,256,640]{2,1,0:T(8,128)(2,1)} %collective-permute-done.13), channel_id=1, source_target_pairs={{0,8},{8,0},{16,24},{24,16},{32,40},{40,32},{48,56},{56,48},{64,72... | collective-permute-start | bytes 3932168 | tf_op jit(solution)/shard_map/ppermute | solution.py:376
  100.7 8.0 %collective-permute-start.18 = (bf16[128,1024]{1,0:T(8,128)(2,1)S(1)}, bf16[128,1024]{1,0:T(8,128)(2,1)S(1)}, u32[]{:S(2)}, u32[]{:S(2)}) collective-permute-start(bf16[128,1024]{1,0:T(8,128)(2,1)S(1)} %slice.19), channel_id=1, source_target_pairs={{0,3},{1,0},{2,1},{3,2},{4,7},{5,4},{6,5},{7,6},{8,11},{9,8},{10,9... | collective-permute-start | bytes 786440 | tf_op jit(solution)/shard_map/ppermute | solution.py:367
  100.8 9.4 %collective-permute-start.17 = (bf16[128,1024]{1,0:T(8,128)(2,1)S(1)}, bf16[128,1024]{1,0:T(8,128)(2,1)S(1)}, u32[]{:S(2)}, u32[]{:S(2)}) collective-permute-start(bf16[128,1024]{1,0:T(8,128)(2,1)S(1)} %slice.18), channel_id=1, source_target_pairs={{0,1},{1,2},{2,3},{3,0},{4,5},{5,6},{6,7},{7,4},{8,9},{9,10},{10,1... | collective-permute-start | bytes 786440 | tf_op jit(solution)/shard_map/ppermute | solution.py:364
  108.1 8.8 %collective-permute-start.19 = (bf16[256,640]{1,0:T(8,128)(2,1)S(1)}, bf16[256,640]{1,0:T(8,128)(2,1)S(1)}, u32[]{:S(2)}, u32[]{:S(2)}) collective-permute-start(bf16[256,640]{1,0:T(8,128)(2,1)S(1)} %fusion.7), channel_id=1, source_target_pairs={{0,4},{1,5},{2,6},{3,7},{4,0},{5,1},{6,2},{7,3},{8,12},{9,13},{10,... | collective-permute-start | bytes 983048 | tf_op jit(solution)/shard_map/ppermute | solution.py:384
  114.1 2.8 %copy-start.1 = (bf16[4,256,640]{2,1,0:T(8,128)(2,1)S(1)}, bf16[4,256,640]{2,1,0:T(8,128)(2,1)}, u32[]{:S(2)}) copy-start(bf16[4,256,640]{2,1,0:T(8,128)(2,1)} %copy-done) | copy-start | bytes 3932164
  116.2 8.5 %collective-permute-start.20 = (bf16[256,640]{1,0:T(8,128)(2,1)S(1)}, bf16[256,640]{1,0:T(8,128)(2,1)S(1)}, u32[]{:S(2)}, u32[]{:S(2)}) collective-permute-start(bf16[256,640]{1,0:T(8,128)(2,1)S(1)} %fusion.6), channel_id=1, source_target_pairs={{0,4},{1,5},{2,6},{3,7},{4,0},{5,1},{6,2},{7,3},{8,12},{9,13},{10,... | collective-permute-start | bytes 983048 | tf_op jit(solution)/shard_map/ppermute | solution.py:388
  118.1 1.3 %copy-start.3 = (bf16[4,256,640]{2,1,0:T(8,128)(2,1)S(1)}, bf16[4,256,640]{2,1,0:T(8,128)(2,1)}, u32[]{:S(2)}) copy-start(bf16[4,256,640]{2,1,0:T(8,128)(2,1)} %copy-done.2) | copy-start | bytes 3932164

commit v4 on v3

--- a/solution.py
+++ b/solution.py
@@ -283,6 +283,7 @@
     leaf_values = rows_ref[: first + 2, :TOK, HD:].reshape(-1, HD)
     keys = jnp.concatenate([cache_keys, leaf_keys], axis=0)
     values = jnp.concatenate([cache_values, leaf_values], axis=0)
+    values = jnp.concatenate([values, jnp.ones_like(values)], axis=1)
     row = lax.broadcasted_iota(jnp.int32, (tokens, tokens), 0)
     col = lax.broadcasted_iota(jnp.int32, (tokens, tokens), 1)
     causal = jnp.where(col <= row, 0.0, MASKED)
@@ -306,9 +307,8 @@
         scores = jnp.concatenate(parts, axis=1)
         largest = jnp.max(scores, axis=1, keepdims=True)
         expon = jnp.exp2((scores - largest) * scale)
-        total = jnp.sum(expon, axis=1, keepdims=True)
-        summed = jnp.dot(expon.astype(jnp.bfloat16), values, preferred_element_type=jnp.float32)
-        done = (summed / total).astype(jnp.bfloat16)
+        both = jnp.dot(expon.astype(jnp.bfloat16), values, preferred_element_type=jnp.float32)
+        done = (both[:, :HD] / both[:, HD:]).astype(jnp.bfloat16)
         for i in range(per):
             g = tile * per + i
             out_ref[top : top + tokens, g * HD : (g + 1) * HD] = done[i * tokens : (i + 1) * tokens]

time: 126 us -> 126 us (level)
  transfers between devices with their start and end apart: 23 -> 23, of which waited for: 15 -> 15; matrix products, arithmetic and copies ran while one was open for 12% -> 12% of each run, Pallas kernels for 27% -> 26%
where the time goes in v4:
time: 126 us; the launch traced here: 125 us
  starting transfers between devices  40 us (32%)
  Pallas kernels  33.9 us (27%)
  waiting for transfers between devices  32 us (25%)
  matrix products  14.9 us (12%)
  local copies, waits for them, and re-layouts  3.07 us (2%)
    pallas_call x3, Pallas kernels, order(): pl.pallas_call(functools.partial(order_body, count), out_shape=[jax.Shape...  17.2 us
    dot_general x16, matrix products, project(): jnp.dot(rows, matrix.reshape(rows.shape[1], -1), preferred_element_type=j...  14.9 us
    ppermute x3, starting transfers between devices, per_device(): slots = [lax.ppermute(cache, 'leaf', z_shift(k)) for k in (1, 2, 3)]  11.3 us
    ppermute x4, waiting for transfers between devices, up(): return lax.ppermute(part, 'seq', y_shift(1))  10.8 us
    pallas_call x2, Pallas kernels, attend(): pl.pallas_call(functools.partial(attend_body, chunk), out_shape=jax.Shape...  9.85 us
    ppermute x4, waiting for transfers between devices, down(): return lax.ppermute(part, 'seq', y_shift(-1))  7.71 us
    ppermute x4, starting transfers between devices, down(): return lax.ppermute(part, 'seq', y_shift(-1))  5.37 us
    all_to_all x1, starting transfers between devices, per_device(): mine = lax.all_to_all(after(packed, rows), 'seq', 0, 0)  5.19 us
  transfers between devices with their start and end apart: 23, of which 15 were waited for; matrix products, arithmetic and copies ran while one was open for 12% of the time, Pallas kernels for 26%

profile of v4, /device:TPU:1, one launch (start us, length us, event | category | flops | bytes accessed | tf_op | source)
XLA Modules:
  0.0 125.2 jit_solution(10556605078829293707)
XLA Ops:
  0.0 3.8 %collective-permute-start = (bf16[16,2048]{1,0:T(8,128)(2,1)}, bf16[16,2048]{1,0:T(8,128)(2,1)S(1)}, u32[]{:S(2)}, u32[]{:S(2)}) collective-permute-start(bf16[16,2048]{1,0:T(8,128)(2,1)} %cache_hbm.1), channel_id=1, source_target_pairs={{0,16},{8,24},{16,32},{24,40},{32,48},{40,56},{48,0},{56,8},{64,80... | collective-permute-start | bytes 196616 | tf_op jit(solution)/shard_map/ppermute | solution.py:347
  3.8 5.1 %collective-permute-start.1 = (bf16[16,2048]{1,0:T(8,128)(2,1)}, bf16[16,2048]{1,0:T(8,128)(2,1)S(1)}, u32[]{:S(2)}, u32[]{:S(2)}) collective-permute-start(bf16[16,2048]{1,0:T(8,128)(2,1)} %cache_hbm.1), channel_id=1, source_target_pairs={{0,32},{8,40},{16,48},{24,56},{32,0},{40,8},{48,16},{56,24},{64,96... | collective-permute-start | bytes 196616 | tf_op jit(solution)/shard_map/ppermute | solution.py:347
  8.9 2.4 %collective-permute-start.2 = (bf16[16,2048]{1,0:T(8,128)(2,1)}, bf16[16,2048]{1,0:T(8,128)(2,1)S(1)}, u32[]{:S(2)}, u32[]{:S(2)}) collective-permute-start(bf16[16,2048]{1,0:T(8,128)(2,1)} %cache_hbm.1), channel_id=1, source_target_pairs={{0,48},{8,56},{16,0},{24,8},{32,16},{40,24},{48,32},{56,40},{64,11... | collective-permute-start | bytes 196616 | tf_op jit(solution)/shard_map/ppermute | solution.py:347
  11.4 4.1 %order.4 = bf16[4,256,640]{2,1,0:T(8,128)(2,1)} custom-call(s32[9]{0:T(128)S(1)} %stack.36.ids_ref, bf16[8,4,256,640]{3,2,1,0:T(8,128)(2,1)} %bitcast.63), custom_call_target="tpu_custom_call" | custom-call | flops 1 | bytes 1 | tf_op jit(solution)/shard_map/order/pallas_call | solution.py:170
  15.5 1.3 %collective-permute-done.2.refs_2_ = bf16[16,2048]{1,0:T(8,128)(2,1)S(1)} collective-permute-done((bf16[16,2048]{1,0:T(8,128)(2,1)}, bf16[16,2048]{1,0:T(8,128)(2,1)S(1)}, u32[]{:S(2)}, u32[]{:S(2)}) %collective-permute-start.2) | collective-permute-done | bytes 65568 | tf_op jit(solution)/shard_map/ppermute | solution.py:347
  16.8 1.0 pack_rows.1
  17.8 4.2 %all-to-all-start = ((bf16[8,128,256]{2,1,0:T(8,128)(2,1)}), bf16[8,128,256]{2,1,0:T(8,128)(2,1)S(1)}, u32[]{:S(2)}, u32[]{:S(2)}) async-start(bf16[8,128,256]{2,1,0:T(8,128)(2,1)} %pack_rows.1), calls=%async_computation | async-start | bytes 1048576 | tf_op jit(solution)/shard_map/all_to_all | solution.py:349
  22.0 4.1 %order.3 = bf16[4,256,640]{2,1,0:T(8,128)(2,1)} custom-call(s32[9]{0:T(128)S(1)} %stack.36.ids_ref, bf16[8,4,256,640]{3,2,1,0:T(8,128)(2,1)} %bitcast.64), custom_call_target="tpu_custom_call" | custom-call | flops 1 | bytes 1 | tf_op jit(solution)/shard_map/order/pallas_call | solution.py:170
  26.1 1.6 %pack_queries.1 = (bf16[8,256,256]{2,1,0:T(8,128)(2,1)}, f32[1,768]{1,0:T(1,128)S(1)}) custom-call(s32[9]{0:T(128)S(1)} %stack.36.ids_ref, s32[48]{0:T(128)S(1)} %copy-done.7, s32[16]{0:T(128)S(1)} %copy-done.9, bf16[64,8192]{1,0:T(8,128)(2,1)S(1)} %bitcast.62), custom_call_target="tpu_custom_call" | custom-call | flops 1 | bytes 1 | tf_op jit(solution)/shard_map/pack_queries/pallas_call | solution.py:133
  27.7 2.1 %all-to-all-done.rows_ref = bf16[8,128,256]{2,1,0:T(8,128)(2,1)S(1)} async-done(((bf16[8,128,256]{2,1,0:T(8,128)(2,1)}), bf16[8,128,256]{2,1,0:T(8,128)(2,1)S(1)}, u32[]{:S(2)}, u32[]{:S(2)}) %all-to-all-start) | async-done | bytes 524320 | tf_op jit(solution)/shard_map/all_to_all | solution.py:349
  29.8 5.2 %all-to-all-start.1 = ((bf16[8,256,256]{2,1,0:T(8,128)(2,1)}), bf16[8,256,256]{2,1,0:T(8,128)(2,1)}, u32[]{:S(2)}, u32[]{:S(2)}) async-start(bf16[8,256,256]{2,1,0:T(8,128)(2,1)} %get-tuple-element.57), calls=%async_computation.1 | async-start | bytes 2097152 | tf_op jit(solution)/shard_map/all_to_all | solution.py:354
  35.1 2.6 %collective-permute-start.5 = (bf16[8,64,256]{2,1,0:T(8,128)(2,1)S(1)}, bf16[8,64,256]{2,1,0:T(8,128)(2,1)S(1)}, u32[]{:S(2)}, u32[]{:S(2)}) collective-permute-start(bf16[8,64,256]{2,1,0:T(8,128)(2,1)S(1)} %slice.20.refs_0_), channel_id=1, source_target_pairs={{0,192},{8,200},{16,208},{24,216},{32,224},{40,232},{48,240},{56,2... | collective-permute-start | bytes 786440 | tf_op jit(solution)/shard_map/ppermute | solution.py:353
  38.1 0.6 collective-permute-start.3
  38.7 9.1 %order.5 = (bf16[4,256,640]{2,1,0:T(8,128)(2,1)S(1)}, bf16[4,256,640]{2,1,0:T(8,128)(2,1)S(1)}, bf16[4,256,640]{2,1,0:T(8,128)(2,1)S(1)}, bf16[4,256,640]{2,1,0:T(8,128)(2,1)S(1)}) custom-call(s32[9]{0:T(128)S(1)} %stack.36.ids_ref, bf16[8,4,256,640]{3,2,1,0:T(8,128)(2,1)} %bitcast.65), custom_call_target="tpu_custom_call" | custom-call | flops 1 | bytes 1 | tf_op jit(solution)/shard_map/order/pallas_call | solution.py:170
  47.9 1.1 copy-done
  48.9 1.1 copy-done.2
  50.0 2.9 %collective-permute-done.3.refs_1_ = bf16[8,64,256]{2,1,0:T(8,128)(2,1)S(1)} collective-permute-done((bf16[8,64,256]{2,1,0:T(8,128)(2,1)S(1)}, bf16[8,64,256]{2,1,0:T(8,128)(2,1)S(1)}, u32[]{:S(2)}, u32[]{:S(2)}) %collective-permute-start.3) | collective-permute-done | bytes 262176 | tf_op jit(solution)/shard_map/ppermute | solution.py:353
  53.0 1.3 %pick.1 = (bf16[6,8,16,256]{3,2,1,0:T(8,128)(2,1)S(1)}, bf16[6,8,16,256]{3,2,1,0:T(8,128)(2,1)S(1)}) custom-call(s32[9]{0:T(128)S(1)} %stack.36.ids_ref, s32[48]{0:T(128)S(1)} %copy-done.7, s32[16]{0:T(128)S(1)} %copy-done.8, bf16[8,64,256]{2,1,0:T(8,128)(2,1)S(1)} %slice.20.refs_0_, bf16[8,64,256]{2,1,0:T(8,128)(2,1)S(1)} %collective-permute-done.3.refs_1_, ...), custom_call_target="tpu_custom_call" | custom-call | flops 1 | bytes 1 | tf_op jit(solution)/shard_map/pick/pallas_call | solution.py:230
  54.3 3.3 %collective-permute-start.11 = (bf16[4,256,640]{2,1,0:T(8,128)(2,1)}, bf16[4,256,640]{2,1,0:T(8,128)(2,1)}, u32[]{:S(2)}, u32[]{:S(2)}) collective-permute-start(bf16[4,256,640]{2,1,0:T(8,128)(2,1)} %order.4), channel_id=1, source_target_pairs={{0,4},{8,60},{1,5},{9,61},{2,6},{10,62},{3,7},{11,63},{4,0},{12,24... | collective-permute-start | bytes 3932168 | tf_op jit(solution)/shard_map/ppermute | solution.py:360
  57.7 1.7 %collective-permute-done.6.received_ref = bf16[6,8,16,256]{3,2,1,0:T(8,128)(2,1)S(1)} collective-permute-done((bf16[6,8,16,256]{3,2,1,0:T(8,128)(2,1)S(1)}, bf16[6,8,16,256]{3,2,1,0:T(8,128)(2,1)S(1)}, u32[]{:S(2)}, u32[]{:S(2)}) %collective-permute-start.6) | collective-permute-done | bytes 393248 | tf_op jit(solution)/shard_map/ppermute | solution.py:358
  59.4 1.3 %merge.1.cache_ref = bf16[6,8,16,256]{3,2,1,0:T(8,128)(2,1)S(1)} custom-call(s32[9]{0:T(128)S(1)} %stack.36.ids_ref, s32[48]{0:T(128)S(1)} %copy-done.7, s32[16]{0:T(128)S(1)} %copy-done.8, bf16[6,8,16,256]{3,2,1,0:T(8,128)(2,1)S(1)} %get-tuple-element.65.own_ref, bf16[6,8,16,256]{3,2,1,0:T(8,128)(2,1)S(1)} %collective-permute-done.6.received_ref), custom_call_target="tpu_custom_call" | custom-call | flops 1 | bytes 1 | tf_op jit(solution)/shard_map/merge/pallas_call | solution.py:258
  60.7 4.5 %attend0.1.own_ref = bf16[256,1024]{1,0:T(8,128)(2,1)S(1)} custom-call(f32[1,768]{1,0:T(1,128)S(1)} %get-tuple-element.51.bias_ref, bf16[8,256,256]{2,1,0:T(8,128)(2,1)} %all-to-all-done.1.mine_ref, bf16[8,128,256]{2,1,0:T(8,128)(2,1)S(1)} %all-to-all-done.rows_ref, bf16[6,8,16,256]{3,2,1,0:T(8,128)(2,1)S(1)} %merge.1.cache_ref), custom_call_target="tpu_custom_call" | custom-call | flops 1500000000 | bytes 1 | tf_op jit(solution)/shard_map/attend0/pallas_call | solution.py:318
  65.2 2.5 %collective-permute-start.8 = (bf16[256,1024]{1,0:T(8,128)(2,1)S(1)}, bf16[256,1024]{1,0:T(8,128)(2,1)S(1)}, u32[]{:S(2)}, u32[]{:S(2)}) collective-permute-start(bf16[256,1024]{1,0:T(8,128)(2,1)S(1)} %attend0.1.own_ref), channel_id=1, source_target_pairs={{0,3},{1,0},{2,1},{3,2},{4,7},{5,4},{6,5},{7,6},{8,11},{9,8},{10,9... | collective-permute-start | bytes 1572872 | tf_op jit(solution)/shard_map/ppermute | solution.py:367
  67.7 5.3 %attend1.1.own_ref = bf16[256,1024]{1,0:T(8,128)(2,1)S(1)} custom-call(f32[1,768]{1,0:T(1,128)S(1)} %get-tuple-element.51.bias_ref, bf16[8,256,256]{2,1,0:T(8,128)(2,1)} %all-to-all-done.1.mine_ref, bf16[8,128,256]{2,1,0:T(8,128)(2,1)S(1)} %all-to-all-done.rows_ref, bf16[6,8,16,256]{3,2,1,0:T(8,128)(2,1)S(1)} %merge.1.cache_ref), custom_call_target="tpu_custom_call" | custom-call | flops 1500000000 | bytes 1 | tf_op jit(solution)/shard_map/attend1/pallas_call | solution.py:318
  73.0 2.7 %collective-permute-start.15 = (bf16[256,1024]{1,0:T(8,128)(2,1)S(1)}, bf16[256,1024]{1,0:T(8,128)(2,1)S(1)}, u32[]{:S(2)}, u32[]{:S(2)}) collective-permute-start(bf16[256,1024]{1,0:T(8,128)(2,1)S(1)} %attend1.1.own_ref), channel_id=1, source_target_pairs={{0,3},{1,0},{2,1},{3,2},{4,7},{5,4},{6,5},{7,6},{8,11},{9,8},{10,9... | collective-permute-start | bytes 1572872 | tf_op jit(solution)/shard_map/ppermute | solution.py:367
  75.7 3.1 %collective-permute-done.8.down_ref = bf16[256,1024]{1,0:T(8,128)(2,1)S(1)} collective-permute-done((bf16[256,1024]{1,0:T(8,128)(2,1)S(1)}, bf16[256,1024]{1,0:T(8,128)(2,1)S(1)}, u32[]{:S(2)}, u32[]{:S(2)}) %collective-permute-start.8) | collective-permute-done | bytes 524320 | tf_op jit(solution)/shard_map/ppermute | solution.py:367
  78.8 3.1 %collective-permute-done.7.up_ref = bf16[256,1024]{1,0:T(8,128)(2,1)S(1)} collective-permute-done((bf16[256,1024]{1,0:T(8,128)(2,1)S(1)}, bf16[256,1024]{1,0:T(8,128)(2,1)S(1)}, u32[]{:S(2)}, u32[]{:S(2)}) %collective-permute-start.7) | collective-permute-done | bytes 524320 | tf_op jit(solution)/shard_map/ppermute | solution.py:364
  81.9 2.1 %collective-permute-start.12 = (bf16[4,256,640]{2,1,0:T(8,128)(2,1)}, bf16[4,256,640]{2,1,0:T(8,128)(2,1)S(1)}, u32[]{:S(2)}, u32[]{:S(2)}) collective-permute-start(bf16[4,256,640]{2,1,0:T(8,128)(2,1)} %collective-permute-done.11), channel_id=1, source_target_pairs={{0,8},{8,0},{16,24},{24,16},{32,40},{40,32},{48,56},{56,48},{64,72... | collective-permute-start | bytes 3932168 | tf_op jit(solution)/shard_map/ppermute | solution.py:375
  84.2 2.9 %collective-permute-done.13 = bf16[4,256,640]{2,1,0:T(8,128)(2,1)} collective-permute-done((bf16[4,256,640]{2,1,0:T(8,128)(2,1)}, bf16[4,256,640]{2,1,0:T(8,128)(2,1)}, u32[]{:S(2)}, u32[]{:S(2)}) %collective-permute-start.13) | collective-permute-done | bytes 1310752 | tf_op jit(solution)/shard_map/ppermute | solution.py:361
  87.1 1.0 collective-permute-start.9
  88.1 2.0 %collective-permute-done.15.down_ref = bf16[256,1024]{1,0:T(8,128)(2,1)S(1)} collective-permute-done((bf16[256,1024]{1,0:T(8,128)(2,1)S(1)}, bf16[256,1024]{1,0:T(8,128)(2,1)S(1)}, u32[]{:S(2)}, u32[]{:S(2)}) %collective-permute-start.15) | collective-permute-done | bytes 524320 | tf_op jit(solution)/shard_map/ppermute | solution.py:367
  90.1 3.1 %collective-permute-done.14.up_ref = bf16[256,1024]{1,0:T(8,128)(2,1)S(1)} collective-permute-done((bf16[256,1024]{1,0:T(8,128)(2,1)S(1)}, bf16[256,1024]{1,0:T(8,128)(2,1)S(1)}, u32[]{:S(2)}, u32[]{:S(2)}) %collective-permute-start.14) | collective-permute-done | bytes 524320 | tf_op jit(solution)/shard_map/ppermute | solution.py:364
  93.2 2.5 %collective-permute-done.10.high_ref = bf16[128,1024]{1,0:T(8,128)(2,1)S(1)} collective-permute-done((bf16[128,1024]{1,0:T(8,128)(2,1)S(1)}, bf16[128,1024]{1,0:T(8,128)(2,1)S(1)}, u32[]{:S(2)}, u32[]{:S(2)}) %collective-permute-start.10) | collective-permute-done | bytes 262176 | tf_op jit(solution)/shard_map/ppermute | solution.py:367
  95.7 3.1 %collective-permute-done.9.low_ref = bf16[128,1024]{1,0:T(8,128)(2,1)S(1)} collective-permute-done((bf16[128,1024]{1,0:T(8,128)(2,1)S(1)}, bf16[128,1024]{1,0:T(8,128)(2,1)S(1)}, u32[]{:S(2)}, u32[]{:S(2)}) %collective-permute-start.9) | collective-permute-done | bytes 262176 | tf_op jit(solution)/shard_map/ppermute | solution.py:364
  98.8 1.3 %collective-permute-start.16 = (bf16[4,256,640]{2,1,0:T(8,128)(2,1)}, bf16[4,256,640]{2,1,0:T(8,128)(2,1)S(1)}, u32[]{:S(2)}, u32[]{:S(2)}) collective-permute-start(bf16[4,256,640]{2,1,0:T(8,128)(2,1)} %collective-permute-done.13), channel_id=1, source_target_pairs={{0,8},{8,0},{16,24},{24,16},{32,40},{40,32},{48,56},{56,48},{64,72... | collective-permute-start | bytes 3932168 | tf_op jit(solution)/shard_map/ppermute | solution.py:376
  100.2 1.5 %collective-permute-start.17 = (bf16[128,1024]{1,0:T(8,128)(2,1)S(1)}, bf16[128,1024]{1,0:T(8,128)(2,1)S(1)}, u32[]{:S(2)}, u32[]{:S(2)}) collective-permute-start(bf16[128,1024]{1,0:T(8,128)(2,1)S(1)} %slice.18), channel_id=1, source_target_pairs={{0,1},{1,2},{2,3},{3,0},{4,5},{5,6},{6,7},{7,4},{8,9},{9,10},{10,1... | collective-permute-start | bytes 786440 | tf_op jit(solution)/shard_map/ppermute | solution.py:364
  101.7 0.8 join.2
  102.5 1.9 %fusion.11 = f32[256,640]{1,0:T(8,128)S(1)} fusion(bf16[256,1024]{1,0:T(8,128)(2,1)S(1)} %get-tuple-element.87, bf16[1024,640]{1,0:T(8,128)(2,1)} %bitcast.12), kind=kOutput, calls=%fused_computation.20 | convolution fusion | flops 335544320 | bytes 2490368 | tf_op jit(solution)/shard_map/dot_general | solution.py:336
  105.6 2.0 %fusion.7 = bf16[256,640]{1,0:T(8,128)(2,1)S(1)} fusion(f32[256,640]{1,0:T(8,128)S(1)} %fusion.12, f32[256,640]{1,0:T(8,128)S(1)} %fusion.11, f32[256,640]{1,0:T(8,128)S(1)} %fusion.10, bf16[256,1024]{1,0:T(8,128)(2,1)S(1)} %get-tuple-element.85, bf16[1024,640]{1,0:T(8,128)(2,1)} %bitcast.10), kind=kOutput, calls=%fused_computation.13 | convolution fusion | flops 336199680 | bytes 4128768 | tf_op jit(solution)/shard_map/dot_general | solution.py:336
  108.1 1.5 %collective-permute-done.17.low_ref = bf16[128,1024]{1,0:T(8,128)(2,1)S(1)} collective-permute-done((bf16[128,1024]{1,0:T(8,128)(2,1)S(1)}, bf16[128,1024]{1,0:T(8,128)(2,1)S(1)}, u32[]{:S(2)}, u32[]{:S(2)}) %collective-permute-start.17) | collective-permute-done | bytes 262176 | tf_op jit(solution)/shard_map/ppermute | solution.py:364
  109.7 0.8 join.3
  111.1 1.9 %fusion.14 = f32[256,640]{1,0:T(8,128)S(1)} fusion(bf16[256,1024]{1,0:T(8,128)(2,1)S(1)} %get-tuple-element.91, bf16[1024,640]{1,0:T(8,128)(2,1)} %bitcast.12), kind=kOutput, calls=%fused_computation.23 | convolution fusion | flops 335544320 | bytes 2490368 | tf_op jit(solution)/shard_map/dot_general | solution.py:336
  113.6 2.1 %fusion.6 = bf16[256,640]{1,0:T(8,128)(2,1)S(1)} fusion(f32[256,640]{1,0:T(8,128)S(1)} %fusion.15, f32[256,640]{1,0:T(8,128)S(1)} %fusion.14, f32[256,640]{1,0:T(8,128)S(1)} %fusion.13, bf16[256,1024]{1,0:T(8,128)(2,1)S(1)} %get-tuple-element.89, bf16[1024,640]{1,0:T(8,128)(2,1)} %bitcast.10), kind=kOutput, calls=%fused_computation.12 | convolution fusion | flops 336199680 | bytes 4128768 | tf_op jit(solution)/shard_map/dot_general | solution.py:336
  118.2 0.7 copy-done.3
  118.9 0.6 fusion.5
  120.1 0.6 convolution_add_fusion.2
  122.0 2.2 %collective-permute-done.20 = bf16[256,640]{1,0:T(8,128)(2,1)S(1)} collective-permute-done((bf16[256,640]{1,0:T(8,128)(2,1)S(1)}, bf16[256,640]{1,0:T(8,128)(2,1)S(1)}, u32[]{:S(2)}, u32[]{:S(2)}) %collective-permute-start.20) | collective-permute-done | bytes 327712 | tf_op jit(solution)/shard_map/ppermute | solution.py:388
  124.3 0.9 pad_maximum_fusion
  (54 shorter events, 8.4 us)
Async XLA Ops:
  0.0 11.4 %collective-permute-start = (bf16[16,2048]{1,0:T(8,128)(2,1)}, bf16[16,2048]{1,0:T(8,128)(2,1)S(1)}, u32[]{:S(2)}, u32[]{:S(2)}) collective-permute-start(bf16[16,2048]{1,0:T(8,128)(2,1)} %cache_hbm.1), channel_id=1, source_target_pairs={{0,16},{8,24},{16,32},{24,40},{32,48},{40,56},{48,0},{56,8},{64,80... | collective-permute-start | bytes 196616 | tf_op jit(solution)/shard_map/ppermute | solution.py:347
  3.8 11.7 %collective-permute-start.1 = (bf16[16,2048]{1,0:T(8,128)(2,1)}, bf16[16,2048]{1,0:T(8,128)(2,1)S(1)}, u32[]{:S(2)}, u32[]{:S(2)}) collective-permute-start(bf16[16,2048]{1,0:T(8,128)(2,1)} %cache_hbm.1), channel_id=1, source_target_pairs={{0,32},{8,40},{16,48},{24,56},{32,0},{40,8},{48,16},{56,24},{64,96... | collective-permute-start | bytes 196616 | tf_op jit(solution)/shard_map/ppermute | solution.py:347
  8.9 7.9 %collective-permute-start.2 = (bf16[16,2048]{1,0:T(8,128)(2,1)}, bf16[16,2048]{1,0:T(8,128)(2,1)S(1)}, u32[]{:S(2)}, u32[]{:S(2)}) collective-permute-start(bf16[16,2048]{1,0:T(8,128)(2,1)} %cache_hbm.1), channel_id=1, source_target_pairs={{0,48},{8,56},{16,0},{24,8},{32,16},{40,24},{48,32},{56,40},{64,11... | collective-permute-start | bytes 196616 | tf_op jit(solution)/shard_map/ppermute | solution.py:347
  11.4 5.4 %copy-start.5 = (bf16[1,64,2048]{2,1,0:T(8,128)(2,1)S(1)}, bf16[1,64,2048]{2,1,0:T(8,128)(2,1)}, u32[]{:S(2)}) copy-start(bf16[1,64,2048]{2,1,0:T(8,128)(2,1)} %kv_hbm.1) | copy-start | bytes 786436
  11.4 5.4 %copy-start.6 = (bf16[16,2048]{1,0:T(8,128)(2,1)S(1)}, bf16[16,2048]{1,0:T(8,128)(2,1)}, u32[]{:S(2)}) copy-start(bf16[16,2048]{1,0:T(8,128)(2,1)} %cache_hbm.1) | copy-start | bytes 196612
  17.8 12.0 %all-to-all-start = ((bf16[8,128,256]{2,1,0:T(8,128)(2,1)}), bf16[8,128,256]{2,1,0:T(8,128)(2,1)S(1)}, u32[]{:S(2)}, u32[]{:S(2)}) async-start(bf16[8,128,256]{2,1,0:T(8,128)(2,1)} %pack_rows.1), calls=%async_computation | async-start | bytes 1048576 | tf_op jit(solution)/shard_map/all_to_all | solution.py:349
  22.0 4.1 %copy-start.4 = (bf16[1,64,8192]{2,1,0:T(8,128)(2,1)S(1)}, bf16[1,64,8192]{2,1,0:T(8,128)(2,1)}, u32[]{:S(2)}) copy-start(bf16[1,64,8192]{2,1,0:T(8,128)(2,1)} %param.7) | copy-start | bytes 3145732
  22.0 4.1 %copy-start.7 = (s32[48]{0:T(128)S(1)}, s32[48]{0:T(128)}, u32[]{:S(2)}) copy-start(s32[48]{0:T(128)} %parent_ref.5) | copy-start | bytes 580
  22.0 4.1 %copy-start.9 = (s32[16]{0:T(128)S(1)}, s32[16]{0:T(128)}, u32[]{:S(2)}) copy-start(s32[16]{0:T(128)} %lengths_ref.1) | copy-start | bytes 196
  29.8 30.8 %all-to-all-start.1 = ((bf16[8,256,256]{2,1,0:T(8,128)(2,1)}), bf16[8,256,256]{2,1,0:T(8,128)(2,1)}, u32[]{:S(2)}, u32[]{:S(2)}) async-start(bf16[8,256,256]{2,1,0:T(8,128)(2,1)} %get-tuple-element.57), calls=%async_computation.1 | async-start | bytes 2097152 | tf_op jit(solution)/shard_map/all_to_all | solution.py:354
  35.0 17.9 %copy-start.8 = (s32[16]{0:T(128)S(1)}, s32[16]{0:T(128)}, u32[]{:S(2)}) copy-start(s32[16]{0:T(128)} %owner_ref.3) | copy-start | bytes 196
  35.1 15.0 %collective-permute-start.5 = (bf16[8,64,256]{2,1,0:T(8,128)(2,1)S(1)}, bf16[8,64,256]{2,1,0:T(8,128)(2,1)S(1)}, u32[]{:S(2)}, u32[]{:S(2)}) collective-permute-start(bf16[8,64,256]{2,1,0:T(8,128)(2,1)S(1)} %slice.20.refs_0_), channel_id=1, source_target_pairs={{0,192},{8,200},{16,208},{24,216},{32,224},{40,232},{48,240},{56,2... | collective-permute-start | bytes 786440 | tf_op jit(solution)/shard_map/ppermute | solution.py:353
  37.6 12.4 %collective-permute-start.4 = (bf16[8,64,256]{2,1,0:T(8,128)(2,1)S(1)}, bf16[8,64,256]{2,1,0:T(8,128)(2,1)S(1)}, u32[]{:S(2)}, u32[]{:S(2)}) collective-permute-start(bf16[8,64,256]{2,1,0:T(8,128)(2,1)S(1)} %slice.20.refs_0_), channel_id=1, source_target_pairs={{0,128},{8,136},{16,144},{24,152},{32,160},{40,168},{48,176},{56,1... | collective-permute-start | bytes 786440 | tf_op jit(solution)/shard_map/ppermute | solution.py:353
  38.1 14.8 %collective-permute-start.3 = (bf16[8,64,256]{2,1,0:T(8,128)(2,1)S(1)}, bf16[8,64,256]{2,1,0:T(8,128)(2,1)S(1)}, u32[]{:S(2)}, u32[]{:S(2)}) collective-permute-start(bf16[8,64,256]{2,1,0:T(8,128)(2,1)S(1)} %slice.20.refs_0_), channel_id=1, source_target_pairs={{0,64},{8,72},{16,80},{24,88},{32,96},{40,104},{48,112},{56,120},{... | collective-permute-start | bytes 786440 | tf_op jit(solution)/shard_map/ppermute | solution.py:353
  47.9 1.1 copy-start
  48.9 1.1 copy-start.2
  54.3 21.5 %collective-permute-start.11 = (bf16[4,256,640]{2,1,0:T(8,128)(2,1)}, bf16[4,256,640]{2,1,0:T(8,128)(2,1)}, u32[]{:S(2)}, u32[]{:S(2)}) collective-permute-start(bf16[4,256,640]{2,1,0:T(8,128)(2,1)} %order.4), channel_id=1, source_target_pairs={{0,4},{8,60},{1,5},{9,61},{2,6},{10,62},{3,7},{11,63},{4,0},{12,24... | collective-permute-start | bytes 3932168 | tf_op jit(solution)/shard_map/ppermute | solution.py:360
  57.6 29.5 %collective-permute-start.13 = (bf16[4,256,640]{2,1,0:T(8,128)(2,1)}, bf16[4,256,640]{2,1,0:T(8,128)(2,1)}, u32[]{:S(2)}, u32[]{:S(2)}) collective-permute-start(bf16[4,256,640]{2,1,0:T(8,128)(2,1)} %order.3), channel_id=1, source_target_pairs={{0,4},{8,60},{1,5},{9,61},{2,6},{10,62},{3,7},{11,63},{4,0},{12,24... | collective-permute-start | bytes 3932168 | tf_op jit(solution)/shard_map/ppermute | solution.py:361
  57.7 1.7 %collective-permute-start.6 = (bf16[6,8,16,256]{3,2,1,0:T(8,128)(2,1)S(1)}, bf16[6,8,16,256]{3,2,1,0:T(8,128)(2,1)S(1)}, u32[]{:S(2)}, u32[]{:S(2)}) collective-permute-start(bf16[6,8,16,256]{3,2,1,0:T(8,128)(2,1)S(1)} %get-tuple-element.66), channel_id=1, source_target_pairs={{0,8},{8,0},{16,24},{24,16},{32,40},{40,32},{48,56},{56,48},{64,72... | collective-permute-start | bytes 1179656 | tf_op jit(solution)/shard_map/ppermute | solution.py:358
  65.2 13.6 %collective-permute-start.8 = (bf16[256,1024]{1,0:T(8,128)(2,1)S(1)}, bf16[256,1024]{1,0:T(8,128)(2,1)S(1)}, u32[]{:S(2)}, u32[]{:S(2)}) collective-permute-start(bf16[256,1024]{1,0:T(8,128)(2,1)S(1)} %attend0.1.own_ref), channel_id=1, source_target_pairs={{0,3},{1,0},{2,1},{3,2},{4,7},{5,4},{6,5},{7,6},{8,11},{9,8},{10,9... | collective-permute-start | bytes 1572872 | tf_op jit(solution)/shard_map/ppermute | solution.py:367
  67.7 14.3 %collective-permute-start.7 = (bf16[256,1024]{1,0:T(8,128)(2,1)S(1)}, bf16[256,1024]{1,0:T(8,128)(2,1)S(1)}, u32[]{:S(2)}, u32[]{:S(2)}) collective-permute-start(bf16[256,1024]{1,0:T(8,128)(2,1)S(1)} %attend0.1.own_ref), channel_id=1, source_target_pairs={{0,1},{1,2},{2,3},{3,0},{4,5},{5,6},{6,7},{7,4},{8,9},{9,10},{10,1... | collective-permute-start | bytes 1572872 | tf_op jit(solution)/shard_map/ppermute | solution.py:364
  73.0 17.1 %collective-permute-start.15 = (bf16[256,1024]{1,0:T(8,128)(2,1)S(1)}, bf16[256,1024]{1,0:T(8,128)(2,1)S(1)}, u32[]{:S(2)}, u32[]{:S(2)}) collective-permute-start(bf16[256,1024]{1,0:T(8,128)(2,1)S(1)} %attend1.1.own_ref), channel_id=1, source_target_pairs={{0,3},{1,0},{2,1},{3,2},{4,7},{5,4},{6,5},{7,6},{8,11},{9,8},{10,9... | collective-permute-start | bytes 1572872 | tf_op jit(solution)/shard_map/ppermute | solution.py:367
  75.7 17.4 %collective-permute-start.14 = (bf16[256,1024]{1,0:T(8,128)(2,1)S(1)}, bf16[256,1024]{1,0:T(8,128)(2,1)S(1)}, u32[]{:S(2)}, u32[]{:S(2)}) collective-permute-start(bf16[256,1024]{1,0:T(8,128)(2,1)S(1)} %attend1.1.own_ref), channel_id=1, source_target_pairs={{0,1},{1,2},{2,3},{3,0},{4,5},{5,6},{6,7},{7,4},{8,9},{9,10},{10,1... | collective-permute-start | bytes 1572872 | tf_op jit(solution)/shard_map/ppermute | solution.py:364
  81.9 22.5 %collective-permute-start.12 = (bf16[4,256,640]{2,1,0:T(8,128)(2,1)}, bf16[4,256,640]{2,1,0:T(8,128)(2,1)S(1)}, u32[]{:S(2)}, u32[]{:S(2)}) collective-permute-start(bf16[4,256,640]{2,1,0:T(8,128)(2,1)} %collective-permute-done.11), channel_id=1, source_target_pairs={{0,8},{8,0},{16,24},{24,16},{32,40},{40,32},{48,56},{56,48},{64,72... | collective-permute-start | bytes 3932168 | tf_op jit(solution)/shard_map/ppermute | solution.py:375
  84.1 11.6 %collective-permute-start.10 = (bf16[128,1024]{1,0:T(8,128)(2,1)S(1)}, bf16[128,1024]{1,0:T(8,128)(2,1)S(1)}, u32[]{:S(2)}, u32[]{:S(2)}) collective-permute-start(bf16[128,1024]{1,0:T(8,128)(2,1)S(1)} %slice.17), channel_id=1, source_target_pairs={{0,3},{1,0},{2,1},{3,2},{4,7},{5,4},{6,5},{7,6},{8,11},{9,8},{10,9... | collective-permute-start | bytes 786440 | tf_op jit(solution)/shard_map/ppermute | solution.py:367
  87.1 11.7 %collective-permute-start.9 = (bf16[128,1024]{1,0:T(8,128)(2,1)S(1)}, bf16[128,1024]{1,0:T(8,128)(2,1)S(1)}, u32[]{:S(2)}, u32[]{:S(2)}) collective-permute-start(bf16[128,1024]{1,0:T(8,128)(2,1)S(1)} %slice.16), channel_id=1, source_target_pairs={{0,1},{1,2},{2,3},{3,0},{4,5},{5,6},{6,7},{7,4},{8,9},{9,10},{10,1... | collective-permute-start | bytes 786440 | tf_op jit(solution)/shard_map/ppermute | solution.py:364
  98.8 6.2 %collective-permute-start.16 = (bf16[4,256,640]{2,1,0:T(8,128)(2,1)}, bf16[4,256,640]{2,1,0:T(8,128)(2,1)S(1)}, u32[]{:S(2)}, u32[]{:S(2)}) collective-permute-start(bf16[4,256,640]{2,1,0:T(8,128)(2,1)} %collective-permute-done.13), channel_id=1, source_target_pairs={{0,8},{8,0},{16,24},{24,16},{32,40},{40,32},{48,56},{56,48},{64,72... | collective-permute-start | bytes 3932168 | tf_op jit(solution)/shard_map/ppermute | solution.py:376
  100.1 8.0 %collective-permute-start.18 = (bf16[128,1024]{1,0:T(8,128)(2,1)S(1)}, bf16[128,1024]{1,0:T(8,128)(2,1)S(1)}, u32[]{:S(2)}, u32[]{:S(2)}) collective-permute-start(bf16[128,1024]{1,0:T(8,128)(2,1)S(1)} %slice.19), channel_id=1, source_target_pairs={{0,3},{1,0},{2,1},{3,2},{4,7},{5,4},{6,5},{7,6},{8,11},{9,8},{10,9... | collective-permute-start | bytes 786440 | tf_op jit(solution)/shard_map/ppermute | solution.py:367
  100.2 9.4 %collective-permute-start.17 = (bf16[128,1024]{1,0:T(8,128)(2,1)S(1)}, bf16[128,1024]{1,0:T(8,128)(2,1)S(1)}, u32[]{:S(2)}, u32[]{:S(2)}) collective-permute-start(bf16[128,1024]{1,0:T(8,128)(2,1)S(1)} %slice.18), channel_id=1, source_target_pairs={{0,1},{1,2},{2,3},{3,0},{4,5},{5,6},{6,7},{7,4},{8,9},{9,10},{10,1... | collective-permute-start | bytes 786440 | tf_op jit(solution)/shard_map/ppermute | solution.py:364
  107.5 8.8 %collective-permute-start.19 = (bf16[256,640]{1,0:T(8,128)(2,1)S(1)}, bf16[256,640]{1,0:T(8,128)(2,1)S(1)}, u32[]{:S(2)}, u32[]{:S(2)}) collective-permute-start(bf16[256,640]{1,0:T(8,128)(2,1)S(1)} %fusion.7), channel_id=1, source_target_pairs={{0,4},{1,5},{2,6},{3,7},{4,0},{5,1},{6,2},{7,3},{8,12},{9,13},{10,... | collective-permute-start | bytes 983048 | tf_op jit(solution)/shard_map/ppermute | solution.py:384
  113.6 2.8 %copy-start.1 = (bf16[4,256,640]{2,1,0:T(8,128)(2,1)S(1)}, bf16[4,256,640]{2,1,0:T(8,128)(2,1)}, u32[]{:S(2)}) copy-start(bf16[4,256,640]{2,1,0:T(8,128)(2,1)} %copy-done) | copy-start | bytes 3932164
  115.6 8.6 %collective-permute-start.20 = (bf16[256,640]{1,0:T(8,128)(2,1)S(1)}, bf16[256,640]{1,0:T(8,128)(2,1)S(1)}, u32[]{:S(2)}, u32[]{:S(2)}) collective-permute-start(bf16[256,640]{1,0:T(8,128)(2,1)S(1)} %fusion.6), channel_id=1, source_target_pairs={{0,4},{1,5},{2,6},{3,7},{4,0},{5,1},{6,2},{7,3},{8,12},{9,13},{10,... | collective-permute-start | bytes 983048 | tf_op jit(solution)/shard_map/ppermute | solution.py:388
  117.6 1.3 %copy-start.3 = (bf16[4,256,640]{2,1,0:T(8,128)(2,1)S(1)}, bf16[4,256,640]{2,1,0:T(8,128)(2,1)}, u32[]{:S(2)}) copy-start(bf16[4,256,640]{2,1,0:T(8,128)(2,1)} %copy-done.2) | copy-start | bytes 3932164
